TPU v7x, 512 devices: a whole 4x4x16 slice. The times are simulated.
512 devices in a mesh: dp: 32 (over z, y_hi), layer: 16 (over y_lo, x, core).
Axes of the slice: x: 4, y: 4 (y_hi: 2, y_lo: 2; y = y_hi * 2 + y_lo), z: 16, core: 2. Of those that a mesh axis runs over, the one named last changes fastest.
Arguments:
- train_grads: float32 [4096, 16, 1024], P('dp', 'layer')
- query_grads: float32 [4096, 16, 1024], P('dp', 'layer'), may hold values from -6 to 6
- inverse_factors: float32 [16, 1024, 1024], P('layer', 'dp')
- repeat_counts: int32 [4096], P('dp'), may hold values from 1 to 4
Outputs:
- influence: float32 [4096, 1152], P(('dp', 'layer'))
All inputs are finite; a program needn't handle non-finite values.
Results may differ from a plain program's by a relative error of at most 0.00014.
Values sent between devices are 32-bit elements; how exact they have to be, the bound alone decides.
No kernel may reach another device: no remote copies, remote signals or barrier semaphores. Data moves between devices by JAX's collectives and lax.ppermute only.
A program may use at most 64 MiB of HBM per device.

v0:
```python
import math

import jax
import jax.numpy as jnp
from jax import lax
from jax.sharding import PartitionSpec as P

DAMPING = 0.5
PRECISE = lax.Precision.HIGHEST


def passed_along(value, axis, steps):
    count = lax.axis_size(axis)
    pairs = [(source, (source + steps) % count) for source in range(count)]
    return lax.ppermute(value, axis, pairs)


def product(left_side, right_side):
    return jnp.dot(left_side, right_side, precision=PRECISE, preferred_element_type=jnp.float32)


def on_device(train_grads, query_grads, inverse_factors, repeat_counts):
    train = train_grads[:, 0, :]
    query = query_grads[:, 0, :]
    weights = repeat_counts.astype(jnp.float32)
    proj_width = train.shape[1]
    partial_fisher = product((train * weights[:, None]).T, train)
    fisher = lax.psum(partial_fisher, "dp")
    total_rows = train.shape[0] * lax.axis_size("dp")
    damped = fisher / total_rows + DAMPING * jnp.eye(proj_width, dtype=jnp.float32)
    inverse = lax.all_gather(inverse_factors[0], "dp", axis=0, tiled=True)
    first = product(query, inverse.T)
    leftover = query - product(first, damped)
    precond = first + product(leftover, inverse.T)
    reach_steps = min(4, (lax.axis_size("dp") - 1) // 2)
    window = 2 * reach_steps + 1
    blocks = [
        passed_along(precond, "dp", reach_steps - offset) if offset != reach_steps else precond
        for offset in range(window)
    ]
    score_scale = 1.0 / math.sqrt(proj_width * lax.axis_size("layer"))
    row_factor = weights * score_scale
    stacked = jnp.concatenate(blocks, axis=0)
    return lax.psum_scatter(
        product(train, stacked.T) * row_factor[:, None], "layer", scatter_dimension=0, tiled=True
    )


def solution(mesh):
    placed = (P("dp", "layer", None), P("dp", "layer", None), P("layer", "dp", None), P("dp"))
    return jax.shard_map(
        on_device, mesh=mesh, in_specs=placed, out_specs=P(("dp", "layer"), None), check_vma=False
    )
```

profile of v0, /device:TPU:1, one launch (start us, length us, event | category | flops | bytes accessed | tf_op | source)
XLA Modules:
  0.0 727.2 jit_solution(2681264612031811712)
XLA Ops:
  6.5 0.7 all-gather.3.cloned.1.call-update
  7.3 0.0 all-reduce.4.cloned.1.call-start
  7.3 0.7 convert_element_type.4
  8.0 1.5 broadcast_multiply_fusion
  9.4 0.0 copy-start.2
  9.4 6.2 fusion.19
  15.6 0.0 all-reduce.4.cloned.1.call-update
  15.6 0.0 all-reduce.6.cloned.1.call-start
  15.7 156.1 %all-gather.3.cloned.1.call-done = f32[1,1024,1024]{2,1,0:T(8,128)} async-done(((f32[1,32,1024]{2,1,0:T(8,128)}), f32[1,1024,1024]{2,1,0:T(8,128)}) %all-gather.3.cloned.1.call-update) | async-done | bytes 4194320 | tf_op jit(solution)/shard_map/all_gather | solution.py:31
  171.8 6.5 fusion.2
  178.4 0.0 copy-start.3
  178.4 305.5 %all-reduce.4.cloned.1.call-done = f32[1024,1024]{1,0:T(8,128)} async-done(((f32[1024,1024]{1,0:T(8,128)}), f32[1024,1024]{1,0:T(8,128)}) %all-reduce.4.cloned.1.call-update) | async-done | bytes 4194320 | tf_op jit(solution)/shard_map/psum | solution.py:28
  483.9 4.9 fusion.15
  488.9 4.5 fusion.12
  493.3 2.5 collective-permute-start
  495.8 4.2 collective-permute-start.1
  500.0 2.8 collective-permute-start.2
  502.8 3.6 collective-permute-start.3
  506.4 0.0 copy-start.1
  506.4 5.5 collective-permute-start.4
  511.9 2.5 collective-permute-start.5
  514.4 4.5 collective-permute-done.1
  519.0 2.8 collective-permute-start.6
  521.8 7.6 %collective-permute-done.2 = f32[128,1024]{1,0:T(8,128)S(1)} collective-permute-done((f32[128,1024]{1,0:T(8,128)S(1)}, f32[128,1024]{1,0:T(8,128)S(1)}, u32[]{:S(2)}, u32[]{:S(2)}) %collective-permute-start.2) | collective-permute-done | bytes 524320 | tf_op jit(solution)/shard_map/ppermute | solution.py:15
  529.4 1.9 collective-permute-start.7
  531.4 26.7 %collective-permute-done.3 = f32[128,1024]{1,0:T(8,128)S(1)} collective-permute-done((f32[128,1024]{1,0:T(8,128)S(1)}, f32[128,1024]{1,0:T(8,128)S(1)}, u32[]{:S(2)}, u32[]{:S(2)}) %collective-permute-start.3) | collective-permute-done | bytes 524320 | tf_op jit(solution)/shard_map/ppermute | solution.py:15
  558.4 4.7 fusion.8
  563.1 0.0 all-reduce.6.cloned.1.call-update
  563.1 1.3 dynamic-slice
  565.0 153.5 %all-reduce.6.cloned.1.call-done = f32[128,1152]{0,1:T(8,128)} async-done(((f32[128,1152]{0,1:T(8,128)}), f32[128,1152]{0,1:T(8,128)}) %all-reduce.6.cloned.1.call-update) | async-done | bytes 589840
  718.5 1.3 constant_dynamic-slice_fusion
  719.8 0.8 copy.6
  (21 shorter events, 0.4 us)
Async XLA Ops:
  6.5 165.3 %all-gather.3.cloned.1.call-start = ((), (), s32[]{:S(2)}) async-start(), calls=%async_computation.1 | async-start | bytes 4325376 | tf_op jit(solution)/shard_map/all_gather | solution.py:31
  7.3 476.6 %all-reduce.4.cloned.1.call-start = ((), (), s32[]{:S(2)}) async-start(), calls=%async_computation | async-start | bytes 8388608 | tf_op jit(solution)/shard_map/psum | solution.py:28
  9.4 162.4 %copy-start.2 = (f32[128,1,1024]{2,1,0:T(1,128)S(1)}, f32[128,1,1024]{2,1,0:T(1,128)}, u32[]{:S(2)}) copy-start(f32[128,1,1024]{2,1,0:T(1,128)} %param.5) | copy-start | bytes 1572868
  15.6 702.9 %all-reduce.6.cloned.1.call-start = ((), (), s32[]{:S(2)}) async-start(), calls=%async_computation.2 | async-start | bytes 1179648
  178.4 328.0 %copy-start.3 = (s32[128]{0:T(128)S(1)}, s32[128]{0:T(128)}, u32[]{:S(2)}) copy-start(s32[128]{0:T(128)} %param.7) | copy-start | bytes 1540
  483.9 5.0 copy-start
  493.3 18.5 %collective-permute-start = (f32[128,1024]{1,0:T(8,128)S(1)}, f32[128,1024]{1,0:T(8,128)S(1)}, u32[]{:S(2)}, u32[]{:S(2)}) collective-permute-start(f32[128,1024]{1,0:T(8,128)S(1)} %fusion.12), channel_id=1, source_target_pairs={{0,64},{16,80},{32,96},{48,112},{64,128},{80,144},{96,160},{112,17... | collective-permute-start | bytes 1572872 | tf_op jit(solution)/shard_map/ppermute | solution.py:15
  495.8 23.1 %collective-permute-start.1 = (f32[128,1024]{1,0:T(8,128)S(1)}, f32[128,1024]{1,0:T(8,128)S(1)}, u32[]{:S(2)}, u32[]{:S(2)}) collective-permute-start(f32[128,1024]{1,0:T(8,128)S(1)} %fusion.12), channel_id=1, source_target_pairs={{0,48},{16,64},{32,80},{48,96},{64,112},{80,128},{96,144},{112,160... | collective-permute-start | bytes 1572872 | tf_op jit(solution)/shard_map/ppermute | solution.py:15
  500.0 29.4 %collective-permute-start.2 = (f32[128,1024]{1,0:T(8,128)S(1)}, f32[128,1024]{1,0:T(8,128)S(1)}, u32[]{:S(2)}, u32[]{:S(2)}) collective-permute-start(f32[128,1024]{1,0:T(8,128)S(1)} %fusion.12), channel_id=1, source_target_pairs={{0,32},{16,48},{32,64},{48,80},{64,96},{80,112},{96,128},{112,144}... | collective-permute-start | bytes 1572872 | tf_op jit(solution)/shard_map/ppermute | solution.py:15
  502.8 55.3 %collective-permute-start.3 = (f32[128,1024]{1,0:T(8,128)S(1)}, f32[128,1024]{1,0:T(8,128)S(1)}, u32[]{:S(2)}, u32[]{:S(2)}) collective-permute-start(f32[128,1024]{1,0:T(8,128)S(1)} %fusion.12), channel_id=1, source_target_pairs={{0,16},{16,32},{32,48},{48,64},{64,80},{80,96},{96,112},{112,128},... | collective-permute-start | bytes 1572872 | tf_op jit(solution)/shard_map/ppermute | solution.py:15
  506.4 52.0 %copy-start.1 = (f32[128,1,1024]{2,1,0:T(1,128)S(1)}, f32[128,1,1024]{2,1,0:T(1,128)}, u32[]{:S(2)}) copy-start(f32[128,1,1024]{2,1,0:T(1,128)} %param.4) | copy-start | bytes 1572868
  506.4 51.8 %collective-permute-start.4 = (f32[128,1024]{1,0:T(8,128)S(1)}, f32[128,1024]{1,0:T(8,128)S(1)}, u32[]{:S(2)}, u32[]{:S(2)}) collective-permute-start(f32[128,1024]{1,0:T(8,128)S(1)} %fusion.12), channel_id=1, source_target_pairs={{0,496},{16,0},{32,16},{48,32},{64,48},{80,64},{96,80},{112,96},{1... | collective-permute-start | bytes 1572872 | tf_op jit(solution)/shard_map/ppermute | solution.py:15
  511.9 46.3 %collective-permute-start.5 = (f32[128,1024]{1,0:T(8,128)S(1)}, f32[128,1024]{1,0:T(8,128)S(1)}, u32[]{:S(2)}, u32[]{:S(2)}) collective-permute-start(f32[128,1024]{1,0:T(8,128)S(1)} %fusion.12), channel_id=1, source_target_pairs={{0,480},{16,496},{32,0},{48,16},{64,32},{80,48},{96,64},{112,80},{... | collective-permute-start | bytes 1572872 | tf_op jit(solution)/shard_map/ppermute | solution.py:15
  519.0 39.3 %collective-permute-start.6 = (f32[128,1024]{1,0:T(8,128)S(1)}, f32[128,1024]{1,0:T(8,128)S(1)}, u32[]{:S(2)}, u32[]{:S(2)}) collective-permute-start(f32[128,1024]{1,0:T(8,128)S(1)} %fusion.12), channel_id=1, source_target_pairs={{0,464},{16,480},{32,496},{48,0},{64,16},{80,32},{96,48},{112,64},... | collective-permute-start | bytes 1572872 | tf_op jit(solution)/shard_map/ppermute | solution.py:15
  529.4 28.9 %collective-permute-start.7 = (f32[128,1024]{1,0:T(8,128)S(1)}, f32[128,1024]{1,0:T(8,128)S(1)}, u32[]{:S(2)}, u32[]{:S(2)}) collective-permute-start(f32[128,1024]{1,0:T(8,128)S(1)} %fusion.12), channel_id=1, source_target_pairs={{0,448},{16,464},{32,480},{48,496},{64,0},{80,16},{96,32},{112,48}... | collective-permute-start | bytes 1572872 | tf_op jit(solution)/shard_map/ppermute | solution.py:15
Sparse Core Ops, SparseCore 0:
  10.5 161.3 all-gather.2
  174.8 309.1 all-reduce.3
  563.2 155.2 all-reduce.5
where the time goes:
time: 730 us; the launch traced here: 727 us
  waiting for transfers between devices  655 us (90%)
  matrix products  26.8 us (4%)
  starting transfers between devices  25.8 us (4%)
  between operations  14 us (2%)
    psum x1, waiting for transfers between devices, on_device(): fisher = lax.psum(partial_fisher, 'dp')  306 us
    all_gather x1, waiting for transfers between devices, on_device(): inverse = lax.all_gather(inverse_factors[0], 'dp', axis=0, tiled=True)  156 us
    unnamed x4, waiting for transfers between devices  154 us
    ppermute x8, waiting for transfers between devices, passed_along(): return lax.ppermute(value, axis, pairs)  38.8 us
    dot_general x5, matrix products, product(): jnp.dot(left_side, right_side, precision=PRECISE, preferred_element_type=...  26.8 us
    ppermute x8, starting transfers between devices, passed_along(): return lax.ppermute(value, axis, pairs)  25.7 us
  transfers between devices with their start and end apart: 11, of which 6 were waited for; matrix products, arithmetic and copies ran while one was open for 2% of the time, Pallas kernels for 0%

commit v1 on v0

v1 whole, which is shorter than its diff:
```python
import math

import jax
import jax.numpy as jnp
from jax import lax
from jax.sharding import Mesh, PartitionSpec as P

DAMPING = 0.5
FAST = lax.Precision.HIGH


def dot(left, right, dims):
    return lax.dot_general(
        left, right, (dims, ((), ())), precision=FAST, preferred_element_type=jnp.float32
    )


def shift_z(value, steps):
    count = lax.axis_size("z")
    return lax.ppermute(value, "z", [(i, (i + steps) % count) for i in range(count)])


def swap_y(value):
    return lax.ppermute(value, "yh", [(0, 1), (1, 0)])


def after(value, *others):
    return lax.optimization_barrier((value, *others))[0]


def reduce_near(blocks, place):
    def of_class(steps):
        return lax.dynamic_index_in_dim(blocks, (place + steps) % 4, 1, keepdims=False)

    opposite = of_class(2)
    from_left = shift_z(of_class(1), 1)
    from_right = shift_z(of_class(3), -1)
    from_left2 = shift_z(opposite[:, :8], 2)
    from_right2 = shift_z(opposite[:, 8:], -2)
    return of_class(0) + from_left + from_right + jnp.concatenate([from_left2, from_right2], axis=1)


def reduce_far(sums, place):
    row = place // 4

    def of_row(steps):
        return lax.dynamic_index_in_dim(sums, (row + steps) % 4, 0, keepdims=False)

    opposite = of_row(2)
    passing_right = shift_z(opposite[:8], 4)
    passing_left = shift_z(opposite[8:], -4)
    right, left = of_row(1), of_row(3)
    from_left = shift_z(jnp.concatenate([right[:8] + passing_right, right[8:]]), 4)
    from_right = shift_z(jnp.concatenate([left[:8], left[8:] + passing_left]), -4)
    return of_row(0) + from_left + from_right


def gather_far(part):
    plus4 = shift_z(part, -4)
    minus4 = shift_z(part, 4)
    plus8 = jnp.concatenate([shift_z(plus4[:8], -4), shift_z(minus4[8:], 4)])
    return jnp.stack([part, plus4, plus8, minus4])


def gather_near(parts):
    plus1 = shift_z(parts, -1)
    minus1 = shift_z(parts, 1)
    plus2 = shift_z(parts[:, :8], -2)
    minus2 = shift_z(parts[:, 8:], 2)
    two = jnp.concatenate([plus2, jnp.roll(minus2, -1, axis=0)], axis=1)
    three = jnp.roll(minus1, -1, axis=0)
    return jnp.stack([parts, plus1, two, three], axis=1)


def on_device(train_grads, query_grads, inverse_factors, repeat_counts):
    place = lax.axis_index("z")
    half = lax.axis_index("yh")
    first_half = half == 0
    query = query_grads[:, 0, :]
    roots = jnp.sqrt(repeat_counts.astype(jnp.float32))
    train = train_grads[:, 0, :] * roots[:, None]
    rows, width = train.shape
    quarter = width // 4
    total_rows = rows * lax.axis_size("z") * lax.axis_size("yh")

    own_rows = inverse_factors[0]
    swapped = swap_y(jnp.concatenate([train, own_rows]))
    other_train, other_rows = swapped[:rows], swapped[rows:]
    pair_rows = jnp.where(
        first_half,
        jnp.concatenate([own_rows, other_rows]),
        jnp.concatenate([other_rows, own_rows]),
    )
    inverse = lax.all_gather(pair_rows, "z", axis=0, tiled=True)

    plus1, minus1 = shift_z(query, -1), shift_z(query, 1)

    pair_train = jnp.where(
        first_half,
        jnp.concatenate([train, other_train]),
        jnp.concatenate([other_train, train]),
    )
    turned = jnp.where(first_half, pair_train, jnp.roll(pair_train, -quarter, axis=1))
    strip0 = dot(turned[:, :quarter], turned[:, : 3 * quarter], ((0,), (0,)))
    strip2 = dot(turned[:, 2 * quarter : 3 * quarter], turned[:, 2 * quarter :], ((0,), (0,)))
    partial = jnp.concatenate([strip0, strip2], axis=1)
    blocks, plus1, minus1 = lax.optimization_barrier(
        (partial.reshape(4, 4, quarter // 16, 5 * quarter), plus1, minus1)
    )
    plus2, minus2 = shift_z(plus1, -1), shift_z(minus1, 1)
    own_queries1 = jnp.concatenate([minus1, query, plus1])
    other_queries1 = swap_y(own_queries1)
    near_sums, plus2, minus2 = lax.optimization_barrier((reduce_near(blocks, place), plus2, minus2))
    own_queries2 = jnp.concatenate([minus2, plus2])
    part, other_queries1 = lax.optimization_barrier((reduce_far(near_sums, place), other_queries1))
    other_queries2 = swap_y(after(own_queries2, other_queries1))
    parts, inverse = lax.optimization_barrier((gather_far(part), inverse))
    gathered = gather_near(parts).reshape(quarter, 5 * quarter)
    strips = jnp.roll(gathered, place * (quarter // 16), axis=0)

    own_queries = jnp.concatenate([own_queries1, own_queries2])
    other_queries = jnp.concatenate([other_queries1, other_queries2])
    own_first = dot(own_queries, inverse, ((1,), (1,)))
    other_first = dot(other_queries, inverse, ((1,), (1,)))

    side = dot(pair_train, inverse, ((1,), (0,)))
    side_turned = jnp.where(first_half, side, jnp.roll(side, -quarter, axis=1))
    s0, s1, s2, s3 = (side_turned[:, i * quarter : (i + 1) * quarter] for i in range(4))
    b00, b01, b02, b22, b23 = (strips[:, i * quarter : (i + 1) * quarter] for i in range(5))
    straight0 = dot(s0, strips[:, : 3 * quarter], ((1,), (0,)))
    straight2 = dot(s2, strips[:, 3 * quarter :], ((1,), (0,)))
    crossed0 = dot(side_turned[:, quarter : 3 * quarter], strips[:, quarter : 3 * quarter], ((1,), (1,)))
    crossed2 = dot(s3, b23, ((1,), (1,)))
    product = jnp.concatenate(
        [
            straight0[:, :quarter] + crossed0,
            straight0[:, quarter : 2 * quarter],
            straight0[:, 2 * quarter :] + straight2[:, :quarter] + crossed2,
            straight2[:, quarter:],
        ],
        axis=1,
    )
    product = jnp.where(first_half, product, jnp.roll(product, quarter, axis=1))
    left = pair_train - (0.5 * DAMPING) * side - product * (1.0 / total_rows)

    own_scores = dot(left, own_first, ((1,), (1,)))
    other_scores = dot(left, other_first, ((1,), (1,)))
    even = jnp.where(first_half, own_scores, other_scores)
    odd = jnp.where(first_half, other_scores, own_scores)

    def tiles(scores, half_rows, offsets):
        at = (3, 0, 1, 2, 4)
        piece = scores[half_rows * rows : (half_rows + 1) * rows]
        return [piece[:, at[i] * rows : (at[i] + 1) * rows] for i in offsets]

    def mixed(first_tiles, second_tiles):
        out = []
        for i in range(9):
            out.append((first_tiles if i % 2 == 0 else second_tiles)[i // 2])
        return jnp.concatenate(out, axis=1)

    upper = mixed(tiles(even, 0, range(5)), tiles(odd, 0, range(4)))
    lower = mixed(tiles(odd, 1, range(5)), tiles(even, 1, range(1, 5)))
    upper, lower = lax.optimization_barrier((upper, lower))
    window = 9 * rows
    shares = lax.axis_size("yl") * lax.axis_size("x") * lax.axis_size("c")
    own = rows // shares
    terms = jnp.stack([upper, lower]).reshape(shares, 2, own, window)
    core = lax.axis_index("c")
    kept = lax.dynamic_index_in_dim(terms, core, 1, keepdims=False)
    sent = lax.dynamic_index_in_dim(terms, 1 - core, 1, keepdims=False)
    halves = kept + lax.ppermute(sent, "c", [(0, 1), (1, 0)])
    received = lax.all_to_all(halves.reshape(shares * own, window), ("yh", "yl", "x"), 0, 0, tiled=True)
    sums = received.reshape(shares, own, window).sum(axis=0)
    rank = lax.axis_index(("yl", "x", "c"))
    scale = lax.dynamic_slice_in_dim(roots, rank * own, own) * (1.0 / math.sqrt(width * shares))
    return sums * scale[:, None]


def solution(mesh):
    parts = Mesh(mesh.devices.reshape(16, 2, 2, 4, 2), ("z", "yh", "yl", "x", "c"))
    dp, layer = ("z", "yh"), ("yl", "x", "c")
    placed = (P(dp, layer, None), P(dp, layer, None), P(layer, dp, None), P(dp))
    return jax.shard_map(
        on_device, mesh=parts, in_specs=placed, out_specs=P(dp + layer, None), check_vma=False
    )
```

time: 730 us -> 245 us (0.34)
  waiting for transfers between devices: 655 us -> 74.6 us
  starting transfers between devices: 25.8 us -> 121 us
    psum x1 -> x0, waiting for transfers between devices: 306 us -> none  [on_device(): fisher = lax.psum(partial_fisher, 'dp')]
    all_gather x1, waiting for transfers between devices: 156 us -> 0.02 us  [on_device(): inverse = lax.all_gather(pair_rows, 'z', axis=0, tiled=True)]
    unnamed x4 -> x1, waiting for transfers between devices: 154 us -> 0.02 us
    ppermute x8 -> x24, starting transfers between devices: 25.7 us -> 114 us  [the longest x20 85 us: shift_z(): lax.ppermute(value, 'z', [(i, (i + steps) % count) for i in range(count)])]
    ppermute x8 -> x24, waiting for transfers between devices: 38.8 us -> 63.2 us  [the longest x20 50.5 us: shift_z(): lax.ppermute(value, 'z', [(i, (i + steps) % count) for i in range(count)])]
    all_to_all x0 -> x1, waiting for transfers between devices: none -> 11.3 us  [on_device(): lax.all_to_all(halves.reshape(shares * own, window), ('yh', 'yl', 'x'), 0...]
    dot_general x5 -> x11, matrix products: 26.8 us -> 20.6 us  [dot(): lax.dot_general(left, right, (dims, ((), ())), precision=FAST, preferred_...]
  transfers between devices with their start and end apart: 11 -> 26, of which waited for: 6 -> 12; matrix products, arithmetic and copies ran while one was open for 2% -> 9% of each run, Pallas kernels for 0% -> 0%
where the time goes in v1:
time: 245 us; the launch traced here: 244 us
  starting transfers between devices  121 us (49%)
  waiting for transfers between devices  74.6 us (30%)
  matrix products  20.6 us (8%)
  between operations  14.4 us (6%)
  other arithmetic  8.09 us (3%)
  local copies, waits for them, and re-layouts  5.69 us (2%)
    ppermute x20, starting transfers between devices, shift_z(): lax.ppermute(value, 'z', [(i, (i + steps) % count) for i in range(count)])  85 us
    ppermute x20, waiting for transfers between devices, shift_z(): lax.ppermute(value, 'z', [(i, (i + steps) % count) for i in range(count)])  50.5 us
    dot_general x11, matrix products, dot(): lax.dot_general(left, right, (dims, ((), ())), precision=FAST, preferred_...  20.6 us
    ppermute x1, starting transfers between devices, on_device(): halves = kept + lax.ppermute(sent, 'c', [(0, 1), (1, 0)])  14.9 us
    ppermute x3, starting transfers between devices, swap_y(): return lax.ppermute(value, 'yh', [(0, 1), (1, 0)])  13.9 us
    all_to_all x1, waiting for transfers between devices, on_device(): lax.all_to_all(halves.reshape(shares * own, window), ('yh', 'yl', 'x'), 0...  11.3 us
    ppermute x3, waiting for transfers between devices, swap_y(): return lax.ppermute(value, 'yh', [(0, 1), (1, 0)])  11.1 us
    all_to_all x1, starting transfers between devices, on_device(): lax.all_to_all(halves.reshape(shares * own, window), ('yh', 'yl', 'x'), 0...  6.85 us
  transfers between devices with their start and end apart: 26, of which 12 were waited for; matrix products, arithmetic and copies ran while one was open for 9% of the time, Pallas kernels for 0%

profile of v1, /device:TPU:1, one launch (start us, length us, event | category | flops | bytes accessed | tf_op | source)
XLA Modules:
  0.0 244.1 jit_solution(6626774108957274885)
XLA Ops:
  9.4 5.7 %collective-permute-start = (f32[160,1024]{1,0:T(8,128)S(1)}, f32[160,1024]{1,0:T(8,128)S(1)}, u32[]{:S(2)}, u32[]{:S(2)}) collective-permute-start(f32[160,1024]{1,0:T(8,128)S(1)} %pad_maximum_fusion.5), channel_id=1, source_target_pairs={{0,16},{16,0},{1,17},{17,1},{2,18},{18,2},{3,19},{19,3},{4,20},{20... | collective-permute-start | bytes 1966088 | tf_op jit(solution)/shard_map/ppermute | solution.py:24
  15.1 11.1 %collective-permute-done = f32[160,1024]{1,0:T(8,128)S(1)} collective-permute-done((f32[160,1024]{1,0:T(8,128)S(1)}, f32[160,1024]{1,0:T(8,128)S(1)}, u32[]{:S(2)}, u32[]{:S(2)}) %collective-permute-start) | collective-permute-done | bytes 655392 | tf_op jit(solution)/shard_map/ppermute | solution.py:24
  27.9 14.2 %collective-permute-start.1 = (f32[128,1024]{1,0:T(8,128)}, f32[128,1024]{1,0:T(8,128)S(1)}, u32[]{:S(2)}, u32[]{:S(2)}) collective-permute-start(f32[128,1024]{1,0:T(8,128)} %bitcast.74), channel_id=1, source_target_pairs={{0,480},{32,0},{64,32},{96,64},{128,96},{160,128},{192,160},{224,1... | collective-permute-start | bytes 1572872 | tf_op jit(solution)/shard_map/ppermute | solution.py:20
  45.7 6.4 %collective-permute-done.1 = f32[128,1024]{1,0:T(8,128)S(1)} collective-permute-done((f32[128,1024]{1,0:T(8,128)}, f32[128,1024]{1,0:T(8,128)S(1)}, u32[]{:S(2)}, u32[]{:S(2)}) %collective-permute-start.1) | collective-permute-done | bytes 524320 | tf_op jit(solution)/shard_map/ppermute | solution.py:20
  52.1 5.4 %collective-permute-done.2 = f32[128,1024]{1,0:T(8,128)S(1)} collective-permute-done((f32[128,1024]{1,0:T(8,128)}, f32[128,1024]{1,0:T(8,128)S(1)}, u32[]{:S(2)}, u32[]{:S(2)}) %collective-permute-start.2) | collective-permute-done | bytes 524320 | tf_op jit(solution)/shard_map/ppermute | solution.py:20
  59.5 4.3 %collective-permute-start.5 = (f32[4,8,1280]{2,1,0:T(8,128)S(1)}, f32[4,8,1280]{2,1,0:T(8,128)S(1)}, u32[]{:S(2)}, u32[]{:S(2)}) collective-permute-start(f32[4,8,1280]{2,1,0:T(8,128)S(1)} %get-tuple-element.60), channel_id=1, source_target_pairs={{0,64},{32,96},{64,128},{96,160},{128,192},{160,224},{192,256},{22... | collective-permute-start | bytes 491528 | tf_op jit(solution)/shard_map/ppermute | solution.py:20
  66.1 2.9 %collective-permute-start.3 = (f32[4,16,1280]{2,1,0:T(8,128)S(1)}, f32[4,16,1280]{2,1,0:T(8,128)S(1)}, u32[]{:S(2)}, u32[]{:S(2)}) collective-permute-start(f32[4,16,1280]{2,1,0:T(8,128)S(1)} %get-tuple-element.33), channel_id=1, source_target_pairs={{0,32},{32,64},{64,96},{96,128},{128,160},{160,192},{192,224},{224... | collective-permute-start | bytes 983048 | tf_op jit(solution)/shard_map/ppermute | solution.py:20
  72.9 4.4 %collective-permute-start.7 = (f32[128,1024]{1,0:T(8,128)S(1)}, f32[128,1024]{1,0:T(8,128)S(1)}, u32[]{:S(2)}, u32[]{:S(2)}) collective-permute-start(f32[128,1024]{1,0:T(8,128)S(1)} %collective-permute-done.1), channel_id=1, source_target_pairs={{0,480},{32,0},{64,32},{96,64},{128,96},{160,128},{192,160},{224,1... | collective-permute-start | bytes 1572872 | tf_op jit(solution)/shard_map/ppermute | solution.py:20
  78.5 5.0 %collective-permute-start.13 = (f32[384,1024]{1,0:T(8,128)S(1)}, f32[384,1024]{1,0:T(8,128)S(1)}, u32[]{:S(2)}, u32[]{:S(2)}) collective-permute-start(f32[384,1024]{1,0:T(8,128)S(1)} %pad_maximum_fusion), channel_id=1, source_target_pairs={{0,16},{16,0},{1,17},{17,1},{2,18},{18,2},{3,19},{19,3},{4,20},{20... | collective-permute-start | bytes 4718600 | tf_op jit(solution)/shard_map/ppermute | solution.py:24
  83.5 4.2 %collective-permute-done.3 = f32[4,16,1280]{2,1,0:T(8,128)S(1)} collective-permute-done((f32[4,16,1280]{2,1,0:T(8,128)S(1)}, f32[4,16,1280]{2,1,0:T(8,128)S(1)}, u32[]{:S(2)}, u32[]{:S(2)}) %collective-permute-start.3) | collective-permute-done | bytes 327712 | tf_op jit(solution)/shard_map/ppermute | solution.py:20
  87.8 17.2 %collective-permute-done.7 = f32[128,1024]{1,0:T(8,128)S(1)} collective-permute-done((f32[128,1024]{1,0:T(8,128)S(1)}, f32[128,1024]{1,0:T(8,128)S(1)}, u32[]{:S(2)}, u32[]{:S(2)}) %collective-permute-start.7) | collective-permute-done | bytes 524320 | tf_op jit(solution)/shard_map/ppermute | solution.py:20
  105.0 5.2 %collective-permute-done.8 = f32[128,1024]{1,0:T(8,128)S(1)} collective-permute-done((f32[128,1024]{1,0:T(8,128)S(1)}, f32[128,1024]{1,0:T(8,128)S(1)}, u32[]{:S(2)}, u32[]{:S(2)}) %collective-permute-start.8) | collective-permute-done | bytes 524320 | tf_op jit(solution)/shard_map/ppermute | solution.py:20
  110.2 3.3 %collective-permute-start.9 = (f32[8,1280]{1,0:T(8,128)S(1)}, f32[8,1280]{1,0:T(8,128)S(1)}, u32[]{:S(2)}, u32[]{:S(2)}) collective-permute-start(f32[8,1280]{1,0:T(8,128)S(1)} %get-tuple-element.56), channel_id=1, source_target_pairs={{0,128},{32,160},{64,192},{96,224},{128,256},{160,288},{192,320},{... | collective-permute-start | bytes 122888 | tf_op jit(solution)/shard_map/ppermute | solution.py:20
  113.5 5.9 %collective-permute-start.11 = (f32[8,1280]{1,0:T(8,128)S(1)}, f32[8,1280]{1,0:T(8,128)S(1)}, u32[]{:S(2)}, u32[]{:S(2)}) collective-permute-start(f32[8,1280]{1,0:T(8,128)S(1)} %get-tuple-element.58), channel_id=1, source_target_pairs={{0,384},{32,416},{64,448},{96,480},{128,0},{160,32},{192,64},{224,... | collective-permute-start | bytes 122888 | tf_op jit(solution)/shard_map/ppermute | solution.py:20
  120.3 3.3 %collective-permute-done.11 = f32[8,1280]{1,0:T(8,128)S(1)} collective-permute-done((f32[8,1280]{1,0:T(8,128)S(1)}, f32[8,1280]{1,0:T(8,128)S(1)}, u32[]{:S(2)}, u32[]{:S(2)}) %collective-permute-start.11) | collective-permute-done | bytes 40992 | tf_op jit(solution)/shard_map/ppermute | solution.py:20
  123.6 6.0 %collective-permute-start.12 = (f32[16,1280]{1,0:T(8,128)S(1)}, f32[16,1280]{1,0:T(8,128)S(1)}, u32[]{:S(2)}, u32[]{:S(2)}) collective-permute-start(f32[16,1280]{1,0:T(8,128)S(1)} %pad_maximum_fusion.8), channel_id=1, source_target_pairs={{0,384},{32,416},{64,448},{96,480},{128,0},{160,32},{192,64},{224,... | collective-permute-start | bytes 245768 | tf_op jit(solution)/shard_map/ppermute | solution.py:20
  129.7 3.1 %collective-permute-start.10 = (f32[16,1280]{1,0:T(8,128)S(1)}, f32[16,1280]{1,0:T(8,128)S(1)}, u32[]{:S(2)}, u32[]{:S(2)}) collective-permute-start(f32[16,1280]{1,0:T(8,128)S(1)} %pad_maximum_fusion.7), channel_id=1, source_target_pairs={{0,128},{32,160},{64,192},{96,224},{128,256},{160,288},{192,320},{... | collective-permute-start | bytes 245768 | tf_op jit(solution)/shard_map/ppermute | solution.py:20
  133.0 3.2 %collective-permute-done.12 = f32[16,1280]{1,0:T(8,128)S(1)} collective-permute-done((f32[16,1280]{1,0:T(8,128)S(1)}, f32[16,1280]{1,0:T(8,128)S(1)}, u32[]{:S(2)}, u32[]{:S(2)}) %collective-permute-start.12) | collective-permute-done | bytes 81952 | tf_op jit(solution)/shard_map/ppermute | solution.py:20
  136.2 3.4 %collective-permute-done.10 = f32[16,1280]{1,0:T(8,128)S(1)} collective-permute-done((f32[16,1280]{1,0:T(8,128)S(1)}, f32[16,1280]{1,0:T(8,128)S(1)}, u32[]{:S(2)}, u32[]{:S(2)}) %collective-permute-start.10) | collective-permute-done | bytes 81952 | tf_op jit(solution)/shard_map/ppermute | solution.py:20
  139.6 3.5 %collective-permute-start.16 = (f32[16,1280]{1,0:T(8,128)S(1)}, f32[16,1280]{1,0:T(8,128)S(1)}, u32[]{:S(2)}, u32[]{:S(2)}) collective-permute-start(f32[16,1280]{1,0:T(8,128)S(1)} %fusion.24), channel_id=1, source_target_pairs={{0,128},{32,160},{64,192},{96,224},{128,256},{160,288},{192,320},{... | collective-permute-start | bytes 245768 | tf_op jit(solution)/shard_map/ppermute | solution.py:20
  143.2 5.7 %collective-permute-start.14 = (f32[16,1280]{1,0:T(8,128)S(1)}, f32[16,1280]{1,0:T(8,128)S(1)}, u32[]{:S(2)}, u32[]{:S(2)}) collective-permute-start(f32[16,1280]{1,0:T(8,128)S(1)} %fusion.24), channel_id=1, source_target_pairs={{0,384},{32,416},{64,448},{96,480},{128,0},{160,32},{192,64},{224,... | collective-permute-start | bytes 245768 | tf_op jit(solution)/shard_map/ppermute | solution.py:20
  154.2 6.8 %collective-permute-start.15 = (f32[8,1280]{1,0:T(8,128)S(1)}, f32[8,1280]{1,0:T(8,128)S(1)}, u32[]{:S(2)}, u32[]{:S(2)}) collective-permute-start(f32[8,1280]{1,0:T(8,128)S(1)} %slice.294), channel_id=1, source_target_pairs={{0,384},{32,416},{64,448},{96,480},{128,0},{160,32},{192,64},{224,... | collective-permute-start | bytes 122888 | tf_op jit(solution)/shard_map/ppermute | solution.py:20
  161.8 3.3 %collective-permute-start.22 = (f32[256,1024]{1,0:T(8,128)S(1)}, f32[256,1024]{1,0:T(8,128)S(1)}, u32[]{:S(2)}, u32[]{:S(2)}) collective-permute-start(f32[256,1024]{1,0:T(8,128)S(1)} %pad_maximum_fusion.4), channel_id=1, source_target_pairs={{0,16},{16,0},{1,17},{17,1},{2,18},{18,2},{3,19},{19,3},{4,20},{20... | collective-permute-start | bytes 3145736 | tf_op jit(solution)/shard_map/ppermute | solution.py:24
  165.2 4.6 %collective-permute-start.21 = (f32[4,16,1280]{2,1,0:T(8,128)S(1)}, f32[4,16,1280]{2,1,0:T(8,128)S(1)}, u32[]{:S(2)}, u32[]{:S(2)}) collective-permute-start(f32[4,16,1280]{2,1,0:T(8,128)S(1)} %pad_maximum_fusion.6), channel_id=1, source_target_pairs={{0,32},{32,64},{64,96},{96,128},{128,160},{160,192},{192,224},{224... | collective-permute-start | bytes 983048 | tf_op jit(solution)/shard_map/ppermute | solution.py:20
  171.8 4.4 %fusion.30 = f32[256,1024]{1,0:T(8,128)S(1)} fusion(f32[256,1024]{1,0:T(8,128)S(1)} %maximum_select_fusion, f32[1024,1024]{1,0:T(8,128)} %all-gather.2.cloned.1.call-done), kind=kOutput, calls=%fused_computation.96 | convolution fusion | flops 1610612736 | bytes 6291456 | tf_op jit(solution)/shard_map/dot_general | solution.py:13
  176.2 3.1 %collective-permute-start.20 = (f32[4,8,1280]{2,1,0:T(8,128)S(1)}, f32[4,8,1280]{2,1,0:T(8,128)S(1)}, u32[]{:S(2)}, u32[]{:S(2)}) collective-permute-start(f32[4,8,1280]{2,1,0:T(8,128)S(1)} %get-tuple-element.53), channel_id=1, source_target_pairs={{0,64},{32,96},{64,128},{96,160},{128,192},{160,224},{192,256},{22... | collective-permute-start | bytes 491528 | tf_op jit(solution)/shard_map/ppermute | solution.py:20
  179.3 4.6 %collective-permute-start.19 = (f32[4,8,1280]{2,1,0:T(8,128)S(1)}, f32[4,8,1280]{2,1,0:T(8,128)S(1)}, u32[]{:S(2)}, u32[]{:S(2)}) collective-permute-start(f32[4,8,1280]{2,1,0:T(8,128)S(1)} %get-tuple-element.52), channel_id=1, source_target_pairs={{0,448},{32,480},{64,0},{96,32},{128,64},{160,96},{192,128},{224,1... | collective-permute-start | bytes 491528 | tf_op jit(solution)/shard_map/ppermute | solution.py:20
  183.9 6.0 %fusion.31 = f32[640,1024]{1,0:T(8,128)S(1)} fusion(f32[640,1024]{1,0:T(8,128)} %constant_dynamic-update-slice_fusion, f32[1024,1024]{1,0:T(8,128)S(1)} %copy-done), kind=kOutput, calls=%fused_computation.97 | convolution fusion | flops 4026531840 | bytes 9437184 | tf_op jit(solution)/shard_map/dot_general | solution.py:13
  190.0 4.3 %fusion = f32[640,1024]{1,0:T(8,128)S(1)} fusion(f32[1024,1024]{1,0:T(8,128)S(1)} %copy-done, f32[256,1024]{1,0:T(8,128)S(1)} %collective-permute-done.22, f32[384,1024]{1,0:T(8,128)S(1)} %copy-done.5), kind=kOutput, calls=%fused_computation.2 | convolution fusion | flops 4027187200 | bytes 9437184 | tf_op jit(solution)/shard_map/dot_general | solution.py:13
  200.8 14.9 %collective-permute-start.23 = (f32[16,8,1152]{2,1,0:T(8,128)S(1)}, f32[16,8,1152]{2,1,0:T(8,128)S(1)}, u32[]{:S(2)}, u32[]{:S(2)}) collective-permute-start(f32[16,8,1152]{2,1,0:T(8,128)S(1)} %dynamic-slice_bitcast_fusion), channel_id=1, source_target_pairs={{0,1},{1,0},{2,3},{3,2},{4,5},{5,4},{6,7},{7,6},{8,9},{9,8},{10,11... | collective-permute-start | bytes 1769480 | tf_op jit(solution)/shard_map/ppermute | solution.py:172
  218.2 6.9 %all-to-all-start = ((f32[16,8,1152]{2,1,0:T(8,128)}), f32[16,8,1152]{2,1,0:T(8,128)S(1)}, u32[]{:S(2)}, u32[]{:S(2)}) async-start(f32[16,8,1152]{2,1,0:T(8,128)} %bitcast_add_fusion), calls=%async_computation | async-start | bytes 1179648 | tf_op jit(solution)/shard_map/all_to_all | solution.py:173
  225.2 11.3 %all-to-all-done = f32[16,8,1152]{2,1,0:T(8,128)S(1)} async-done(((f32[16,8,1152]{2,1,0:T(8,128)}), f32[16,8,1152]{2,1,0:T(8,128)S(1)}, u32[]{:S(2)}, u32[]{:S(2)}) %all-to-all-start) | async-done | bytes 589856 | tf_op jit(solution)/shard_map/all_to_all | solution.py:173
  (110 shorter events, 36.2 us)
Async XLA Ops:
  6.5 19.7 %copy-start.6 = (f32[1,32,1024]{2,1,0:T(8,128)S(1)}, f32[1,32,1024]{2,1,0:T(8,128)}, u32[]{:S(2)}) copy-start(f32[1,32,1024]{2,1,0:T(8,128)} %param.6) | copy-start | bytes 393220
  6.5 20.5 %copy-start.3 = (f32[128,1,1024]{2,1,0:T(1,128)S(1)}, f32[128,1,1024]{2,1,0:T(1,128)}, u32[]{:S(2)}) copy-start(f32[128,1,1024]{2,1,0:T(1,128)} %param.5) | copy-start | bytes 1572868
  6.5 158.7 %all-gather.2.cloned.1.call-start = ((), (), s32[]{:S(2)}) async-start(), calls=%async_computation.1 | async-start | bytes 4456448 | tf_op jit(solution)/shard_map/all_gather | solution.py:94
  9.4 16.8 %collective-permute-start = (f32[160,1024]{1,0:T(8,128)S(1)}, f32[160,1024]{1,0:T(8,128)S(1)}, u32[]{:S(2)}, u32[]{:S(2)}) collective-permute-start(f32[160,1024]{1,0:T(8,128)S(1)} %pad_maximum_fusion.5), channel_id=1, source_target_pairs={{0,16},{16,0},{1,17},{17,1},{2,18},{18,2},{3,19},{19,3},{4,20},{20... | collective-permute-start | bytes 1966088 | tf_op jit(solution)/shard_map/ppermute | solution.py:24
  27.9 24.1 %collective-permute-start.1 = (f32[128,1024]{1,0:T(8,128)}, f32[128,1024]{1,0:T(8,128)S(1)}, u32[]{:S(2)}, u32[]{:S(2)}) collective-permute-start(f32[128,1024]{1,0:T(8,128)} %bitcast.74), channel_id=1, source_target_pairs={{0,480},{32,0},{64,32},{96,64},{128,96},{160,128},{192,160},{224,1... | collective-permute-start | bytes 1572872 | tf_op jit(solution)/shard_map/ppermute | solution.py:20
  42.1 15.3 %collective-permute-start.2 = (f32[128,1024]{1,0:T(8,128)}, f32[128,1024]{1,0:T(8,128)S(1)}, u32[]{:S(2)}, u32[]{:S(2)}) collective-permute-start(f32[128,1024]{1,0:T(8,128)} %bitcast.74), channel_id=1, source_target_pairs={{0,32},{32,64},{64,96},{96,128},{128,160},{160,192},{192,224},{224... | collective-permute-start | bytes 1572872 | tf_op jit(solution)/shard_map/ppermute | solution.py:20
  57.5 15.4 %collective-permute-start.6 = (f32[4,8,1280]{2,1,0:T(8,128)S(1)}, f32[4,8,1280]{2,1,0:T(8,128)S(1)}, u32[]{:S(2)}, u32[]{:S(2)}) collective-permute-start(f32[4,8,1280]{2,1,0:T(8,128)S(1)} %get-tuple-element.61), channel_id=1, source_target_pairs={{0,448},{32,480},{64,0},{96,32},{128,64},{160,96},{192,128},{224,1... | collective-permute-start | bytes 491528 | tf_op jit(solution)/shard_map/ppermute | solution.py:20
  59.5 19.0 %collective-permute-start.5 = (f32[4,8,1280]{2,1,0:T(8,128)S(1)}, f32[4,8,1280]{2,1,0:T(8,128)S(1)}, u32[]{:S(2)}, u32[]{:S(2)}) collective-permute-start(f32[4,8,1280]{2,1,0:T(8,128)S(1)} %get-tuple-element.60), channel_id=1, source_target_pairs={{0,64},{32,96},{64,128},{96,160},{128,192},{160,224},{192,256},{22... | collective-permute-start | bytes 491528 | tf_op jit(solution)/shard_map/ppermute | solution.py:20
  63.7 19.7 %collective-permute-start.4 = (f32[4,16,1280]{2,1,0:T(8,128)S(1)}, f32[4,16,1280]{2,1,0:T(8,128)S(1)}, u32[]{:S(2)}, u32[]{:S(2)}) collective-permute-start(f32[4,16,1280]{2,1,0:T(8,128)S(1)} %get-tuple-element.35), channel_id=1, source_target_pairs={{0,480},{32,0},{64,32},{96,64},{128,96},{160,128},{192,160},{224,1... | collective-permute-start | bytes 983048 | tf_op jit(solution)/shard_map/ppermute | solution.py:20
  66.1 21.6 %collective-permute-start.3 = (f32[4,16,1280]{2,1,0:T(8,128)S(1)}, f32[4,16,1280]{2,1,0:T(8,128)S(1)}, u32[]{:S(2)}, u32[]{:S(2)}) collective-permute-start(f32[4,16,1280]{2,1,0:T(8,128)S(1)} %get-tuple-element.33), channel_id=1, source_target_pairs={{0,32},{32,64},{64,96},{96,128},{128,160},{160,192},{192,224},{224... | collective-permute-start | bytes 983048 | tf_op jit(solution)/shard_map/ppermute | solution.py:20
  69.0 41.1 %collective-permute-start.8 = (f32[128,1024]{1,0:T(8,128)S(1)}, f32[128,1024]{1,0:T(8,128)S(1)}, u32[]{:S(2)}, u32[]{:S(2)}) collective-permute-start(f32[128,1024]{1,0:T(8,128)S(1)} %collective-permute-done.2), channel_id=1, source_target_pairs={{0,32},{32,64},{64,96},{96,128},{128,160},{160,192},{192,224},{224... | collective-permute-start | bytes 1572872 | tf_op jit(solution)/shard_map/ppermute | solution.py:20
  72.9 32.1 %collective-permute-start.7 = (f32[128,1024]{1,0:T(8,128)S(1)}, f32[128,1024]{1,0:T(8,128)S(1)}, u32[]{:S(2)}, u32[]{:S(2)}) collective-permute-start(f32[128,1024]{1,0:T(8,128)S(1)} %collective-permute-done.1), channel_id=1, source_target_pairs={{0,480},{32,0},{64,32},{96,64},{128,96},{160,128},{192,160},{224,1... | collective-permute-start | bytes 1572872 | tf_op jit(solution)/shard_map/ppermute | solution.py:20
  78.5 61.1 %collective-permute-start.13 = (f32[384,1024]{1,0:T(8,128)S(1)}, f32[384,1024]{1,0:T(8,128)S(1)}, u32[]{:S(2)}, u32[]{:S(2)}) collective-permute-start(f32[384,1024]{1,0:T(8,128)S(1)} %pad_maximum_fusion), channel_id=1, source_target_pairs={{0,16},{16,0},{1,17},{17,1},{2,18},{18,2},{3,19},{19,3},{4,20},{20... | collective-permute-start | bytes 4718600 | tf_op jit(solution)/shard_map/ppermute | solution.py:24
  110.2 10.1 %collective-permute-start.9 = (f32[8,1280]{1,0:T(8,128)S(1)}, f32[8,1280]{1,0:T(8,128)S(1)}, u32[]{:S(2)}, u32[]{:S(2)}) collective-permute-start(f32[8,1280]{1,0:T(8,128)S(1)} %get-tuple-element.56), channel_id=1, source_target_pairs={{0,128},{32,160},{64,192},{96,224},{128,256},{160,288},{192,320},{... | collective-permute-start | bytes 122888 | tf_op jit(solution)/shard_map/ppermute | solution.py:20
  113.5 10.1 %collective-permute-start.11 = (f32[8,1280]{1,0:T(8,128)S(1)}, f32[8,1280]{1,0:T(8,128)S(1)}, u32[]{:S(2)}, u32[]{:S(2)}) collective-permute-start(f32[8,1280]{1,0:T(8,128)S(1)} %get-tuple-element.58), channel_id=1, source_target_pairs={{0,384},{32,416},{64,448},{96,480},{128,0},{160,32},{192,64},{224,... | collective-permute-start | bytes 122888 | tf_op jit(solution)/shard_map/ppermute | solution.py:20
  123.6 12.6 %collective-permute-start.12 = (f32[16,1280]{1,0:T(8,128)S(1)}, f32[16,1280]{1,0:T(8,128)S(1)}, u32[]{:S(2)}, u32[]{:S(2)}) collective-permute-start(f32[16,1280]{1,0:T(8,128)S(1)} %pad_maximum_fusion.8), channel_id=1, source_target_pairs={{0,384},{32,416},{64,448},{96,480},{128,0},{160,32},{192,64},{224,... | collective-permute-start | bytes 245768 | tf_op jit(solution)/shard_map/ppermute | solution.py:20
  129.7 9.9 %collective-permute-start.10 = (f32[16,1280]{1,0:T(8,128)S(1)}, f32[16,1280]{1,0:T(8,128)S(1)}, u32[]{:S(2)}, u32[]{:S(2)}) collective-permute-start(f32[16,1280]{1,0:T(8,128)S(1)} %pad_maximum_fusion.7), channel_id=1, source_target_pairs={{0,128},{32,160},{64,192},{96,224},{128,256},{160,288},{192,320},{... | collective-permute-start | bytes 245768 | tf_op jit(solution)/shard_map/ppermute | solution.py:20
  139.6 25.6 %copy-start.4 = (f32[384,1024]{1,0:T(8,128)}, f32[384,1024]{1,0:T(8,128)S(1)}, u32[]{:S(2)}) copy-start(f32[384,1024]{1,0:T(8,128)S(1)} %collective-permute-done.13) | copy-start | bytes 4718596
  139.6 12.1 %collective-permute-start.16 = (f32[16,1280]{1,0:T(8,128)S(1)}, f32[16,1280]{1,0:T(8,128)S(1)}, u32[]{:S(2)}, u32[]{:S(2)}) collective-permute-start(f32[16,1280]{1,0:T(8,128)S(1)} %fusion.24), channel_id=1, source_target_pairs={{0,128},{32,160},{64,192},{96,224},{128,256},{160,288},{192,320},{... | collective-permute-start | bytes 245768 | tf_op jit(solution)/shard_map/ppermute | solution.py:20
  143.2 11.0 %collective-permute-start.14 = (f32[16,1280]{1,0:T(8,128)S(1)}, f32[16,1280]{1,0:T(8,128)S(1)}, u32[]{:S(2)}, u32[]{:S(2)}) collective-permute-start(f32[16,1280]{1,0:T(8,128)S(1)} %fusion.24), channel_id=1, source_target_pairs={{0,384},{32,416},{64,448},{96,480},{128,0},{160,32},{192,64},{224,... | collective-permute-start | bytes 245768 | tf_op jit(solution)/shard_map/ppermute | solution.py:20
  151.8 13.4 %collective-permute-start.17 = (f32[8,1280]{1,0:T(8,128)S(1)}, f32[8,1280]{1,0:T(8,128)S(1)}, u32[]{:S(2)}, u32[]{:S(2)}) collective-permute-start(f32[8,1280]{1,0:T(8,128)S(1)} %slice.295), channel_id=1, source_target_pairs={{0,128},{32,160},{64,192},{96,224},{128,256},{160,288},{192,320},{... | collective-permute-start | bytes 122888 | tf_op jit(solution)/shard_map/ppermute | solution.py:20
  154.2 10.9 %collective-permute-start.15 = (f32[8,1280]{1,0:T(8,128)S(1)}, f32[8,1280]{1,0:T(8,128)S(1)}, u32[]{:S(2)}, u32[]{:S(2)}) collective-permute-start(f32[8,1280]{1,0:T(8,128)S(1)} %slice.294), channel_id=1, source_target_pairs={{0,384},{32,416},{64,448},{96,480},{128,0},{160,32},{192,64},{224,... | collective-permute-start | bytes 122888 | tf_op jit(solution)/shard_map/ppermute | solution.py:20
  161.8 28.2 %collective-permute-start.22 = (f32[256,1024]{1,0:T(8,128)S(1)}, f32[256,1024]{1,0:T(8,128)S(1)}, u32[]{:S(2)}, u32[]{:S(2)}) collective-permute-start(f32[256,1024]{1,0:T(8,128)S(1)} %pad_maximum_fusion.4), channel_id=1, source_target_pairs={{0,16},{16,0},{1,17},{17,1},{2,18},{18,2},{3,19},{19,3},{4,20},{20... | collective-permute-start | bytes 3145736 | tf_op jit(solution)/shard_map/ppermute | solution.py:24
  165.2 29.4 %collective-permute-start.21 = (f32[4,16,1280]{2,1,0:T(8,128)S(1)}, f32[4,16,1280]{2,1,0:T(8,128)S(1)}, u32[]{:S(2)}, u32[]{:S(2)}) collective-permute-start(f32[4,16,1280]{2,1,0:T(8,128)S(1)} %pad_maximum_fusion.6), channel_id=1, source_target_pairs={{0,32},{32,64},{64,96},{96,128},{128,160},{160,192},{192,224},{224... | collective-permute-start | bytes 983048 | tf_op jit(solution)/shard_map/ppermute | solution.py:20
  169.8 24.8 %collective-permute-start.18 = (f32[4,16,1280]{2,1,0:T(8,128)S(1)}, f32[4,16,1280]{2,1,0:T(8,128)S(1)}, u32[]{:S(2)}, u32[]{:S(2)}) collective-permute-start(f32[4,16,1280]{2,1,0:T(8,128)S(1)} %pad_maximum_fusion.6), channel_id=1, source_target_pairs={{0,480},{32,0},{64,32},{96,64},{128,96},{160,128},{192,160},{224,1... | collective-permute-start | bytes 983048 | tf_op jit(solution)/shard_map/ppermute | solution.py:20
  171.8 12.1 %copy-start = (f32[1024,1024]{1,0:T(8,128)S(1)}, f32[1024,1024]{1,0:T(8,128)}, u32[]{:S(2)}) copy-start(f32[1024,1024]{1,0:T(8,128)} %all-gather.2.cloned.1.call-done) | copy-start | bytes 12582916
  176.1 13.8 %copy-start.1 = (f32[256,1024]{1,0:T(8,128)}, f32[256,1024]{1,0:T(8,128)S(1)}, u32[]{:S(2)}) copy-start(f32[256,1024]{1,0:T(8,128)S(1)} %fusion.30) | copy-start | bytes 3145732
  176.2 18.3 %collective-permute-start.20 = (f32[4,8,1280]{2,1,0:T(8,128)S(1)}, f32[4,8,1280]{2,1,0:T(8,128)S(1)}, u32[]{:S(2)}, u32[]{:S(2)}) collective-permute-start(f32[4,8,1280]{2,1,0:T(8,128)S(1)} %get-tuple-element.53), channel_id=1, source_target_pairs={{0,64},{32,96},{64,128},{96,160},{128,192},{160,224},{192,256},{22... | collective-permute-start | bytes 491528 | tf_op jit(solution)/shard_map/ppermute | solution.py:20
  179.3 10.7 %copy-start.5 = (f32[384,1024]{1,0:T(8,128)S(1)}, f32[384,1024]{1,0:T(8,128)}, u32[]{:S(2)}) copy-start(f32[384,1024]{1,0:T(8,128)} %copy-done.4) | copy-start | bytes 4718596
  179.3 15.2 %collective-permute-start.19 = (f32[4,8,1280]{2,1,0:T(8,128)S(1)}, f32[4,8,1280]{2,1,0:T(8,128)S(1)}, u32[]{:S(2)}, u32[]{:S(2)}) collective-permute-start(f32[4,8,1280]{2,1,0:T(8,128)S(1)} %get-tuple-element.52), channel_id=1, source_target_pairs={{0,448},{32,480},{64,0},{96,32},{128,64},{160,96},{192,128},{224,1... | collective-permute-start | bytes 491528 | tf_op jit(solution)/shard_map/ppermute | solution.py:20
  200.8 16.5 %collective-permute-start.23 = (f32[16,8,1152]{2,1,0:T(8,128)S(1)}, f32[16,8,1152]{2,1,0:T(8,128)S(1)}, u32[]{:S(2)}, u32[]{:S(2)}) collective-permute-start(f32[16,8,1152]{2,1,0:T(8,128)S(1)} %dynamic-slice_bitcast_fusion), channel_id=1, source_target_pairs={{0,1},{1,0},{2,3},{3,2},{4,5},{5,4},{6,7},{7,6},{8,9},{9,8},{10,11... | collective-permute-start | bytes 1769480 | tf_op jit(solution)/shard_map/ppermute | solution.py:172
  218.2 18.3 %all-to-all-start = ((f32[16,8,1152]{2,1,0:T(8,128)}), f32[16,8,1152]{2,1,0:T(8,128)S(1)}, u32[]{:S(2)}, u32[]{:S(2)}) async-start(f32[16,8,1152]{2,1,0:T(8,128)} %bitcast_add_fusion), calls=%async_computation | async-start | bytes 1179648 | tf_op jit(solution)/shard_map/all_to_all | solution.py:173
  (3 other events, 13.0 us)
Sparse Core Ops, SparseCore 0:
  27.2 105.7 all-gather.1

commit v2 on v1

--- a/solution.py
+++ b/solution.py
@@ -63,10 +63,16 @@
 
 
 def gather_near(parts):
-    plus1 = shift_z(parts, -1)
-    minus1 = shift_z(parts, 1)
-    plus2 = shift_z(parts[:, :8], -2)
-    minus2 = shift_z(parts[:, 8:], 2)
+    return (
+        parts,
+        shift_z(parts, -1),
+        shift_z(parts, 1),
+        shift_z(parts[:, :8], -2),
+        shift_z(parts[:, 8:], 2),
+    )
+
+
+def joined(parts, plus1, minus1, plus2, minus2):
     two = jnp.concatenate([plus2, jnp.roll(minus2, -1, axis=0)], axis=1)
     three = jnp.roll(minus1, -1, axis=0)
     return jnp.stack([parts, plus1, two, three], axis=1)
@@ -84,7 +90,9 @@
     total_rows = rows * lax.axis_size("z") * lax.axis_size("yh")
 
     own_rows = inverse_factors[0]
-    swapped = swap_y(jnp.concatenate([train, own_rows]))
+    swapped, plus1, minus1 = lax.optimization_barrier(
+        (swap_y(jnp.concatenate([train, own_rows])), shift_z(query, -1), shift_z(query, 1))
+    )
     other_train, other_rows = swapped[:rows], swapped[rows:]
     pair_rows = jnp.where(
         first_half,
@@ -92,8 +100,6 @@
         jnp.concatenate([other_rows, own_rows]),
     )
     inverse = lax.all_gather(pair_rows, "z", axis=0, tiled=True)
-
-    plus1, minus1 = shift_z(query, -1), shift_z(query, 1)
 
     pair_train = jnp.where(
         first_half,
@@ -104,26 +110,28 @@
     strip0 = dot(turned[:, :quarter], turned[:, : 3 * quarter], ((0,), (0,)))
     strip2 = dot(turned[:, 2 * quarter : 3 * quarter], turned[:, 2 * quarter :], ((0,), (0,)))
     partial = jnp.concatenate([strip0, strip2], axis=1)
-    blocks, plus1, minus1 = lax.optimization_barrier(
-        (partial.reshape(4, 4, quarter // 16, 5 * quarter), plus1, minus1)
-    )
-    plus2, minus2 = shift_z(plus1, -1), shift_z(minus1, 1)
+    blocks = partial.reshape(4, 4, quarter // 16, 5 * quarter)
     own_queries1 = jnp.concatenate([minus1, query, plus1])
     other_queries1 = swap_y(own_queries1)
-    near_sums, plus2, minus2 = lax.optimization_barrier((reduce_near(blocks, place), plus2, minus2))
+    near_sums, plus1, minus1 = lax.optimization_barrier((reduce_near(blocks, place), plus1, minus1))
+    plus2, minus2 = shift_z(plus1, -1), shift_z(minus1, 1)
+    part, plus2, minus2, other_queries1 = lax.optimization_barrier(
+        (reduce_far(near_sums, place), plus2, minus2, other_queries1)
+    )
     own_queries2 = jnp.concatenate([minus2, plus2])
-    part, other_queries1 = lax.optimization_barrier((reduce_far(near_sums, place), other_queries1))
-    other_queries2 = swap_y(after(own_queries2, other_queries1))
-    parts, inverse = lax.optimization_barrier((gather_far(part), inverse))
-    gathered = gather_near(parts).reshape(quarter, 5 * quarter)
-    strips = jnp.roll(gathered, place * (quarter // 16), axis=0)
-
+    other_queries2 = swap_y(own_queries2)
+    parts, other_queries2 = lax.optimization_barrier((gather_far(part), other_queries2))
     own_queries = jnp.concatenate([own_queries1, own_queries2])
     other_queries = jnp.concatenate([other_queries1, other_queries2])
     own_first = dot(own_queries, inverse, ((1,), (1,)))
     other_first = dot(other_queries, inverse, ((1,), (1,)))
 
     side = dot(pair_train, inverse, ((1,), (0,)))
+    pieces, side, own_first, other_first = lax.optimization_barrier(
+        (gather_near(parts), side, own_first, other_first)
+    )
+    gathered = joined(*pieces).reshape(quarter, 5 * quarter)
+    strips = jnp.roll(gathered, place * (quarter // 16), axis=0)
     side_turned = jnp.where(first_half, side, jnp.roll(side, -quarter, axis=1))
     s0, s1, s2, s3 = (side_turned[:, i * quarter : (i + 1) * quarter] for i in range(4))
     b00, b01, b02, b22, b23 = (strips[:, i * quarter : (i + 1) * quarter] for i in range(5))

time: 245 us -> 229 us (0.935)
  waiting for transfers between devices: 74.6 us -> 58 us
  starting transfers between devices: 121 us -> 110 us
  other arithmetic: 8.09 us -> 13.3 us
  local copies, waits for them, and re-layouts: 5.69 us -> 10.7 us
    ppermute x3, waiting for transfers between devices: 11.1 us -> 0.01 us  [swap_y(): return lax.ppermute(value, 'yh', [(0, 1), (1, 0)])]
    ppermute x20, waiting for transfers between devices: 50.5 us -> 45 us  [shift_z(): lax.ppermute(value, 'z', [(i, (i + steps) % count) for i in range(count)])]
    ppermute x20, starting transfers between devices: 85 us -> 80.5 us  [shift_z(): lax.ppermute(value, 'z', [(i, (i + steps) % count) for i in range(count)])]
    ppermute x3, starting transfers between devices: 13.9 us -> 9.51 us  [swap_y(): return lax.ppermute(value, 'yh', [(0, 1), (1, 0)])]
    unnamed x27 -> x31, local copies, waits for them, and re-layouts: 4.46 us -> 6.04 us
  transfers between devices with their start and end apart: 26 -> 26, of which waited for: 12 -> 10; matrix products, arithmetic and copies ran while one was open for 9% -> 13% of each run, Pallas kernels for 0% -> 0%
where the time goes in v2:
time: 229 us; the launch traced here: 228 us
  starting transfers between devices  110 us (48%)
  waiting for transfers between devices  58 us (25%)
  matrix products  21.1 us (9%)
  between operations  14.3 us (6%)
  other arithmetic  13.3 us (6%)
  local copies, waits for them, and re-layouts  10.7 us (5%)
    ppermute x20, starting transfers between devices, shift_z(): lax.ppermute(value, 'z', [(i, (i + steps) % count) for i in range(count)])  80.5 us
    ppermute x20, waiting for transfers between devices, shift_z(): lax.ppermute(value, 'z', [(i, (i + steps) % count) for i in range(count)])  45 us
    dot_general x11, matrix products, dot(): lax.dot_general(left, right, (dims, ((), ())), precision=FAST, preferred_...  21.1 us
    ppermute x1, starting transfers between devices, on_device(): halves = kept + lax.ppermute(sent, 'c', [(0, 1), (1, 0)])  12.9 us
    all_to_all x1, waiting for transfers between devices, on_device(): lax.all_to_all(halves.reshape(shares * own, window), ('yh', 'yl', 'x'), 0...  11.3 us
    ppermute x3, starting transfers between devices, swap_y(): return lax.ppermute(value, 'yh', [(0, 1), (1, 0)])  9.51 us
    all_to_all x1, starting transfers between devices, on_device(): lax.all_to_all(halves.reshape(shares * own, window), ('yh', 'yl', 'x'), 0...  7.57 us
    unnamed x31, local copies, waits for them, and re-layouts  6.04 us
  transfers between devices with their start and end apart: 26, of which 10 were waited for; matrix products, arithmetic and copies ran while one was open for 13% of the time, Pallas kernels for 0%

profile of v2, /device:TPU:1, one launch (start us, length us, event | category | flops | bytes accessed | tf_op | source)
XLA Modules:
  0.0 227.9 jit_solution(4506885580391851350)
XLA Ops:
  10.3 5.6 %collective-permute-start = (f32[160,1024]{1,0:T(8,128)}, f32[160,1024]{1,0:T(8,128)S(1)}, u32[]{:S(2)}, u32[]{:S(2)}) collective-permute-start(f32[160,1024]{1,0:T(8,128)} %pad_maximum_fusion.5), channel_id=1, source_target_pairs={{0,16},{16,0},{1,17},{17,1},{2,18},{18,2},{3,19},{19,3},{4,20},{20... | collective-permute-start | bytes 1966088 | tf_op jit(solution)/shard_map/ppermute | solution.py:24
  16.1 11.1 %collective-permute-start.1 = (f32[128,1024]{1,0:T(8,128)S(1)}, f32[128,1024]{1,0:T(8,128)S(1)}, u32[]{:S(2)}, u32[]{:S(2)}) collective-permute-start(f32[128,1024]{1,0:T(8,128)S(1)} %bitcast.81), channel_id=1, source_target_pairs={{0,480},{32,0},{64,32},{96,64},{128,96},{160,128},{192,160},{224,1... | collective-permute-start | bytes 1572872 | tf_op jit(solution)/shard_map/ppermute | solution.py:20
  27.2 1.9 collective-permute-start.2
  29.1 8.3 %collective-permute-done.1 = f32[128,1024]{1,0:T(8,128)S(1)} collective-permute-done((f32[128,1024]{1,0:T(8,128)S(1)}, f32[128,1024]{1,0:T(8,128)S(1)}, u32[]{:S(2)}, u32[]{:S(2)}) %collective-permute-start.1) | collective-permute-done | bytes 524320 | tf_op jit(solution)/shard_map/ppermute | solution.py:20
  37.4 5.0 %collective-permute-done.2 = f32[128,1024]{1,0:T(8,128)S(1)} collective-permute-done((f32[128,1024]{1,0:T(8,128)S(1)}, f32[128,1024]{1,0:T(8,128)S(1)}, u32[]{:S(2)}, u32[]{:S(2)}) %collective-permute-start.2) | collective-permute-done | bytes 524320 | tf_op jit(solution)/shard_map/ppermute | solution.py:20
  47.8 4.6 %collective-permute-start.4 = (f32[4,16,1280]{2,1,0:T(8,128)}, f32[4,16,1280]{2,1,0:T(8,128)}, u32[]{:S(2)}, u32[]{:S(2)}) collective-permute-start(f32[4,16,1280]{2,1,0:T(8,128)} %get-tuple-element.53), channel_id=1, source_target_pairs={{0,480},{32,0},{64,32},{96,64},{128,96},{160,128},{192,160},{224,1... | collective-permute-start | bytes 983048 | tf_op jit(solution)/shard_map/ppermute | solution.py:20
  55.0 5.5 %collective-permute-start.6 = (f32[4,8,1280]{2,1,0:T(8,128)}, f32[4,8,1280]{2,1,0:T(8,128)}, u32[]{:S(2)}, u32[]{:S(2)}) collective-permute-start(f32[4,8,1280]{2,1,0:T(8,128)} %get-tuple-element.79), channel_id=1, source_target_pairs={{0,448},{32,480},{64,0},{96,32},{128,64},{160,96},{192,128},{224,1... | collective-permute-start | bytes 491528 | tf_op jit(solution)/shard_map/ppermute | solution.py:20
  60.6 2.5 %pad_maximum_fusion = f32[384,1024]{1,0:T(8,128)} fusion(f32[128,1024]{1,0:T(8,128)S(1)} %collective-permute-done.1, f32[128,1024]{1,0:T(8,128)} %bitcast.83, f32[128,1024]{1,0:T(8,128)} %copy-done.2), kind=kLoop, calls=%fused_computation.6 | loop fusion | flops 786432 | bytes 3145728 | tf_op jit(solution)/shard_map/concatenate | solution.py:114
  63.1 2.0 collective-permute-start.13
  65.1 3.2 %collective-permute-done.5 = f32[4,8,1280]{2,1,0:T(8,128)} collective-permute-done((f32[4,8,1280]{2,1,0:T(8,128)}, f32[4,8,1280]{2,1,0:T(8,128)}, u32[]{:S(2)}, u32[]{:S(2)}) %collective-permute-start.5) | collective-permute-done | bytes 163872 | tf_op jit(solution)/shard_map/ppermute | solution.py:20
  68.3 2.0 collective-permute-done.6
  72.3 4.9 %collective-permute-start.7 = (f32[8,1280]{1,0:T(8,128)S(1)}, f32[8,1280]{1,0:T(8,128)S(1)}, u32[]{:S(2)}, u32[]{:S(2)}) collective-permute-start(f32[8,1280]{1,0:T(8,128)S(1)} %get-tuple-element.74), channel_id=1, source_target_pairs={{0,128},{32,160},{64,192},{96,224},{128,256},{160,288},{192,320},{... | collective-permute-start | bytes 122888 | tf_op jit(solution)/shard_map/ppermute | solution.py:20
  77.2 4.3 %collective-permute-start.9 = (f32[8,1280]{1,0:T(8,128)S(1)}, f32[8,1280]{1,0:T(8,128)S(1)}, u32[]{:S(2)}, u32[]{:S(2)}) collective-permute-start(f32[8,1280]{1,0:T(8,128)S(1)} %get-tuple-element.76), channel_id=1, source_target_pairs={{0,384},{32,416},{64,448},{96,480},{128,0},{160,32},{192,64},{224,... | collective-permute-start | bytes 122888 | tf_op jit(solution)/shard_map/ppermute | solution.py:20
  81.6 4.4 %collective-permute-start.11 = (f32[128,1024]{1,0:T(8,128)S(1)}, f32[128,1024]{1,0:T(8,128)S(1)}, u32[]{:S(2)}, u32[]{:S(2)}) collective-permute-start(f32[128,1024]{1,0:T(8,128)S(1)} %collective-permute-done.1), channel_id=1, source_target_pairs={{0,480},{32,0},{64,32},{96,64},{128,96},{160,128},{192,160},{224,1... | collective-permute-start | bytes 1572872 | tf_op jit(solution)/shard_map/ppermute | solution.py:20
  88.8 4.0 %collective-permute-start.8 = (f32[16,1280]{1,0:T(8,128)S(1)}, f32[16,1280]{1,0:T(8,128)S(1)}, u32[]{:S(2)}, u32[]{:S(2)}) collective-permute-start(f32[16,1280]{1,0:T(8,128)S(1)} %pad_maximum_fusion.7), channel_id=1, source_target_pairs={{0,128},{32,160},{64,192},{96,224},{128,256},{160,288},{192,320},{... | collective-permute-start | bytes 245768 | tf_op jit(solution)/shard_map/ppermute | solution.py:20
  92.9 5.1 %collective-permute-start.10 = (f32[16,1280]{1,0:T(8,128)S(1)}, f32[16,1280]{1,0:T(8,128)S(1)}, u32[]{:S(2)}, u32[]{:S(2)}) collective-permute-start(f32[16,1280]{1,0:T(8,128)S(1)} %pad_maximum_fusion.8), channel_id=1, source_target_pairs={{0,384},{32,416},{64,448},{96,480},{128,0},{160,32},{192,64},{224,... | collective-permute-start | bytes 245768 | tf_op jit(solution)/shard_map/ppermute | solution.py:20
  99.9 19.1 %collective-permute-done.8 = f32[16,1280]{1,0:T(8,128)S(1)} collective-permute-done((f32[16,1280]{1,0:T(8,128)S(1)}, f32[16,1280]{1,0:T(8,128)S(1)}, u32[]{:S(2)}, u32[]{:S(2)}) %collective-permute-start.8) | collective-permute-done | bytes 81952 | tf_op jit(solution)/shard_map/ppermute | solution.py:20
  120.0 1.9 collective-permute-start.18
  123.7 4.2 %collective-permute-start.14 = (f32[16,1280]{1,0:T(8,128)S(1)}, f32[16,1280]{1,0:T(8,128)S(1)}, u32[]{:S(2)}, u32[]{:S(2)}) collective-permute-start(f32[16,1280]{1,0:T(8,128)S(1)} %fusion.24), channel_id=1, source_target_pairs={{0,384},{32,416},{64,448},{96,480},{128,0},{160,32},{192,64},{224,... | collective-permute-start | bytes 245768 | tf_op jit(solution)/shard_map/ppermute | solution.py:20
  127.9 5.0 %collective-permute-start.16 = (f32[16,1280]{1,0:T(8,128)S(1)}, f32[16,1280]{1,0:T(8,128)S(1)}, u32[]{:S(2)}, u32[]{:S(2)}) collective-permute-start(f32[16,1280]{1,0:T(8,128)S(1)} %fusion.24), channel_id=1, source_target_pairs={{0,128},{32,160},{64,192},{96,224},{128,256},{160,288},{192,320},{... | collective-permute-start | bytes 245768 | tf_op jit(solution)/shard_map/ppermute | solution.py:20
  133.7 2.7 %collective-permute-done.14 = f32[16,1280]{1,0:T(8,128)S(1)} collective-permute-done((f32[16,1280]{1,0:T(8,128)S(1)}, f32[16,1280]{1,0:T(8,128)S(1)}, u32[]{:S(2)}, u32[]{:S(2)}) %collective-permute-start.14) | collective-permute-done | bytes 81952 | tf_op jit(solution)/shard_map/ppermute | solution.py:20
  136.4 3.5 %collective-permute-start.15 = (f32[8,1280]{1,0:T(8,128)S(1)}, f32[8,1280]{1,0:T(8,128)S(1)}, u32[]{:S(2)}, u32[]{:S(2)}) collective-permute-start(f32[8,1280]{1,0:T(8,128)S(1)} %slice.293), channel_id=1, source_target_pairs={{0,384},{32,416},{64,448},{96,480},{128,0},{160,32},{192,64},{224,... | collective-permute-start | bytes 122888 | tf_op jit(solution)/shard_map/ppermute | solution.py:20
  140.9 4.8 %collective-permute-start.17 = (f32[8,1280]{1,0:T(8,128)S(1)}, f32[8,1280]{1,0:T(8,128)S(1)}, u32[]{:S(2)}, u32[]{:S(2)}) collective-permute-start(f32[8,1280]{1,0:T(8,128)S(1)} %slice.294), channel_id=1, source_target_pairs={{0,128},{32,160},{64,192},{96,224},{128,256},{160,288},{192,320},{... | collective-permute-start | bytes 122888 | tf_op jit(solution)/shard_map/ppermute | solution.py:20
  146.5 3.7 %collective-permute-done.17 = f32[8,1280]{1,0:T(8,128)S(1)} collective-permute-done((f32[8,1280]{1,0:T(8,128)S(1)}, f32[8,1280]{1,0:T(8,128)S(1)}, u32[]{:S(2)}, u32[]{:S(2)}) %collective-permute-start.17) | collective-permute-done | bytes 40992 | tf_op jit(solution)/shard_map/ppermute | solution.py:20
  152.2 3.4 %collective-permute-start.20 = (f32[4,16,1280]{2,1,0:T(8,128)S(1)}, f32[4,16,1280]{2,1,0:T(8,128)S(1)}, u32[]{:S(2)}, u32[]{:S(2)}) collective-permute-start(f32[4,16,1280]{2,1,0:T(8,128)S(1)} %pad_maximum_fusion.6), channel_id=1, source_target_pairs={{0,32},{32,64},{64,96},{96,128},{128,160},{160,192},{192,224},{224... | collective-permute-start | bytes 983048 | tf_op jit(solution)/shard_map/ppermute | solution.py:20
  158.2 4.3 %collective-permute-start.22 = (f32[4,8,1280]{2,1,0:T(8,128)}, f32[4,8,1280]{2,1,0:T(8,128)S(1)}, u32[]{:S(2)}, u32[]{:S(2)}) collective-permute-start(f32[4,8,1280]{2,1,0:T(8,128)} %get-tuple-element.70), channel_id=1, source_target_pairs={{0,64},{32,96},{64,128},{96,160},{128,192},{160,224},{192,256},{22... | collective-permute-start | bytes 491528 | tf_op jit(solution)/shard_map/ppermute | solution.py:20
  162.5 7.7 %fusion.31 = f32[640,1024]{1,0:T(8,128)S(1)} fusion(f32[640,1024]{1,0:T(8,128)} %constant_dynamic-update-slice_fusion, f32[1024,1024]{1,0:T(8,128)} %all-gather.2.cloned.1.call-done), kind=kOutput, calls=%fused_computation.97 | convolution fusion | flops 4026531840 | bytes 9437184 | tf_op jit(solution)/shard_map/dot_general | solution.py:13
  170.2 5.7 %fusion = f32[640,1024]{1,0:T(8,128)S(1)} fusion(f32[1024,1024]{1,0:T(8,128)S(1)} %copy-done, f32[256,1024]{1,0:T(8,128)S(1)} %collective-permute-done.18, f32[384,1024]{1,0:T(8,128)} %collective-permute-done.13), kind=kOutput, calls=%fused_computation | convolution fusion | flops 4027187200 | bytes 9437184 | tf_op jit(solution)/shard_map/dot_general | solution.py:13
  175.9 2.1 fusion.30
  185.9 12.9 %collective-permute-start.23 = (f32[16,8,1152]{2,1,0:T(8,128)S(1)}, f32[16,8,1152]{2,1,0:T(8,128)S(1)}, u32[]{:S(2)}, u32[]{:S(2)}) collective-permute-start(f32[16,8,1152]{2,1,0:T(8,128)S(1)} %dynamic-slice_bitcast_fusion), channel_id=1, source_target_pairs={{0,1},{1,0},{2,3},{3,2},{4,5},{5,4},{6,7},{7,6},{8,9},{9,8},{10,11... | collective-permute-start | bytes 1769480 | tf_op jit(solution)/shard_map/ppermute | solution.py:180
  201.3 7.6 %all-to-all-start = ((f32[16,8,1152]{2,1,0:T(8,128)}), f32[16,8,1152]{2,1,0:T(8,128)S(1)}, u32[]{:S(2)}, u32[]{:S(2)}) async-start(f32[16,8,1152]{2,1,0:T(8,128)} %bitcast_add_fusion), calls=%async_computation | async-start | bytes 1179648 | tf_op jit(solution)/shard_map/all_to_all | solution.py:181
  209.0 11.3 %all-to-all-done = f32[16,8,1152]{2,1,0:T(8,128)S(1)} async-done(((f32[16,8,1152]{2,1,0:T(8,128)}), f32[16,8,1152]{2,1,0:T(8,128)S(1)}, u32[]{:S(2)}, u32[]{:S(2)}) %all-to-all-start) | async-done | bytes 589856 | tf_op jit(solution)/shard_map/all_to_all | solution.py:181
  (112 shorter events, 39.3 us)
Async XLA Ops:
  6.5 36.0 %copy-start.5 = (f32[1,32,1024]{2,1,0:T(8,128)S(1)}, f32[1,32,1024]{2,1,0:T(8,128)}, u32[]{:S(2)}) copy-start(f32[1,32,1024]{2,1,0:T(8,128)} %param.6) | copy-start | bytes 393220
  6.5 9.4 %copy-start.1 = (f32[128,1,1024]{2,1,0:T(1,128)S(1)}, f32[128,1,1024]{2,1,0:T(1,128)}, u32[]{:S(2)}) copy-start(f32[128,1,1024]{2,1,0:T(1,128)} %param.5) | copy-start | bytes 1572868
  6.5 156.0 %all-gather.2.cloned.1.call-start = ((), (), s32[]{:S(2)}) async-start(), calls=%async_computation.1 | async-start | bytes 4456448 | tf_op jit(solution)/shard_map/all_gather | solution.py:102
  10.3 32.2 %collective-permute-start = (f32[160,1024]{1,0:T(8,128)}, f32[160,1024]{1,0:T(8,128)S(1)}, u32[]{:S(2)}, u32[]{:S(2)}) collective-permute-start(f32[160,1024]{1,0:T(8,128)} %pad_maximum_fusion.5), channel_id=1, source_target_pairs={{0,16},{16,0},{1,17},{17,1},{2,18},{18,2},{3,19},{19,3},{4,20},{20... | collective-permute-start | bytes 1966088 | tf_op jit(solution)/shard_map/ppermute | solution.py:24
  16.1 27.3 %copy-start.3 = (f32[128,1,1024]{2,0,1:T(8,128)}, f32[128,1,1024]{2,0,1:T(8,128)S(1)}, u32[]{:S(2)}) copy-start(f32[128,1,1024]{2,0,1:T(8,128)S(1)} %copy.20) | copy-start | bytes 1572868
  16.1 21.4 %collective-permute-start.1 = (f32[128,1024]{1,0:T(8,128)S(1)}, f32[128,1024]{1,0:T(8,128)S(1)}, u32[]{:S(2)}, u32[]{:S(2)}) collective-permute-start(f32[128,1024]{1,0:T(8,128)S(1)} %bitcast.81), channel_id=1, source_target_pairs={{0,480},{32,0},{64,32},{96,64},{128,96},{160,128},{192,160},{224,1... | collective-permute-start | bytes 1572872 | tf_op jit(solution)/shard_map/ppermute | solution.py:20
  27.2 15.3 %collective-permute-start.2 = (f32[128,1024]{1,0:T(8,128)S(1)}, f32[128,1024]{1,0:T(8,128)S(1)}, u32[]{:S(2)}, u32[]{:S(2)}) collective-permute-start(f32[128,1024]{1,0:T(8,128)S(1)} %bitcast.82), channel_id=1, source_target_pairs={{0,32},{32,64},{64,96},{96,128},{128,160},{160,192},{192,224},{224... | collective-permute-start | bytes 1572872 | tf_op jit(solution)/shard_map/ppermute | solution.py:20
  45.8 24.4 %collective-permute-start.3 = (f32[4,16,1280]{2,1,0:T(8,128)}, f32[4,16,1280]{2,1,0:T(8,128)}, u32[]{:S(2)}, u32[]{:S(2)}) collective-permute-start(f32[4,16,1280]{2,1,0:T(8,128)} %get-tuple-element.51), channel_id=1, source_target_pairs={{0,32},{32,64},{64,96},{96,128},{128,160},{160,192},{192,224},{224... | collective-permute-start | bytes 983048 | tf_op jit(solution)/shard_map/ppermute | solution.py:20
  47.8 22.5 %collective-permute-start.4 = (f32[4,16,1280]{2,1,0:T(8,128)}, f32[4,16,1280]{2,1,0:T(8,128)}, u32[]{:S(2)}, u32[]{:S(2)}) collective-permute-start(f32[4,16,1280]{2,1,0:T(8,128)} %get-tuple-element.53), channel_id=1, source_target_pairs={{0,480},{32,0},{64,32},{96,64},{128,96},{160,128},{192,160},{224,1... | collective-permute-start | bytes 983048 | tf_op jit(solution)/shard_map/ppermute | solution.py:20
  53.1 15.2 %collective-permute-start.5 = (f32[4,8,1280]{2,1,0:T(8,128)}, f32[4,8,1280]{2,1,0:T(8,128)}, u32[]{:S(2)}, u32[]{:S(2)}) collective-permute-start(f32[4,8,1280]{2,1,0:T(8,128)} %get-tuple-element.78), channel_id=1, source_target_pairs={{0,64},{32,96},{64,128},{96,160},{128,192},{160,224},{192,256},{22... | collective-permute-start | bytes 491528 | tf_op jit(solution)/shard_map/ppermute | solution.py:20
  55.0 15.2 %collective-permute-start.6 = (f32[4,8,1280]{2,1,0:T(8,128)}, f32[4,8,1280]{2,1,0:T(8,128)}, u32[]{:S(2)}, u32[]{:S(2)}) collective-permute-start(f32[4,8,1280]{2,1,0:T(8,128)} %get-tuple-element.79), channel_id=1, source_target_pairs={{0,448},{32,480},{64,0},{96,32},{128,64},{160,96},{192,128},{224,1... | collective-permute-start | bytes 491528 | tf_op jit(solution)/shard_map/ppermute | solution.py:20
  63.1 56.8 %collective-permute-start.13 = (f32[384,1024]{1,0:T(8,128)}, f32[384,1024]{1,0:T(8,128)}, u32[]{:S(2)}, u32[]{:S(2)}) collective-permute-start(f32[384,1024]{1,0:T(8,128)} %pad_maximum_fusion), channel_id=1, source_target_pairs={{0,16},{16,0},{1,17},{17,1},{2,18},{18,2},{3,19},{19,3},{4,20},{20... | collective-permute-start | bytes 4718600 | tf_op jit(solution)/shard_map/ppermute | solution.py:24
  72.3 15.6 %collective-permute-start.7 = (f32[8,1280]{1,0:T(8,128)S(1)}, f32[8,1280]{1,0:T(8,128)S(1)}, u32[]{:S(2)}, u32[]{:S(2)}) collective-permute-start(f32[8,1280]{1,0:T(8,128)S(1)} %get-tuple-element.74), channel_id=1, source_target_pairs={{0,128},{32,160},{64,192},{96,224},{128,256},{160,288},{192,320},{... | collective-permute-start | bytes 122888 | tf_op jit(solution)/shard_map/ppermute | solution.py:20
  77.2 10.7 %collective-permute-start.9 = (f32[8,1280]{1,0:T(8,128)S(1)}, f32[8,1280]{1,0:T(8,128)S(1)}, u32[]{:S(2)}, u32[]{:S(2)}) collective-permute-start(f32[8,1280]{1,0:T(8,128)S(1)} %get-tuple-element.76), channel_id=1, source_target_pairs={{0,384},{32,416},{64,448},{96,480},{128,0},{160,32},{192,64},{224,... | collective-permute-start | bytes 122888 | tf_op jit(solution)/shard_map/ppermute | solution.py:20
  81.6 38.3 %collective-permute-start.11 = (f32[128,1024]{1,0:T(8,128)S(1)}, f32[128,1024]{1,0:T(8,128)S(1)}, u32[]{:S(2)}, u32[]{:S(2)}) collective-permute-start(f32[128,1024]{1,0:T(8,128)S(1)} %collective-permute-done.1), channel_id=1, source_target_pairs={{0,480},{32,0},{64,32},{96,64},{128,96},{160,128},{192,160},{224,1... | collective-permute-start | bytes 1572872 | tf_op jit(solution)/shard_map/ppermute | solution.py:20
  86.0 33.9 %collective-permute-start.12 = (f32[128,1024]{1,0:T(8,128)}, f32[128,1024]{1,0:T(8,128)S(1)}, u32[]{:S(2)}, u32[]{:S(2)}) collective-permute-start(f32[128,1024]{1,0:T(8,128)} %copy-done.2), channel_id=1, source_target_pairs={{0,32},{32,64},{64,96},{96,128},{128,160},{160,192},{192,224},{224... | collective-permute-start | bytes 1572872 | tf_op jit(solution)/shard_map/ppermute | solution.py:20
  88.8 30.2 %collective-permute-start.8 = (f32[16,1280]{1,0:T(8,128)S(1)}, f32[16,1280]{1,0:T(8,128)S(1)}, u32[]{:S(2)}, u32[]{:S(2)}) collective-permute-start(f32[16,1280]{1,0:T(8,128)S(1)} %pad_maximum_fusion.7), channel_id=1, source_target_pairs={{0,128},{32,160},{64,192},{96,224},{128,256},{160,288},{192,320},{... | collective-permute-start | bytes 245768 | tf_op jit(solution)/shard_map/ppermute | solution.py:20
  92.9 26.1 %collective-permute-start.10 = (f32[16,1280]{1,0:T(8,128)S(1)}, f32[16,1280]{1,0:T(8,128)S(1)}, u32[]{:S(2)}, u32[]{:S(2)}) collective-permute-start(f32[16,1280]{1,0:T(8,128)S(1)} %pad_maximum_fusion.8), channel_id=1, source_target_pairs={{0,384},{32,416},{64,448},{96,480},{128,0},{160,32},{192,64},{224,... | collective-permute-start | bytes 245768 | tf_op jit(solution)/shard_map/ppermute | solution.py:20
  120.0 30.2 %collective-permute-start.18 = (f32[256,1024]{1,0:T(8,128)S(1)}, f32[256,1024]{1,0:T(8,128)S(1)}, u32[]{:S(2)}, u32[]{:S(2)}) collective-permute-start(f32[256,1024]{1,0:T(8,128)S(1)} %pad_maximum_fusion.4), channel_id=1, source_target_pairs={{0,16},{16,0},{1,17},{17,1},{2,18},{18,2},{3,19},{19,3},{4,20},{20... | collective-permute-start | bytes 3145736 | tf_op jit(solution)/shard_map/ppermute | solution.py:24
  123.7 12.7 %collective-permute-start.14 = (f32[16,1280]{1,0:T(8,128)S(1)}, f32[16,1280]{1,0:T(8,128)S(1)}, u32[]{:S(2)}, u32[]{:S(2)}) collective-permute-start(f32[16,1280]{1,0:T(8,128)S(1)} %fusion.24), channel_id=1, source_target_pairs={{0,384},{32,416},{64,448},{96,480},{128,0},{160,32},{192,64},{224,... | collective-permute-start | bytes 245768 | tf_op jit(solution)/shard_map/ppermute | solution.py:20
  127.9 12.9 %collective-permute-start.16 = (f32[16,1280]{1,0:T(8,128)S(1)}, f32[16,1280]{1,0:T(8,128)S(1)}, u32[]{:S(2)}, u32[]{:S(2)}) collective-permute-start(f32[16,1280]{1,0:T(8,128)S(1)} %fusion.24), channel_id=1, source_target_pairs={{0,128},{32,160},{64,192},{96,224},{128,256},{160,288},{192,320},{... | collective-permute-start | bytes 245768 | tf_op jit(solution)/shard_map/ppermute | solution.py:20
  136.4 10.1 %collective-permute-start.15 = (f32[8,1280]{1,0:T(8,128)S(1)}, f32[8,1280]{1,0:T(8,128)S(1)}, u32[]{:S(2)}, u32[]{:S(2)}) collective-permute-start(f32[8,1280]{1,0:T(8,128)S(1)} %slice.293), channel_id=1, source_target_pairs={{0,384},{32,416},{64,448},{96,480},{128,0},{160,32},{192,64},{224,... | collective-permute-start | bytes 122888 | tf_op jit(solution)/shard_map/ppermute | solution.py:20
  140.9 9.3 %collective-permute-start.17 = (f32[8,1280]{1,0:T(8,128)S(1)}, f32[8,1280]{1,0:T(8,128)S(1)}, u32[]{:S(2)}, u32[]{:S(2)}) collective-permute-start(f32[8,1280]{1,0:T(8,128)S(1)} %slice.294), channel_id=1, source_target_pairs={{0,128},{32,160},{64,192},{96,224},{128,256},{160,288},{192,320},{... | collective-permute-start | bytes 122888 | tf_op jit(solution)/shard_map/ppermute | solution.py:20
  150.2 27.8 %collective-permute-start.19 = (f32[4,16,1280]{2,1,0:T(8,128)S(1)}, f32[4,16,1280]{2,1,0:T(8,128)S(1)}, u32[]{:S(2)}, u32[]{:S(2)}) collective-permute-start(f32[4,16,1280]{2,1,0:T(8,128)S(1)} %pad_maximum_fusion.6), channel_id=1, source_target_pairs={{0,480},{32,0},{64,32},{96,64},{128,96},{160,128},{192,160},{224,1... | collective-permute-start | bytes 983048 | tf_op jit(solution)/shard_map/ppermute | solution.py:20
  152.2 25.9 %collective-permute-start.20 = (f32[4,16,1280]{2,1,0:T(8,128)S(1)}, f32[4,16,1280]{2,1,0:T(8,128)S(1)}, u32[]{:S(2)}, u32[]{:S(2)}) collective-permute-start(f32[4,16,1280]{2,1,0:T(8,128)S(1)} %pad_maximum_fusion.6), channel_id=1, source_target_pairs={{0,32},{32,64},{64,96},{96,128},{128,160},{160,192},{192,224},{224... | collective-permute-start | bytes 983048 | tf_op jit(solution)/shard_map/ppermute | solution.py:20
  156.3 21.7 %collective-permute-start.21 = (f32[4,8,1280]{2,1,0:T(8,128)}, f32[4,8,1280]{2,1,0:T(8,128)S(1)}, u32[]{:S(2)}, u32[]{:S(2)}) collective-permute-start(f32[4,8,1280]{2,1,0:T(8,128)} %get-tuple-element.71), channel_id=1, source_target_pairs={{0,448},{32,480},{64,0},{96,32},{128,64},{160,96},{192,128},{224,1... | collective-permute-start | bytes 491528 | tf_op jit(solution)/shard_map/ppermute | solution.py:20
  158.2 19.8 %collective-permute-start.22 = (f32[4,8,1280]{2,1,0:T(8,128)}, f32[4,8,1280]{2,1,0:T(8,128)S(1)}, u32[]{:S(2)}, u32[]{:S(2)}) collective-permute-start(f32[4,8,1280]{2,1,0:T(8,128)} %get-tuple-element.70), channel_id=1, source_target_pairs={{0,64},{32,96},{64,128},{96,160},{128,192},{160,224},{192,256},{22... | collective-permute-start | bytes 491528 | tf_op jit(solution)/shard_map/ppermute | solution.py:20
  162.5 7.7 %copy-start = (f32[1024,1024]{1,0:T(8,128)S(1)}, f32[1024,1024]{1,0:T(8,128)}, u32[]{:S(2)}) copy-start(f32[1024,1024]{1,0:T(8,128)} %all-gather.2.cloned.1.call-done) | copy-start | bytes 12582916
  178.8 1.1 slice-start
  178.8 1.1 copy-start.8
  185.9 14.5 %collective-permute-start.23 = (f32[16,8,1152]{2,1,0:T(8,128)S(1)}, f32[16,8,1152]{2,1,0:T(8,128)S(1)}, u32[]{:S(2)}, u32[]{:S(2)}) collective-permute-start(f32[16,8,1152]{2,1,0:T(8,128)S(1)} %dynamic-slice_bitcast_fusion), channel_id=1, source_target_pairs={{0,1},{1,0},{2,3},{3,2},{4,5},{5,4},{6,7},{7,6},{8,9},{9,8},{10,11... | collective-permute-start | bytes 1769480 | tf_op jit(solution)/shard_map/ppermute | solution.py:180
  201.3 19.0 %all-to-all-start = ((f32[16,8,1152]{2,1,0:T(8,128)}), f32[16,8,1152]{2,1,0:T(8,128)S(1)}, u32[]{:S(2)}, u32[]{:S(2)}) async-start(f32[16,8,1152]{2,1,0:T(8,128)} %bitcast_add_fusion), calls=%async_computation | async-start | bytes 1179648 | tf_op jit(solution)/shard_map/all_to_all | solution.py:181
  (4 other events, 3.0 us)
Sparse Core Ops, SparseCore 0:
  43.5 93.7 all-gather.1

commit v3 on v2

--- a/solution.py
+++ b/solution.py
@@ -46,20 +46,14 @@
     def of_row(steps):
         return lax.dynamic_index_in_dim(sums, (row + steps) % 4, 0, keepdims=False)
 
-    opposite = of_row(2)
-    passing_right = shift_z(opposite[:8], 4)
-    passing_left = shift_z(opposite[8:], -4)
-    right, left = of_row(1), of_row(3)
-    from_left = shift_z(jnp.concatenate([right[:8] + passing_right, right[8:]]), 4)
-    from_right = shift_z(jnp.concatenate([left[:8], left[8:] + passing_left]), -4)
-    return of_row(0) + from_left + from_right
+    from_left = shift_z(of_row(1), 4)
+    from_right = shift_z(of_row(3), -4)
+    across = shift_z(of_row(2), 8)
+    return of_row(0) + from_left + from_right + across
 
 
 def gather_far(part):
-    plus4 = shift_z(part, -4)
-    minus4 = shift_z(part, 4)
-    plus8 = jnp.concatenate([shift_z(plus4[:8], -4), shift_z(minus4[8:], 4)])
-    return jnp.stack([part, plus4, plus8, minus4])
+    return jnp.stack([part, shift_z(part, -4), shift_z(part, 8), shift_z(part, 4)])
 
 
 def gather_near(parts):
@@ -67,13 +61,11 @@
         parts,
         shift_z(parts, -1),
         shift_z(parts, 1),
-        shift_z(parts[:, :8], -2),
-        shift_z(parts[:, 8:], 2),
+        shift_z(parts, -2),
     )
 
 
-def joined(parts, plus1, minus1, plus2, minus2):
-    two = jnp.concatenate([plus2, jnp.roll(minus2, -1, axis=0)], axis=1)
+def joined(parts, plus1, minus1, two):
     three = jnp.roll(minus1, -1, axis=0)
     return jnp.stack([parts, plus1, two, three], axis=1)
 
@@ -115,20 +107,20 @@
     other_queries1 = swap_y(own_queries1)
     near_sums, plus1, minus1 = lax.optimization_barrier((reduce_near(blocks, place), plus1, minus1))
     plus2, minus2 = shift_z(plus1, -1), shift_z(minus1, 1)
-    part, plus2, minus2, other_queries1 = lax.optimization_barrier(
-        (reduce_far(near_sums, place), plus2, minus2, other_queries1)
-    )
+    part, other_queries1 = lax.optimization_barrier((reduce_far(near_sums, place), other_queries1))
+    parts, plus2, minus2 = lax.optimization_barrier((gather_far(part), plus2, minus2))
     own_queries2 = jnp.concatenate([minus2, plus2])
     other_queries2 = swap_y(own_queries2)
-    parts, other_queries2 = lax.optimization_barrier((gather_far(part), other_queries2))
-    own_queries = jnp.concatenate([own_queries1, own_queries2])
-    other_queries = jnp.concatenate([other_queries1, other_queries2])
-    own_first = dot(own_queries, inverse, ((1,), (1,)))
-    other_first = dot(other_queries, inverse, ((1,), (1,)))
+
+    def first(queries):
+        return dot(queries, inverse, ((1,), (1,)))
 
     side = dot(pair_train, inverse, ((1,), (0,)))
-    pieces, side, own_first, other_first = lax.optimization_barrier(
-        (gather_near(parts), side, own_first, other_first)
+    near_first = first(own_queries1), first(own_queries2), first(other_queries1)
+    side, near_first, other_queries2 = lax.optimization_barrier((side, near_first, other_queries2))
+    own_first, other_first = near_first[:2], (near_first[2], first(other_queries2))
+    pieces, own_first, other_first = lax.optimization_barrier(
+        (gather_near(parts), own_first, other_first)
     )
     gathered = joined(*pieces).reshape(quarter, 5 * quarter)
     strips = jnp.roll(gathered, place * (quarter // 16), axis=0)
@@ -151,15 +143,15 @@
     product = jnp.where(first_half, product, jnp.roll(product, quarter, axis=1))
     left = pair_train - (0.5 * DAMPING) * side - product * (1.0 / total_rows)
 
-    own_scores = dot(left, own_first, ((1,), (1,)))
-    other_scores = dot(left, other_first, ((1,), (1,)))
-    even = jnp.where(first_half, own_scores, other_scores)
-    odd = jnp.where(first_half, other_scores, own_scores)
+    own_scores = [dot(left, piece, ((1,), (1,))) for piece in own_first]
+    other_scores = [dot(left, piece, ((1,), (1,))) for piece in other_first]
+    even = [jnp.where(first_half, own, other) for own, other in zip(own_scores, other_scores)]
+    odd = [jnp.where(first_half, other, own) for own, other in zip(own_scores, other_scores)]
 
     def tiles(scores, half_rows, offsets):
-        at = (3, 0, 1, 2, 4)
-        piece = scores[half_rows * rows : (half_rows + 1) * rows]
-        return [piece[:, at[i] * rows : (at[i] + 1) * rows] for i in offsets]
+        at = ((1, 0), (0, 0), (0, 1), (0, 2), (1, 1))
+        piece = [part[half_rows * rows : (half_rows + 1) * rows] for part in scores]
+        return [piece[at[i][0]][:, at[i][1] * rows : (at[i][1] + 1) * rows] for i in offsets]
 
     def mixed(first_tiles, second_tiles):
         out = []

time: 229 us -> 230 us (level)
  starting transfers between devices: 110 us -> 114 us
  waiting for transfers between devices: 58 us -> 55.3 us
  local copies, waits for them, and re-layouts: 10.7 us -> 8.26 us
    ppermute x20 -> x17, waiting for transfers between devices: 45 us -> 39.6 us  [shift_z(): lax.ppermute(value, 'z', [(i, (i + steps) % count) for i in range(count)])]
    ppermute x1, starting transfers between devices: 12.9 us -> 9.3 us  [on_device(): halves = kept + lax.ppermute(sent, 'c', [(0, 1), (1, 0)])]
    ppermute x3, starting transfers between devices: 9.51 us -> 13.1 us  [swap_y(): return lax.ppermute(value, 'yh', [(0, 1), (1, 0)])]
    unnamed x31 -> x33, local copies, waits for them, and re-layouts: 6.04 us -> 2.68 us
    ppermute x20 -> x17, starting transfers between devices: 80.5 us -> 83.7 us  [shift_z(): lax.ppermute(value, 'z', [(i, (i + steps) % count) for i in range(count)])]
    ppermute x3, waiting for transfers between devices: 0.01 us -> 2.76 us  [swap_y(): return lax.ppermute(value, 'yh', [(0, 1), (1, 0)])]
    dot_general x11 -> x15, matrix products: 21.1 us -> 22.9 us  [dot(): lax.dot_general(left, right, (dims, ((), ())), precision=FAST, preferred_...]
  transfers between devices with their start and end apart: 26 -> 23, of which waited for: 10 -> 11; matrix products, arithmetic and copies ran while one was open for 13% -> 12% of each run, Pallas kernels for 0% -> 0%
where the time goes in v3:
time: 230 us; the launch traced here: 228 us
  starting transfers between devices  114 us (50%)
  waiting for transfers between devices  55.3 us (24%)
  matrix products  22.9 us (10%)
  between operations  14.3 us (6%)
  other arithmetic  13.3 us (6%)
  local copies, waits for them, and re-layouts  8.26 us (4%)
    ppermute x17, starting transfers between devices, shift_z(): lax.ppermute(value, 'z', [(i, (i + steps) % count) for i in range(count)])  83.7 us
    ppermute x17, waiting for transfers between devices, shift_z(): lax.ppermute(value, 'z', [(i, (i + steps) % count) for i in range(count)])  39.6 us
    dot_general x15, matrix products, dot(): lax.dot_general(left, right, (dims, ((), ())), precision=FAST, preferred_...  22.9 us
    ppermute x3, starting transfers between devices, swap_y(): return lax.ppermute(value, 'yh', [(0, 1), (1, 0)])  13.1 us
    all_to_all x1, waiting for transfers between devices, on_device(): lax.all_to_all(halves.reshape(shares * own, window), ('yh', 'yl', 'x'), 0...  11.3 us
    ppermute x1, starting transfers between devices, on_device(): halves = kept + lax.ppermute(sent, 'c', [(0, 1), (1, 0)])  9.3 us
    all_to_all x1, starting transfers between devices, on_device(): lax.all_to_all(halves.reshape(shares * own, window), ('yh', 'yl', 'x'), 0...  8.18 us
  transfers between devices with their start and end apart: 23, of which 11 were waited for; matrix products, arithmetic and copies ran while one was open for 12% of the time, Pallas kernels for 0%

profile of v3, /device:TPU:1, one launch (start us, length us, event | category | flops | bytes accessed | tf_op | source)
XLA Modules:
  0.0 228.4 jit_solution(14649640077337044342)
XLA Ops:
  10.3 5.6 %collective-permute-start = (f32[160,1024]{1,0:T(8,128)}, f32[160,1024]{1,0:T(8,128)S(1)}, u32[]{:S(2)}, u32[]{:S(2)}) collective-permute-start(f32[160,1024]{1,0:T(8,128)} %pad_maximum_fusion.4), channel_id=1, source_target_pairs={{0,16},{16,0},{1,17},{17,1},{2,18},{18,2},{3,19},{19,3},{4,20},{20... | collective-permute-start | bytes 1966088 | tf_op jit(solution)/shard_map/ppermute | solution.py:24
  16.1 3.5 %collective-permute-start.2 = (f32[128,1024]{1,0:T(8,128)S(1)}, f32[128,1024]{1,0:T(8,128)S(1)}, u32[]{:S(2)}, u32[]{:S(2)}) collective-permute-start(f32[128,1024]{1,0:T(8,128)S(1)} %bitcast.74), channel_id=1, source_target_pairs={{0,32},{32,64},{64,96},{96,128},{128,160},{160,192},{192,224},{224... | collective-permute-start | bytes 1572872 | tf_op jit(solution)/shard_map/ppermute | solution.py:20
  19.7 9.5 %collective-permute-start.1 = (f32[128,1024]{1,0:T(8,128)S(1)}, f32[128,1024]{1,0:T(8,128)S(1)}, u32[]{:S(2)}, u32[]{:S(2)}) collective-permute-start(f32[128,1024]{1,0:T(8,128)S(1)} %bitcast.75), channel_id=1, source_target_pairs={{0,480},{32,0},{64,32},{96,64},{128,96},{160,128},{192,160},{224,1... | collective-permute-start | bytes 1572872 | tf_op jit(solution)/shard_map/ppermute | solution.py:20
  29.2 9.4 %collective-permute-done.2 = f32[128,1024]{1,0:T(8,128)S(1)} collective-permute-done((f32[128,1024]{1,0:T(8,128)S(1)}, f32[128,1024]{1,0:T(8,128)S(1)}, u32[]{:S(2)}, u32[]{:S(2)}) %collective-permute-start.2) | collective-permute-done | bytes 524320 | tf_op jit(solution)/shard_map/ppermute | solution.py:20
  44.8 5.3 %collective-permute-start.4 = (f32[4,16,1280]{2,1,0:T(8,128)}, f32[4,16,1280]{2,1,0:T(8,128)}, u32[]{:S(2)}, u32[]{:S(2)}) collective-permute-start(f32[4,16,1280]{2,1,0:T(8,128)} %get-tuple-element.59), channel_id=1, source_target_pairs={{0,480},{32,0},{64,32},{96,64},{128,96},{160,128},{192,160},{224,1... | collective-permute-start | bytes 983048 | tf_op jit(solution)/shard_map/ppermute | solution.py:20
  51.4 2.0 collective-permute-start.10
  56.0 5.5 %collective-permute-start.6 = (f32[4,8,1280]{2,1,0:T(8,128)}, f32[4,8,1280]{2,1,0:T(8,128)}, u32[]{:S(2)}, u32[]{:S(2)}) collective-permute-start(f32[4,8,1280]{2,1,0:T(8,128)} %get-tuple-element.80), channel_id=1, source_target_pairs={{0,448},{32,480},{64,0},{96,32},{128,64},{160,96},{192,128},{224,1... | collective-permute-start | bytes 491528 | tf_op jit(solution)/shard_map/ppermute | solution.py:20
  61.6 7.7 %collective-permute-done.5 = f32[4,8,1280]{2,1,0:T(8,128)} collective-permute-done((f32[4,8,1280]{2,1,0:T(8,128)}, f32[4,8,1280]{2,1,0:T(8,128)}, u32[]{:S(2)}, u32[]{:S(2)}) %collective-permute-start.5) | collective-permute-done | bytes 163872 | tf_op jit(solution)/shard_map/ppermute | solution.py:20
  72.4 5.7 %collective-permute-start.7 = (f32[16,1280]{1,0:T(8,128)S(1)}, f32[16,1280]{1,0:T(8,128)S(1)}, u32[]{:S(2)}, u32[]{:S(2)}) collective-permute-start(f32[16,1280]{1,0:T(8,128)S(1)} %get-tuple-element.76), channel_id=1, source_target_pairs={{0,128},{32,160},{64,192},{96,224},{128,256},{160,288},{192,320},{... | collective-permute-start | bytes 245768 | tf_op jit(solution)/shard_map/ppermute | solution.py:20
  78.1 6.5 %collective-permute-start.9 = (f32[16,1280]{1,0:T(8,128)S(1)}, f32[16,1280]{1,0:T(8,128)S(1)}, u32[]{:S(2)}, u32[]{:S(2)}) collective-permute-start(f32[16,1280]{1,0:T(8,128)S(1)} %get-tuple-element.77), channel_id=1, source_target_pairs={{0,256},{32,288},{64,320},{96,352},{128,384},{160,416},{192,448},{... | collective-permute-start | bytes 245768 | tf_op jit(solution)/shard_map/ppermute | solution.py:20
  84.6 6.9 %collective-permute-start.8 = (f32[16,1280]{1,0:T(8,128)S(1)}, f32[16,1280]{1,0:T(8,128)}, u32[]{:S(2)}, u32[]{:S(2)}) collective-permute-start(f32[16,1280]{1,0:T(8,128)S(1)} %get-tuple-element.78), channel_id=1, source_target_pairs={{0,384},{32,416},{64,448},{96,480},{128,0},{160,32},{192,64},{224,... | collective-permute-start | bytes 245768 | tf_op jit(solution)/shard_map/ppermute | solution.py:20
  91.5 1.9 collective-permute-start.14
  93.4 3.4 %collective-permute-start.15 = (f32[128,1024]{1,0:T(8,128)S(1)}, f32[128,1024]{1,0:T(8,128)S(1)}, u32[]{:S(2)}, u32[]{:S(2)}) collective-permute-start(f32[128,1024]{1,0:T(8,128)S(1)} %collective-permute-done.2), channel_id=1, source_target_pairs={{0,32},{32,64},{64,96},{96,128},{128,160},{160,192},{192,224},{224... | collective-permute-start | bytes 1572872 | tf_op jit(solution)/shard_map/ppermute | solution.py:20
  97.8 2.1 collective-permute-done.8
  100.8 3.6 %collective-permute-start.13 = (f32[16,1280]{1,0:T(8,128)S(1)}, f32[16,1280]{1,0:T(8,128)S(1)}, u32[]{:S(2)}, u32[]{:S(2)}) collective-permute-start(f32[16,1280]{1,0:T(8,128)S(1)} %fusion.21), channel_id=1, source_target_pairs={{0,128},{32,160},{64,192},{96,224},{128,256},{160,288},{192,320},{... | collective-permute-start | bytes 245768 | tf_op jit(solution)/shard_map/ppermute | solution.py:20
  104.5 11.0 %collective-permute-start.12 = (f32[16,1280]{1,0:T(8,128)S(1)}, f32[16,1280]{1,0:T(8,128)S(1)}, u32[]{:S(2)}, u32[]{:S(2)}) collective-permute-start(f32[16,1280]{1,0:T(8,128)S(1)} %fusion.21), channel_id=1, source_target_pairs={{0,256},{32,288},{64,320},{96,352},{128,384},{160,416},{192,448},{... | collective-permute-start | bytes 245768 | tf_op jit(solution)/shard_map/ppermute | solution.py:20
  115.5 3.4 %collective-permute-start.11 = (f32[16,1280]{1,0:T(8,128)S(1)}, f32[16,1280]{1,0:T(8,128)S(1)}, u32[]{:S(2)}, u32[]{:S(2)}) collective-permute-start(f32[16,1280]{1,0:T(8,128)S(1)} %fusion.21), channel_id=1, source_target_pairs={{0,384},{32,416},{64,448},{96,480},{128,0},{160,32},{192,64},{224,... | collective-permute-start | bytes 245768 | tf_op jit(solution)/shard_map/ppermute | solution.py:20
  118.9 8.0 %collective-permute-done.13 = f32[16,1280]{1,0:T(8,128)S(1)} collective-permute-done((f32[16,1280]{1,0:T(8,128)S(1)}, f32[16,1280]{1,0:T(8,128)S(1)}, u32[]{:S(2)}, u32[]{:S(2)}) %collective-permute-start.13) | collective-permute-done | bytes 81952 | tf_op jit(solution)/shard_map/ppermute | solution.py:20
  126.9 9.5 %collective-permute-done.12 = f32[16,1280]{1,0:T(8,128)S(1)} collective-permute-done((f32[16,1280]{1,0:T(8,128)S(1)}, f32[16,1280]{1,0:T(8,128)S(1)}, u32[]{:S(2)}, u32[]{:S(2)}) %collective-permute-start.12) | collective-permute-done | bytes 81952 | tf_op jit(solution)/shard_map/ppermute | solution.py:20
  137.2 7.2 %collective-permute-start.19 = (f32[4,16,1280]{2,1,0:T(8,128)}, f32[4,16,1280]{2,1,0:T(8,128)}, u32[]{:S(2)}, u32[]{:S(2)}) collective-permute-start(f32[4,16,1280]{2,1,0:T(8,128)} %pad_maximum_fusion.5), channel_id=1, source_target_pairs={{0,448},{32,480},{64,0},{96,32},{128,64},{160,96},{192,128},{224,1... | collective-permute-start | bytes 983048 | tf_op jit(solution)/shard_map/ppermute | solution.py:20
  144.4 4.6 %collective-permute-start.18 = (f32[4,16,1280]{2,1,0:T(8,128)}, f32[4,16,1280]{2,1,0:T(8,128)}, u32[]{:S(2)}, u32[]{:S(2)}) collective-permute-start(f32[4,16,1280]{2,1,0:T(8,128)} %pad_maximum_fusion.5), channel_id=1, source_target_pairs={{0,32},{32,64},{64,96},{96,128},{128,160},{160,192},{192,224},{224... | collective-permute-start | bytes 983048 | tf_op jit(solution)/shard_map/ppermute | solution.py:20
  149.0 1.9 collective-permute-start.17
  153.1 5.5 %collective-permute-start.16 = (f32[256,1024]{1,0:T(8,128)S(1)}, f32[256,1024]{1,0:T(8,128)}, u32[]{:S(2)}, u32[]{:S(2)}) collective-permute-start(f32[256,1024]{1,0:T(8,128)S(1)} %constant_dynamic-update-slice_fusion), channel_id=1, source_target_pairs={{0,16},{16,0},{1,17},{17,1},{2,18},{18,2},{3,19},{19,3},{4,20},{20... | collective-permute-start | bytes 3145736 | tf_op jit(solution)/shard_map/ppermute | solution.py:24
  158.7 4.4 %fusion.24 = f32[256,1024]{1,0:T(8,128)S(1)} fusion(f32[256,1024]{1,0:T(8,128)S(1)} %maximum_select_fusion, f32[1024,1024]{1,0:T(8,128)} %all-gather.2.cloned.1.call-done), kind=kOutput, calls=%fused_computation.81 | convolution fusion | flops 1610612736 | bytes 6291456 | tf_op jit(solution)/shard_map/dot_general | solution.py:13
  163.1 2.9 %fusion.22 = f32[384,1024]{1,0:T(8,128)S(1)} fusion(f32[1024,1024]{1,0:T(8,128)S(1)} %copy-done, f32[128,1024]{1,0:T(8,128)S(1)} %copy-done.5, f32[128,1024]{1,0:T(8,128)S(1)} %bitcast.77, f32[128,1024]{1,0:T(8,128)S(1)} %collective-permute-done.2), kind=kOutput, calls=%fused_computation.79 | convolution fusion | flops 2416705536 | bytes 7340032 | tf_op jit(solution)/shard_map/dot_general | solution.py:13
  166.0 2.2 fusion.25
  168.2 4.3 %fusion.26 = f32[384,1024]{1,0:T(8,128)S(1)} fusion(f32[384,1024]{1,0:T(8,128)} %collective-permute-done.10, f32[1024,1024]{1,0:T(8,128)S(1)} %copy-done), kind=kOutput, calls=%fused_computation.83 | convolution fusion | flops 2415919104 | bytes 7340032 | tf_op jit(solution)/shard_map/dot_general | solution.py:13
  172.5 2.8 %collective-permute-done.16 = f32[256,1024]{1,0:T(8,128)} collective-permute-done((f32[256,1024]{1,0:T(8,128)S(1)}, f32[256,1024]{1,0:T(8,128)}, u32[]{:S(2)}, u32[]{:S(2)}) %collective-permute-start.16) | collective-permute-done | bytes 1048608 | tf_op jit(solution)/shard_map/ppermute | solution.py:24
  175.2 3.4 %fusion.27 = f32[256,1024]{1,0:T(8,128)S(1)} fusion(f32[256,1024]{1,0:T(8,128)} %collective-permute-done.16, f32[1024,1024]{1,0:T(8,128)S(1)} %copy-done), kind=kOutput, calls=%fused_computation.84 | convolution fusion | flops 1610612736 | bytes 6291456 | tf_op jit(solution)/shard_map/dot_general | solution.py:13
  189.4 9.3 %collective-permute-start.20 = (f32[16,8,1152]{2,1,0:T(8,128)S(1)}, f32[16,8,1152]{2,1,0:T(8,128)S(1)}, u32[]{:S(2)}, u32[]{:S(2)}) collective-permute-start(f32[16,8,1152]{2,1,0:T(8,128)S(1)} %dynamic-slice_bitcast_fusion), channel_id=1, source_target_pairs={{0,1},{1,0},{2,3},{3,2},{4,5},{5,4},{6,7},{7,6},{8,9},{9,8},{10,11... | collective-permute-start | bytes 1769480 | tf_op jit(solution)/shard_map/ppermute | solution.py:172
  201.2 8.2 %all-to-all-start = ((f32[16,8,1152]{2,1,0:T(8,128)}), f32[16,8,1152]{2,1,0:T(8,128)S(1)}, u32[]{:S(2)}, u32[]{:S(2)}) async-start(f32[16,8,1152]{2,1,0:T(8,128)} %bitcast_add_fusion), calls=%async_computation | async-start | bytes 1179648 | tf_op jit(solution)/shard_map/all_to_all | solution.py:173
  209.5 11.3 %all-to-all-done = f32[16,8,1152]{2,1,0:T(8,128)S(1)} async-done(((f32[16,8,1152]{2,1,0:T(8,128)}), f32[16,8,1152]{2,1,0:T(8,128)S(1)}, u32[]{:S(2)}, u32[]{:S(2)}) %all-to-all-start) | async-done | bytes 589856 | tf_op jit(solution)/shard_map/all_to_all | solution.py:173
  (103 shorter events, 35.6 us)
Async XLA Ops:
  6.5 9.5 %copy-start.8 = (f32[128,1,1024]{2,1,0:T(1,128)S(1)}, f32[128,1,1024]{2,1,0:T(1,128)}, u32[]{:S(2)}) copy-start(f32[128,1,1024]{2,1,0:T(1,128)} %param.5) | copy-start | bytes 1572868
  6.5 152.1 %all-gather.2.cloned.1.call-start = ((), (), s32[]{:S(2)}) async-start(), calls=%async_computation.1 | async-start | bytes 4456448 | tf_op jit(solution)/shard_map/all_gather | solution.py:94
  8.5 31.0 %copy-start.7 = (f32[1,32,1024]{2,1,0:T(8,128)S(1)}, f32[1,32,1024]{2,1,0:T(8,128)}, u32[]{:S(2)}) copy-start(f32[1,32,1024]{2,1,0:T(8,128)} %param.6) | copy-start | bytes 393220
  10.3 29.1 %collective-permute-start = (f32[160,1024]{1,0:T(8,128)}, f32[160,1024]{1,0:T(8,128)S(1)}, u32[]{:S(2)}, u32[]{:S(2)}) collective-permute-start(f32[160,1024]{1,0:T(8,128)} %pad_maximum_fusion.4), channel_id=1, source_target_pairs={{0,16},{16,0},{1,17},{17,1},{2,18},{18,2},{3,19},{19,3},{4,20},{20... | collective-permute-start | bytes 1966088 | tf_op jit(solution)/shard_map/ppermute | solution.py:24
  16.1 22.4 %collective-permute-start.2 = (f32[128,1024]{1,0:T(8,128)S(1)}, f32[128,1024]{1,0:T(8,128)S(1)}, u32[]{:S(2)}, u32[]{:S(2)}) collective-permute-start(f32[128,1024]{1,0:T(8,128)S(1)} %bitcast.74), channel_id=1, source_target_pairs={{0,32},{32,64},{64,96},{96,128},{128,160},{160,192},{192,224},{224... | collective-permute-start | bytes 1572872 | tf_op jit(solution)/shard_map/ppermute | solution.py:20
  19.7 19.8 %collective-permute-start.1 = (f32[128,1024]{1,0:T(8,128)S(1)}, f32[128,1024]{1,0:T(8,128)S(1)}, u32[]{:S(2)}, u32[]{:S(2)}) collective-permute-start(f32[128,1024]{1,0:T(8,128)S(1)} %bitcast.75), channel_id=1, source_target_pairs={{0,480},{32,0},{64,32},{96,64},{128,96},{160,128},{192,160},{224,1... | collective-permute-start | bytes 1572872 | tf_op jit(solution)/shard_map/ppermute | solution.py:20
  41.8 8.2 %copy-start.4 = (f32[128,1024]{1,0:T(8,128)S(1)}, f32[128,1024]{1,0:T(8,128)}, u32[]{:S(2)}) copy-start(f32[128,1024]{1,0:T(8,128)} %copy-done.3) | copy-start | bytes 1572868
  42.8 27.4 %collective-permute-start.3 = (f32[4,16,1280]{2,1,0:T(8,128)}, f32[4,16,1280]{2,1,0:T(8,128)}, u32[]{:S(2)}, u32[]{:S(2)}) collective-permute-start(f32[4,16,1280]{2,1,0:T(8,128)} %get-tuple-element.57), channel_id=1, source_target_pairs={{0,32},{32,64},{64,96},{96,128},{128,160},{160,192},{192,224},{224... | collective-permute-start | bytes 983048 | tf_op jit(solution)/shard_map/ppermute | solution.py:20
  44.8 25.5 %collective-permute-start.4 = (f32[4,16,1280]{2,1,0:T(8,128)}, f32[4,16,1280]{2,1,0:T(8,128)}, u32[]{:S(2)}, u32[]{:S(2)}) collective-permute-start(f32[4,16,1280]{2,1,0:T(8,128)} %get-tuple-element.59), channel_id=1, source_target_pairs={{0,480},{32,0},{64,32},{96,64},{128,96},{160,128},{192,160},{224,1... | collective-permute-start | bytes 983048 | tf_op jit(solution)/shard_map/ppermute | solution.py:20
  51.4 49.5 %collective-permute-start.10 = (f32[384,1024]{1,0:T(8,128)}, f32[384,1024]{1,0:T(8,128)}, u32[]{:S(2)}, u32[]{:S(2)}) collective-permute-start(f32[384,1024]{1,0:T(8,128)} %pad_maximum_fusion), channel_id=1, source_target_pairs={{0,16},{16,0},{1,17},{17,1},{2,18},{18,2},{3,19},{19,3},{4,20},{20... | collective-permute-start | bytes 4718600 | tf_op jit(solution)/shard_map/ppermute | solution.py:24
  54.1 15.2 %collective-permute-start.5 = (f32[4,8,1280]{2,1,0:T(8,128)}, f32[4,8,1280]{2,1,0:T(8,128)}, u32[]{:S(2)}, u32[]{:S(2)}) collective-permute-start(f32[4,8,1280]{2,1,0:T(8,128)} %get-tuple-element.79), channel_id=1, source_target_pairs={{0,64},{32,96},{64,128},{96,160},{128,192},{160,224},{192,256},{22... | collective-permute-start | bytes 491528 | tf_op jit(solution)/shard_map/ppermute | solution.py:20
  56.0 14.3 %collective-permute-start.6 = (f32[4,8,1280]{2,1,0:T(8,128)}, f32[4,8,1280]{2,1,0:T(8,128)}, u32[]{:S(2)}, u32[]{:S(2)}) collective-permute-start(f32[4,8,1280]{2,1,0:T(8,128)} %get-tuple-element.80), channel_id=1, source_target_pairs={{0,448},{32,480},{64,0},{96,32},{128,64},{160,96},{192,128},{224,1... | collective-permute-start | bytes 491528 | tf_op jit(solution)/shard_map/ppermute | solution.py:20
  72.4 21.0 %collective-permute-start.7 = (f32[16,1280]{1,0:T(8,128)S(1)}, f32[16,1280]{1,0:T(8,128)S(1)}, u32[]{:S(2)}, u32[]{:S(2)}) collective-permute-start(f32[16,1280]{1,0:T(8,128)S(1)} %get-tuple-element.76), channel_id=1, source_target_pairs={{0,128},{32,160},{64,192},{96,224},{128,256},{160,288},{192,320},{... | collective-permute-start | bytes 245768 | tf_op jit(solution)/shard_map/ppermute | solution.py:20
  78.1 19.7 %collective-permute-start.9 = (f32[16,1280]{1,0:T(8,128)S(1)}, f32[16,1280]{1,0:T(8,128)S(1)}, u32[]{:S(2)}, u32[]{:S(2)}) collective-permute-start(f32[16,1280]{1,0:T(8,128)S(1)} %get-tuple-element.77), channel_id=1, source_target_pairs={{0,256},{32,288},{64,320},{96,352},{128,384},{160,416},{192,448},{... | collective-permute-start | bytes 245768 | tf_op jit(solution)/shard_map/ppermute | solution.py:20
  84.6 15.3 %collective-permute-start.8 = (f32[16,1280]{1,0:T(8,128)S(1)}, f32[16,1280]{1,0:T(8,128)}, u32[]{:S(2)}, u32[]{:S(2)}) collective-permute-start(f32[16,1280]{1,0:T(8,128)S(1)} %get-tuple-element.78), channel_id=1, source_target_pairs={{0,384},{32,416},{64,448},{96,480},{128,0},{160,32},{192,64},{224,... | collective-permute-start | bytes 245768 | tf_op jit(solution)/shard_map/ppermute | solution.py:20
  91.5 45.7 %collective-permute-start.14 = (f32[128,1024]{1,0:T(8,128)}, f32[128,1024]{1,0:T(8,128)S(1)}, u32[]{:S(2)}, u32[]{:S(2)}) collective-permute-start(f32[128,1024]{1,0:T(8,128)} %copy-done.3), channel_id=1, source_target_pairs={{0,480},{32,0},{64,32},{96,64},{128,96},{160,128},{192,160},{224,1... | collective-permute-start | bytes 1572872 | tf_op jit(solution)/shard_map/ppermute | solution.py:20
  93.4 43.8 %collective-permute-start.15 = (f32[128,1024]{1,0:T(8,128)S(1)}, f32[128,1024]{1,0:T(8,128)S(1)}, u32[]{:S(2)}, u32[]{:S(2)}) collective-permute-start(f32[128,1024]{1,0:T(8,128)S(1)} %collective-permute-done.2), channel_id=1, source_target_pairs={{0,32},{32,64},{64,96},{96,128},{128,160},{160,192},{192,224},{224... | collective-permute-start | bytes 1572872 | tf_op jit(solution)/shard_map/ppermute | solution.py:20
  100.8 26.1 %collective-permute-start.13 = (f32[16,1280]{1,0:T(8,128)S(1)}, f32[16,1280]{1,0:T(8,128)S(1)}, u32[]{:S(2)}, u32[]{:S(2)}) collective-permute-start(f32[16,1280]{1,0:T(8,128)S(1)} %fusion.21), channel_id=1, source_target_pairs={{0,128},{32,160},{64,192},{96,224},{128,256},{160,288},{192,320},{... | collective-permute-start | bytes 245768 | tf_op jit(solution)/shard_map/ppermute | solution.py:20
  104.5 32.0 %collective-permute-start.12 = (f32[16,1280]{1,0:T(8,128)S(1)}, f32[16,1280]{1,0:T(8,128)S(1)}, u32[]{:S(2)}, u32[]{:S(2)}) collective-permute-start(f32[16,1280]{1,0:T(8,128)S(1)} %fusion.21), channel_id=1, source_target_pairs={{0,256},{32,288},{64,320},{96,352},{128,384},{160,416},{192,448},{... | collective-permute-start | bytes 245768 | tf_op jit(solution)/shard_map/ppermute | solution.py:20
  115.5 20.9 %collective-permute-start.11 = (f32[16,1280]{1,0:T(8,128)S(1)}, f32[16,1280]{1,0:T(8,128)S(1)}, u32[]{:S(2)}, u32[]{:S(2)}) collective-permute-start(f32[16,1280]{1,0:T(8,128)S(1)} %fusion.21), channel_id=1, source_target_pairs={{0,384},{32,416},{64,448},{96,480},{128,0},{160,32},{192,64},{224,... | collective-permute-start | bytes 245768 | tf_op jit(solution)/shard_map/ppermute | solution.py:20
  137.2 11.8 %copy-start.9 = (f32[128,1024]{1,0:T(8,128)}, f32[128,1024]{1,0:T(8,128)S(1)}, u32[]{:S(2)}) copy-start(f32[128,1024]{1,0:T(8,128)S(1)} %collective-permute-done.14) | copy-start | bytes 1572868
  137.2 11.8 %copy-start.10 = (f32[128,1024]{1,0:T(8,128)}, f32[128,1024]{1,0:T(8,128)S(1)}, u32[]{:S(2)}) copy-start(f32[128,1024]{1,0:T(8,128)S(1)} %collective-permute-done.15) | copy-start | bytes 1572868
  137.2 41.5 %collective-permute-start.19 = (f32[4,16,1280]{2,1,0:T(8,128)}, f32[4,16,1280]{2,1,0:T(8,128)}, u32[]{:S(2)}, u32[]{:S(2)}) collective-permute-start(f32[4,16,1280]{2,1,0:T(8,128)} %pad_maximum_fusion.5), channel_id=1, source_target_pairs={{0,448},{32,480},{64,0},{96,32},{128,64},{160,96},{192,128},{224,1... | collective-permute-start | bytes 983048 | tf_op jit(solution)/shard_map/ppermute | solution.py:20
  144.4 34.3 %collective-permute-start.18 = (f32[4,16,1280]{2,1,0:T(8,128)}, f32[4,16,1280]{2,1,0:T(8,128)}, u32[]{:S(2)}, u32[]{:S(2)}) collective-permute-start(f32[4,16,1280]{2,1,0:T(8,128)} %pad_maximum_fusion.5), channel_id=1, source_target_pairs={{0,32},{32,64},{64,96},{96,128},{128,160},{160,192},{192,224},{224... | collective-permute-start | bytes 983048 | tf_op jit(solution)/shard_map/ppermute | solution.py:20
  149.0 29.7 %collective-permute-start.17 = (f32[4,16,1280]{2,1,0:T(8,128)}, f32[4,16,1280]{2,1,0:T(8,128)}, u32[]{:S(2)}, u32[]{:S(2)}) collective-permute-start(f32[4,16,1280]{2,1,0:T(8,128)} %pad_maximum_fusion.5), channel_id=1, source_target_pairs={{0,480},{32,0},{64,32},{96,64},{128,96},{160,128},{192,160},{224,1... | collective-permute-start | bytes 983048 | tf_op jit(solution)/shard_map/ppermute | solution.py:20
  153.1 22.2 %collective-permute-start.16 = (f32[256,1024]{1,0:T(8,128)S(1)}, f32[256,1024]{1,0:T(8,128)}, u32[]{:S(2)}, u32[]{:S(2)}) collective-permute-start(f32[256,1024]{1,0:T(8,128)S(1)} %constant_dynamic-update-slice_fusion), channel_id=1, source_target_pairs={{0,16},{16,0},{1,17},{17,1},{2,18},{18,2},{3,19},{19,3},{4,20},{20... | collective-permute-start | bytes 3145736 | tf_op jit(solution)/shard_map/ppermute | solution.py:24
  158.7 4.4 %copy-start = (f32[1024,1024]{1,0:T(8,128)S(1)}, f32[1024,1024]{1,0:T(8,128)}, u32[]{:S(2)}) copy-start(f32[1024,1024]{1,0:T(8,128)} %all-gather.2.cloned.1.call-done) | copy-start | bytes 12582916
  158.7 4.4 %copy-start.5 = (f32[128,1024]{1,0:T(8,128)S(1)}, f32[128,1024]{1,0:T(8,128)}, u32[]{:S(2)}) copy-start(f32[128,1024]{1,0:T(8,128)} %copy-done.3) | copy-start | bytes 1572868
  163.1 17.5 %copy-start.1 = (f32[256,1024]{1,0:T(8,128)}, f32[256,1024]{1,0:T(8,128)S(1)}, u32[]{:S(2)}) copy-start(f32[256,1024]{1,0:T(8,128)S(1)} %fusion.24) | copy-start | bytes 3145732
  181.9 1.5 slice-start.1
  189.4 10.9 %collective-permute-start.20 = (f32[16,8,1152]{2,1,0:T(8,128)S(1)}, f32[16,8,1152]{2,1,0:T(8,128)S(1)}, u32[]{:S(2)}, u32[]{:S(2)}) collective-permute-start(f32[16,8,1152]{2,1,0:T(8,128)S(1)} %dynamic-slice_bitcast_fusion), channel_id=1, source_target_pairs={{0,1},{1,0},{2,3},{3,2},{4,5},{5,4},{6,7},{7,6},{8,9},{9,8},{10,11... | collective-permute-start | bytes 1769480 | tf_op jit(solution)/shard_map/ppermute | solution.py:172
  201.2 19.6 %all-to-all-start = ((f32[16,8,1152]{2,1,0:T(8,128)}), f32[16,8,1152]{2,1,0:T(8,128)S(1)}, u32[]{:S(2)}, u32[]{:S(2)}) async-start(f32[16,8,1152]{2,1,0:T(8,128)} %bitcast_add_fusion), calls=%async_computation | async-start | bytes 1179648 | tf_op jit(solution)/shard_map/all_to_all | solution.py:173
  (4 other events, 4.3 us)
Sparse Core Ops, SparseCore 0:
  40.4 116.4 all-gather.1

commit v4 on v3

--- a/solution.py
+++ b/solution.py
@@ -81,18 +81,10 @@
     quarter = width // 4
     total_rows = rows * lax.axis_size("z") * lax.axis_size("yh")
 
-    own_rows = inverse_factors[0]
-    swapped, plus1, minus1 = lax.optimization_barrier(
-        (swap_y(jnp.concatenate([train, own_rows])), shift_z(query, -1), shift_z(query, 1))
+    own_inverse = lax.all_gather(inverse_factors[0], "z", axis=0)
+    other_train, plus1, minus1 = lax.optimization_barrier(
+        (swap_y(train), shift_z(query, -1), shift_z(query, 1))
     )
-    other_train, other_rows = swapped[:rows], swapped[rows:]
-    pair_rows = jnp.where(
-        first_half,
-        jnp.concatenate([own_rows, other_rows]),
-        jnp.concatenate([other_rows, own_rows]),
-    )
-    inverse = lax.all_gather(pair_rows, "z", axis=0, tiled=True)
-
     pair_train = jnp.where(
         first_half,
         jnp.concatenate([train, other_train]),
@@ -103,25 +95,18 @@
     strip2 = dot(turned[:, 2 * quarter : 3 * quarter], turned[:, 2 * quarter :], ((0,), (0,)))
     partial = jnp.concatenate([strip0, strip2], axis=1)
     blocks = partial.reshape(4, 4, quarter // 16, 5 * quarter)
-    own_queries1 = jnp.concatenate([minus1, query, plus1])
-    other_queries1 = swap_y(own_queries1)
     near_sums, plus1, minus1 = lax.optimization_barrier((reduce_near(blocks, place), plus1, minus1))
     plus2, minus2 = shift_z(plus1, -1), shift_z(minus1, 1)
-    part, other_queries1 = lax.optimization_barrier((reduce_far(near_sums, place), other_queries1))
-    parts, plus2, minus2 = lax.optimization_barrier((gather_far(part), plus2, minus2))
-    own_queries2 = jnp.concatenate([minus2, plus2])
-    other_queries2 = swap_y(own_queries2)
+    part, own_inverse = lax.optimization_barrier((reduce_far(near_sums, place), own_inverse))
+    other_inverse = swap_y(own_inverse)
+    pieces = gather_near(gather_far(part))
+    inverse = jnp.where(
+        first_half,
+        jnp.stack([own_inverse, other_inverse], axis=1),
+        jnp.stack([other_inverse, own_inverse], axis=1),
+    ).reshape(width, width)
+    side = dot(pair_train, inverse, ((1,), (0,)))
 
-    def first(queries):
-        return dot(queries, inverse, ((1,), (1,)))
-
-    side = dot(pair_train, inverse, ((1,), (0,)))
-    near_first = first(own_queries1), first(own_queries2), first(other_queries1)
-    side, near_first, other_queries2 = lax.optimization_barrier((side, near_first, other_queries2))
-    own_first, other_first = near_first[:2], (near_first[2], first(other_queries2))
-    pieces, own_first, other_first = lax.optimization_barrier(
-        (gather_near(parts), own_first, other_first)
-    )
     gathered = joined(*pieces).reshape(quarter, 5 * quarter)
     strips = jnp.roll(gathered, place * (quarter // 16), axis=0)
     side_turned = jnp.where(first_half, side, jnp.roll(side, -quarter, axis=1))
@@ -141,40 +126,33 @@
         axis=1,
     )
     product = jnp.where(first_half, product, jnp.roll(product, quarter, axis=1))
-    left = pair_train - (0.5 * DAMPING) * side - product * (1.0 / total_rows)
-
-    own_scores = [dot(left, piece, ((1,), (1,))) for piece in own_first]
-    other_scores = [dot(left, piece, ((1,), (1,))) for piece in other_first]
-    even = [jnp.where(first_half, own, other) for own, other in zip(own_scores, other_scores)]
-    odd = [jnp.where(first_half, other, own) for own, other in zip(own_scores, other_scores)]
-
-    def tiles(scores, half_rows, offsets):
-        at = ((1, 0), (0, 0), (0, 1), (0, 2), (1, 1))
-        piece = [part[half_rows * rows : (half_rows + 1) * rows] for part in scores]
-        return [piece[at[i][0]][:, at[i][1] * rows : (at[i][1] + 1) * rows] for i in offsets]
-
-    def mixed(first_tiles, second_tiles):
-        out = []
-        for i in range(9):
-            out.append((first_tiles if i % 2 == 0 else second_tiles)[i // 2])
-        return jnp.concatenate(out, axis=1)
-
-    upper = mixed(tiles(even, 0, range(5)), tiles(odd, 0, range(4)))
-    lower = mixed(tiles(odd, 1, range(5)), tiles(even, 1, range(1, 5)))
+    other_product = swap_y(product)
+    queries = jnp.concatenate([minus1, query, plus1]), jnp.concatenate([minus2, plus2])
+    first = [dot(piece, inverse, ((1,), (1,))) for piece in queries]
+    left = 2.0 * pair_train - DAMPING * side - (product + other_product) * (1.0 / total_rows)
+    inner, outer = (dot(left, piece, ((1,), (1,))) for piece in first)
+    before, after_ = outer[:, :rows], outer[:, rows:]
+    upper = jnp.concatenate([before[:rows], inner[:rows], after_[:rows]], axis=1)
+    lower = [before[rows:], inner[rows:], after_[rows:]]
+    lower = jnp.where(
+        first_half,
+        jnp.concatenate([lower[1], lower[2], lower[0]], axis=1),
+        jnp.concatenate(lower, axis=1),
+    )
     upper, lower = lax.optimization_barrier((upper, lower))
-    window = 9 * rows
+    received = lax.all_to_all(
+        jnp.concatenate([upper, lower]), ("yh", "yl", "x", "c"), 0, 0, tiled=True
+    )
     shares = lax.axis_size("yl") * lax.axis_size("x") * lax.axis_size("c")
     own = rows // shares
-    terms = jnp.stack([upper, lower]).reshape(shares, 2, own, window)
-    core = lax.axis_index("c")
-    kept = lax.dynamic_index_in_dim(terms, core, 1, keepdims=False)
-    sent = lax.dynamic_index_in_dim(terms, 1 - core, 1, keepdims=False)
-    halves = kept + lax.ppermute(sent, "c", [(0, 1), (1, 0)])
-    received = lax.all_to_all(halves.reshape(shares * own, window), ("yh", "yl", "x"), 0, 0, tiled=True)
-    sums = received.reshape(shares, own, window).sum(axis=0)
+    sums = received.reshape(2, shares, own, 5 * rows).sum(axis=1)
+    same = jnp.where(first_half, sums[0], sums[1]).reshape(own, 5, rows)
+    cross = jnp.where(first_half, sums[1], sums[0]).reshape(own, 5, rows)
+    window = 9 * rows
+    scores = jnp.stack([same, cross], axis=2).reshape(own, 10 * rows)[:, :window]
     rank = lax.axis_index(("yl", "x", "c"))
     scale = lax.dynamic_slice_in_dim(roots, rank * own, own) * (1.0 / math.sqrt(width * shares))
-    return sums * scale[:, None]
+    return scores * scale[:, None]
 
 
 def solution(mesh):

time: 230 us -> 226 us (0.983)
  waiting for transfers between devices: 55.3 us -> 73.1 us
  matrix products: 22.9 us -> 15.2 us
  starting transfers between devices: 114 us -> 107 us
  other arithmetic: 13.3 us -> 9.31 us
  local copies, waits for them, and re-layouts: 8.26 us -> 5.38 us
    all_to_all x1, starting transfers between devices: 8.18 us -> 22.6 us  [on_device(): lax.all_to_all(jnp.concatenate([upper, lower]), ('yh', 'yl', 'x', 'c'), 0...]
    ppermute x17, waiting for transfers between devices: 39.6 us -> 51.7 us  [shift_z(): lax.ppermute(value, 'z', [(i, (i + steps) % count) for i in range(count)])]
    ppermute x17, starting transfers between devices: 83.7 us -> 72.2 us  [shift_z(): lax.ppermute(value, 'z', [(i, (i + steps) % count) for i in range(count)])]
    ppermute x1 -> x0, starting transfers between devices: 9.3 us -> none  [on_device(): halves = kept + lax.ppermute(sent, 'c', [(0, 1), (1, 0)])]
    dot_general x15 -> x11, matrix products: 22.9 us -> 15.2 us  [dot(): lax.dot_general(left, right, (dims, ((), ())), precision=FAST, preferred_...]
    ppermute x3, waiting for transfers between devices: 2.76 us -> 7.91 us  [swap_y(): return lax.ppermute(value, 'yh', [(0, 1), (1, 0)])]
    concatenate x2 -> x1, other arithmetic: 3.12 us -> 0.05 us  [on_device(): jnp.concatenate([before[:rows], inner[:rows], after_[:rows]], axis=1)]
  transfers between devices with their start and end apart: 23 -> 22, of which waited for: 11 -> 12; matrix products, arithmetic and copies ran while one was open for 12% -> 10% of each run, Pallas kernels for 0% -> 0%
where the time goes in v4:
time: 226 us; the launch traced here: 225 us
  starting transfers between devices  107 us (47%)
  waiting for transfers between devices  73.1 us (32%)
  matrix products  15.2 us (7%)
  between operations  14.1 us (6%)
  other arithmetic  9.31 us (4%)
  local copies, waits for them, and re-layouts  5.38 us (2%)
    ppermute x17, starting transfers between devices, shift_z(): lax.ppermute(value, 'z', [(i, (i + steps) % count) for i in range(count)])  72.2 us
    ppermute x17, waiting for transfers between devices, shift_z(): lax.ppermute(value, 'z', [(i, (i + steps) % count) for i in range(count)])  51.7 us
    all_to_all x1, starting transfers between devices, on_device(): lax.all_to_all(jnp.concatenate([upper, lower]), ('yh', 'yl', 'x', 'c'), 0...  22.6 us
    dot_general x11, matrix products, dot(): lax.dot_general(left, right, (dims, ((), ())), precision=FAST, preferred_...  15.2 us
    all_to_all x1, waiting for transfers between devices, on_device(): lax.all_to_all(jnp.concatenate([upper, lower]), ('yh', 'yl', 'x', 'c'), 0...  12.8 us
    ppermute x3, starting transfers between devices, swap_y(): return lax.ppermute(value, 'yh', [(0, 1), (1, 0)])  12.7 us
    ppermute x3, waiting for transfers between devices, swap_y(): return lax.ppermute(value, 'yh', [(0, 1), (1, 0)])  7.91 us
  transfers between devices with their start and end apart: 22, of which 12 were waited for; matrix products, arithmetic and copies ran while one was open for 10% of the time, Pallas kernels for 0%

profile of v4, /device:TPU:1, one launch (start us, length us, event | category | flops | bytes accessed | tf_op | source)
XLA Modules:
  0.0 224.6 jit_solution(9872195625190028959)
XLA Ops:
  9.1 5.7 %collective-permute-start = (f32[128,1024]{1,0:T(8,128)S(1)}, f32[128,1024]{1,0:T(8,128)S(1)}, u32[]{:S(2)}, u32[]{:S(2)}) collective-permute-start(f32[128,1024]{1,0:T(8,128)S(1)} %bitcast_multiply_fusion), channel_id=1, source_target_pairs={{0,16},{16,0},{1,17},{17,1},{2,18},{18,2},{3,19},{19,3},{4,20},{20... | collective-permute-start | bytes 1572872 | tf_op jit(solution)/shard_map/ppermute | solution.py:24
  15.9 11.1 %collective-permute-start.1 = (f32[128,1024]{1,0:T(8,128)S(1)}, f32[128,1024]{1,0:T(8,128)S(1)}, u32[]{:S(2)}, u32[]{:S(2)}) collective-permute-start(f32[128,1024]{1,0:T(8,128)S(1)} %bitcast.73), channel_id=1, source_target_pairs={{0,480},{32,0},{64,32},{96,64},{128,96},{160,128},{192,160},{224,1... | collective-permute-start | bytes 1572872 | tf_op jit(solution)/shard_map/ppermute | solution.py:20
  29.0 10.5 %collective-permute-done.1 = f32[128,1024]{1,0:T(8,128)S(1)} collective-permute-done((f32[128,1024]{1,0:T(8,128)S(1)}, f32[128,1024]{1,0:T(8,128)S(1)}, u32[]{:S(2)}, u32[]{:S(2)}) %collective-permute-start.1) | collective-permute-done | bytes 524320 | tf_op jit(solution)/shard_map/ppermute | solution.py:20
  40.4 6.4 %collective-permute-done.2 = f32[128,1024]{1,0:T(8,128)} collective-permute-done((f32[128,1024]{1,0:T(8,128)S(1)}, f32[128,1024]{1,0:T(8,128)}, u32[]{:S(2)}, u32[]{:S(2)}) %collective-permute-start.2) | collective-permute-done | bytes 524320 | tf_op jit(solution)/shard_map/ppermute | solution.py:20
  51.0 3.4 %collective-permute-start.3 = (f32[4,16,1280]{2,1,0:T(8,128)S(1)}, f32[4,16,1280]{2,1,0:T(8,128)}, u32[]{:S(2)}, u32[]{:S(2)}) collective-permute-start(f32[4,16,1280]{2,1,0:T(8,128)S(1)} %get-tuple-element.25), channel_id=1, source_target_pairs={{0,32},{32,64},{64,96},{96,128},{128,160},{160,192},{192,224},{224... | collective-permute-start | bytes 983048 | tf_op jit(solution)/shard_map/ppermute | solution.py:20
  57.0 4.3 %collective-permute-start.5 = (f32[4,8,1280]{2,1,0:T(8,128)}, f32[4,8,1280]{2,1,0:T(8,128)}, u32[]{:S(2)}, u32[]{:S(2)}) collective-permute-start(f32[4,8,1280]{2,1,0:T(8,128)} %get-tuple-element.35), channel_id=1, source_target_pairs={{0,64},{32,96},{64,128},{96,160},{128,192},{160,224},{192,256},{22... | collective-permute-start | bytes 491528 | tf_op jit(solution)/shard_map/ppermute | solution.py:20
  61.4 7.5 %collective-permute-done.6 = f32[4,8,1280]{2,1,0:T(8,128)} collective-permute-done((f32[4,8,1280]{2,1,0:T(8,128)}, f32[4,8,1280]{2,1,0:T(8,128)}, u32[]{:S(2)}, u32[]{:S(2)}) %collective-permute-start.6) | collective-permute-done | bytes 163872 | tf_op jit(solution)/shard_map/ppermute | solution.py:20
  71.6 6.3 %collective-permute-start.9 = (f32[16,1280]{1,0:T(8,128)S(1)}, f32[16,1280]{1,0:T(8,128)S(1)}, u32[]{:S(2)}, u32[]{:S(2)}) collective-permute-start(f32[16,1280]{1,0:T(8,128)S(1)} %get-tuple-element.33), channel_id=1, source_target_pairs={{0,256},{32,288},{64,320},{96,352},{128,384},{160,416},{192,448},{... | collective-permute-start | bytes 245768 | tf_op jit(solution)/shard_map/ppermute | solution.py:20
  78.0 4.6 %collective-permute-start.8 = (f32[16,1280]{1,0:T(8,128)S(1)}, f32[16,1280]{1,0:T(8,128)S(1)}, u32[]{:S(2)}, u32[]{:S(2)}) collective-permute-start(f32[16,1280]{1,0:T(8,128)S(1)} %get-tuple-element.34), channel_id=1, source_target_pairs={{0,384},{32,416},{64,448},{96,480},{128,0},{160,32},{192,64},{224,... | collective-permute-start | bytes 245768 | tf_op jit(solution)/shard_map/ppermute | solution.py:20
  82.7 4.5 %collective-permute-start.7 = (f32[16,1280]{1,0:T(8,128)S(1)}, f32[16,1280]{1,0:T(8,128)S(1)}, u32[]{:S(2)}, u32[]{:S(2)}) collective-permute-start(f32[16,1280]{1,0:T(8,128)S(1)} %get-tuple-element.32), channel_id=1, source_target_pairs={{0,128},{32,160},{64,192},{96,224},{128,256},{160,288},{192,320},{... | collective-permute-start | bytes 245768 | tf_op jit(solution)/shard_map/ppermute | solution.py:20
  87.2 8.1 %collective-permute-done.8 = f32[16,1280]{1,0:T(8,128)S(1)} collective-permute-done((f32[16,1280]{1,0:T(8,128)S(1)}, f32[16,1280]{1,0:T(8,128)S(1)}, u32[]{:S(2)}, u32[]{:S(2)}) %collective-permute-start.8) | collective-permute-done | bytes 81952 | tf_op jit(solution)/shard_map/ppermute | solution.py:20
  95.4 4.5 %collective-permute-start.10 = (f32[16,32,1024]{2,1,0:T(8,128)}, f32[16,32,1024]{2,1,0:T(8,128)}, u32[]{:S(2)}, u32[]{:S(2)}) collective-permute-start(f32[16,32,1024]{2,1,0:T(8,128)} %all-gather.2.cloned.1.call-done), channel_id=1, source_target_pairs={{0,16},{16,0},{1,17},{17,1},{2,18},{18,2},{3,19},{19,3},{4,20},{20... | collective-permute-start | bytes 6291464 | tf_op jit(solution)/shard_map/ppermute | solution.py:24
  99.9 2.4 %collective-permute-start.13 = (f32[16,1280]{1,0:T(8,128)S(1)}, f32[16,1280]{1,0:T(8,128)S(1)}, u32[]{:S(2)}, u32[]{:S(2)}) collective-permute-start(f32[16,1280]{1,0:T(8,128)S(1)} %fusion.29), channel_id=1, source_target_pairs={{0,128},{32,160},{64,192},{96,224},{128,256},{160,288},{192,320},{... | collective-permute-start | bytes 245768 | tf_op jit(solution)/shard_map/ppermute | solution.py:20
  102.3 7.7 %collective-permute-start.12 = (f32[16,1280]{1,0:T(8,128)S(1)}, f32[16,1280]{1,0:T(8,128)S(1)}, u32[]{:S(2)}, u32[]{:S(2)}) collective-permute-start(f32[16,1280]{1,0:T(8,128)S(1)} %fusion.29), channel_id=1, source_target_pairs={{0,256},{32,288},{64,320},{96,352},{128,384},{160,416},{192,448},{... | collective-permute-start | bytes 245768 | tf_op jit(solution)/shard_map/ppermute | solution.py:20
  110.0 5.0 %collective-permute-start.11 = (f32[16,1280]{1,0:T(8,128)S(1)}, f32[16,1280]{1,0:T(8,128)S(1)}, u32[]{:S(2)}, u32[]{:S(2)}) collective-permute-start(f32[16,1280]{1,0:T(8,128)S(1)} %fusion.29), channel_id=1, source_target_pairs={{0,384},{32,416},{64,448},{96,480},{128,0},{160,32},{192,64},{224,... | collective-permute-start | bytes 245768 | tf_op jit(solution)/shard_map/ppermute | solution.py:20
  115.1 2.4 %collective-permute-done.12 = f32[16,1280]{1,0:T(8,128)S(1)} collective-permute-done((f32[16,1280]{1,0:T(8,128)S(1)}, f32[16,1280]{1,0:T(8,128)S(1)}, u32[]{:S(2)}, u32[]{:S(2)}) %collective-permute-start.12) | collective-permute-done | bytes 81952 | tf_op jit(solution)/shard_map/ppermute | solution.py:20
  117.5 3.7 %collective-permute-done.11 = f32[16,1280]{1,0:T(8,128)S(1)} collective-permute-done((f32[16,1280]{1,0:T(8,128)S(1)}, f32[16,1280]{1,0:T(8,128)S(1)}, u32[]{:S(2)}, u32[]{:S(2)}) %collective-permute-start.11) | collective-permute-done | bytes 81952 | tf_op jit(solution)/shard_map/ppermute | solution.py:20
  121.3 3.6 %collective-permute-start.16 = (f32[4,16,1280]{2,1,0:T(8,128)S(1)}, f32[4,16,1280]{2,1,0:T(8,128)S(1)}, u32[]{:S(2)}, u32[]{:S(2)}) collective-permute-start(f32[4,16,1280]{2,1,0:T(8,128)S(1)} %get-tuple-element.31), channel_id=1, source_target_pairs={{0,32},{32,64},{64,96},{96,128},{128,160},{160,192},{192,224},{224... | collective-permute-start | bytes 983048 | tf_op jit(solution)/shard_map/ppermute | solution.py:20
  124.9 6.2 %collective-permute-start.15 = (f32[4,16,1280]{2,1,0:T(8,128)S(1)}, f32[4,16,1280]{2,1,0:T(8,128)S(1)}, u32[]{:S(2)}, u32[]{:S(2)}) collective-permute-start(f32[4,16,1280]{2,1,0:T(8,128)S(1)} %get-tuple-element.31), channel_id=1, source_target_pairs={{0,448},{32,480},{64,0},{96,32},{128,64},{160,96},{192,128},{224,1... | collective-permute-start | bytes 983048 | tf_op jit(solution)/shard_map/ppermute | solution.py:20
  133.0 2.2 collective-permute-start.19
  135.2 3.1 %collective-permute-start.18 = (f32[128,1024]{1,0:T(8,128)}, f32[128,1024]{1,0:T(8,128)S(1)}, u32[]{:S(2)}, u32[]{:S(2)}) collective-permute-start(f32[128,1024]{1,0:T(8,128)} %collective-permute-done.2), channel_id=1, source_target_pairs={{0,32},{32,64},{64,96},{96,128},{128,160},{160,192},{192,224},{224... | collective-permute-start | bytes 1572872 | tf_op jit(solution)/shard_map/ppermute | solution.py:20
  138.3 2.3 %collective-permute-done.15 = f32[4,16,1280]{2,1,0:T(8,128)S(1)} collective-permute-done((f32[4,16,1280]{2,1,0:T(8,128)S(1)}, f32[4,16,1280]{2,1,0:T(8,128)S(1)}, u32[]{:S(2)}, u32[]{:S(2)}) %collective-permute-start.15) | collective-permute-done | bytes 327712 | tf_op jit(solution)/shard_map/ppermute | solution.py:20
  140.7 8.5 %collective-permute-done.14 = f32[4,16,1280]{2,1,0:T(8,128)S(1)} collective-permute-done((f32[4,16,1280]{2,1,0:T(8,128)S(1)}, f32[4,16,1280]{2,1,0:T(8,128)S(1)}, u32[]{:S(2)}, u32[]{:S(2)}) %collective-permute-start.14) | collective-permute-done | bytes 327712 | tf_op jit(solution)/shard_map/ppermute | solution.py:20
  150.8 2.9 %maximum_select_fusion = f32[16,2,32,1024]{3,2,1,0:T(8,128)S(1)} fusion(f32[16,1,32,1024]{3,2,1,0:T(8,128)} %bitcast.10, f32[16,1,32,1024]{3,2,1,0:T(8,128)S(1)} %bitcast.76, pred[]{:T(512)S(6)} %eq.15), kind=kLoop, calls=%fused_computation | loop fusion | flops 3145728 | bytes 8388609 | tf_op jit(solution)/shard_map/jit(_where)/select_n | solution.py:103
  153.8 2.3 %fusion.36 = f32[256,1024]{1,0:T(8,128)S(1)} fusion(f32[256,1024]{1,0:T(8,128)S(1)} %maximum_select_fusion.1, f32[1024,1024]{1,0:T(8,128)S(1)} %bitcast.67), kind=kOutput, calls=%fused_computation.72 | convolution fusion | flops 1610612736 | bytes 6291456 | tf_op jit(solution)/shard_map/dot_general | solution.py:13
  158.2 2.6 %collective-permute-start.17 = (f32[256,1024]{1,0:T(8,128)S(1)}, f32[256,1024]{1,0:T(8,128)S(1)}, u32[]{:S(2)}, u32[]{:S(2)}) collective-permute-start(f32[256,1024]{1,0:T(8,128)S(1)} %maximum_select_fusion.4), channel_id=1, source_target_pairs={{0,16},{16,0},{1,17},{17,1},{2,18},{18,2},{3,19},{19,3},{4,20},{20... | collective-permute-start | bytes 3145736 | tf_op jit(solution)/shard_map/ppermute | solution.py:24
  161.4 2.2 fusion.7
  163.6 5.1 %fusion = f32[384,1024]{1,0:T(8,128)} fusion(f32[1024,1024]{1,0:T(8,128)S(1)} %bitcast.69, f32[128,1024]{1,0:T(8,128)S(1)} %copy-done.2, f32[128,1024]{1,0:T(8,128)S(1)} %bitcast.75, f32[128,1024]{1,0:T(8,128)} %collective-permute-done.2), kind=kOutput, calls=%fused_computation.3 | convolution fusion | flops 2416705536 | bytes 7340032 | tf_op jit(solution)/shard_map/dot_general | solution.py:13
  168.7 7.9 %collective-permute-done.17 = f32[256,1024]{1,0:T(8,128)S(1)} collective-permute-done((f32[256,1024]{1,0:T(8,128)S(1)}, f32[256,1024]{1,0:T(8,128)S(1)}, u32[]{:S(2)}, u32[]{:S(2)}) %collective-permute-start.17) | collective-permute-done | bytes 1048608 | tf_op jit(solution)/shard_map/ppermute | solution.py:24
  177.8 2.4 %fusion.38 = f32[256,384]{1,0:T(8,128)S(1)} fusion(f32[256,1024]{1,0:T(8,128)S(1)} %multiply_subtract_fusion, f32[384,1024]{1,0:T(8,128)} %fusion), kind=kOutput, calls=%fused_computation.74 | convolution fusion | flops 603979776 | bytes 3014656 | tf_op jit(solution)/shard_map/dot_general | solution.py:13
  181.5 22.6 %all-to-all-start = ((f32[32,8,640]{2,1,0:T(8,128)}), f32[32,8,640]{2,1,0:T(8,128)S(1)}, u32[]{:S(2)}, u32[]{:S(2)}) async-start(f32[32,8,640]{2,1,0:T(8,128)} %maximum_bitcast_fusion), calls=%async_computation | async-start | bytes 1310720 | tf_op jit(solution)/shard_map/all_to_all | solution.py:143
  204.2 12.8 %all-to-all-done = f32[32,8,640]{2,1,0:T(8,128)S(1)} async-done(((f32[32,8,640]{2,1,0:T(8,128)}), f32[32,8,640]{2,1,0:T(8,128)S(1)}, u32[]{:S(2)}, u32[]{:S(2)}) %all-to-all-start) | async-done | bytes 655392 | tf_op jit(solution)/shard_map/all_to_all | solution.py:143
  (70 shorter events, 25.7 us)
Async XLA Ops:
  6.5 88.8 %all-gather.2.cloned.1.call-start = ((), (), s32[]{:S(2)}) async-start(), calls=%async_computation.1 | async-start | bytes 2228224 | tf_op jit(solution)/shard_map/all_gather | solution.py:84
  9.1 19.9 %collective-permute-start = (f32[128,1024]{1,0:T(8,128)S(1)}, f32[128,1024]{1,0:T(8,128)S(1)}, u32[]{:S(2)}, u32[]{:S(2)}) collective-permute-start(f32[128,1024]{1,0:T(8,128)S(1)} %bitcast_multiply_fusion), channel_id=1, source_target_pairs={{0,16},{16,0},{1,17},{17,1},{2,18},{18,2},{3,19},{19,3},{4,20},{20... | collective-permute-start | bytes 1572872 | tf_op jit(solution)/shard_map/ppermute | solution.py:24
  15.9 23.7 %collective-permute-start.1 = (f32[128,1024]{1,0:T(8,128)S(1)}, f32[128,1024]{1,0:T(8,128)S(1)}, u32[]{:S(2)}, u32[]{:S(2)}) collective-permute-start(f32[128,1024]{1,0:T(8,128)S(1)} %bitcast.73), channel_id=1, source_target_pairs={{0,480},{32,0},{64,32},{96,64},{128,96},{160,128},{192,160},{224,1... | collective-permute-start | bytes 1572872 | tf_op jit(solution)/shard_map/ppermute | solution.py:20
  27.1 19.8 %collective-permute-start.2 = (f32[128,1024]{1,0:T(8,128)S(1)}, f32[128,1024]{1,0:T(8,128)}, u32[]{:S(2)}, u32[]{:S(2)}) collective-permute-start(f32[128,1024]{1,0:T(8,128)S(1)} %bitcast.74), channel_id=1, source_target_pairs={{0,32},{32,64},{64,96},{96,128},{128,160},{160,192},{192,224},{224... | collective-permute-start | bytes 1572872 | tf_op jit(solution)/shard_map/ppermute | solution.py:20
  39.6 0.8 copy-start.1
  49.1 21.3 %collective-permute-start.4 = (f32[4,16,1280]{2,1,0:T(8,128)}, f32[4,16,1280]{2,1,0:T(8,128)S(1)}, u32[]{:S(2)}, u32[]{:S(2)}) collective-permute-start(f32[4,16,1280]{2,1,0:T(8,128)} %get-tuple-element.27), channel_id=1, source_target_pairs={{0,480},{32,0},{64,32},{96,64},{128,96},{160,128},{192,160},{224,1... | collective-permute-start | bytes 983048 | tf_op jit(solution)/shard_map/ppermute | solution.py:20
  51.0 19.4 %collective-permute-start.3 = (f32[4,16,1280]{2,1,0:T(8,128)S(1)}, f32[4,16,1280]{2,1,0:T(8,128)}, u32[]{:S(2)}, u32[]{:S(2)}) collective-permute-start(f32[4,16,1280]{2,1,0:T(8,128)S(1)} %get-tuple-element.25), channel_id=1, source_target_pairs={{0,32},{32,64},{64,96},{96,128},{128,160},{160,192},{192,224},{224... | collective-permute-start | bytes 983048 | tf_op jit(solution)/shard_map/ppermute | solution.py:20
  55.1 13.8 %collective-permute-start.6 = (f32[4,8,1280]{2,1,0:T(8,128)}, f32[4,8,1280]{2,1,0:T(8,128)}, u32[]{:S(2)}, u32[]{:S(2)}) collective-permute-start(f32[4,8,1280]{2,1,0:T(8,128)} %get-tuple-element.36), channel_id=1, source_target_pairs={{0,448},{32,480},{64,0},{96,32},{128,64},{160,96},{192,128},{224,1... | collective-permute-start | bytes 491528 | tf_op jit(solution)/shard_map/ppermute | solution.py:20
  57.0 13.4 %collective-permute-start.5 = (f32[4,8,1280]{2,1,0:T(8,128)}, f32[4,8,1280]{2,1,0:T(8,128)}, u32[]{:S(2)}, u32[]{:S(2)}) collective-permute-start(f32[4,8,1280]{2,1,0:T(8,128)} %get-tuple-element.35), channel_id=1, source_target_pairs={{0,64},{32,96},{64,128},{96,160},{128,192},{160,224},{192,256},{22... | collective-permute-start | bytes 491528 | tf_op jit(solution)/shard_map/ppermute | solution.py:20
  71.6 15.6 %collective-permute-start.9 = (f32[16,1280]{1,0:T(8,128)S(1)}, f32[16,1280]{1,0:T(8,128)S(1)}, u32[]{:S(2)}, u32[]{:S(2)}) collective-permute-start(f32[16,1280]{1,0:T(8,128)S(1)} %get-tuple-element.33), channel_id=1, source_target_pairs={{0,256},{32,288},{64,320},{96,352},{128,384},{160,416},{192,448},{... | collective-permute-start | bytes 245768 | tf_op jit(solution)/shard_map/ppermute | solution.py:20
  78.0 17.3 %collective-permute-start.8 = (f32[16,1280]{1,0:T(8,128)S(1)}, f32[16,1280]{1,0:T(8,128)S(1)}, u32[]{:S(2)}, u32[]{:S(2)}) collective-permute-start(f32[16,1280]{1,0:T(8,128)S(1)} %get-tuple-element.34), channel_id=1, source_target_pairs={{0,384},{32,416},{64,448},{96,480},{128,0},{160,32},{192,64},{224,... | collective-permute-start | bytes 245768 | tf_op jit(solution)/shard_map/ppermute | solution.py:20
  82.7 12.7 %collective-permute-start.7 = (f32[16,1280]{1,0:T(8,128)S(1)}, f32[16,1280]{1,0:T(8,128)S(1)}, u32[]{:S(2)}, u32[]{:S(2)}) collective-permute-start(f32[16,1280]{1,0:T(8,128)S(1)} %get-tuple-element.32), channel_id=1, source_target_pairs={{0,128},{32,160},{64,192},{96,224},{128,256},{160,288},{192,320},{... | collective-permute-start | bytes 245768 | tf_op jit(solution)/shard_map/ppermute | solution.py:20
  95.4 54.2 %collective-permute-start.10 = (f32[16,32,1024]{2,1,0:T(8,128)}, f32[16,32,1024]{2,1,0:T(8,128)}, u32[]{:S(2)}, u32[]{:S(2)}) collective-permute-start(f32[16,32,1024]{2,1,0:T(8,128)} %all-gather.2.cloned.1.call-done), channel_id=1, source_target_pairs={{0,16},{16,0},{1,17},{17,1},{2,18},{18,2},{3,19},{19,3},{4,20},{20... | collective-permute-start | bytes 6291464 | tf_op jit(solution)/shard_map/ppermute | solution.py:24
  99.9 15.2 %collective-permute-start.13 = (f32[16,1280]{1,0:T(8,128)S(1)}, f32[16,1280]{1,0:T(8,128)S(1)}, u32[]{:S(2)}, u32[]{:S(2)}) collective-permute-start(f32[16,1280]{1,0:T(8,128)S(1)} %fusion.29), channel_id=1, source_target_pairs={{0,128},{32,160},{64,192},{96,224},{128,256},{160,288},{192,320},{... | collective-permute-start | bytes 245768 | tf_op jit(solution)/shard_map/ppermute | solution.py:20
  102.3 15.2 %collective-permute-start.12 = (f32[16,1280]{1,0:T(8,128)S(1)}, f32[16,1280]{1,0:T(8,128)S(1)}, u32[]{:S(2)}, u32[]{:S(2)}) collective-permute-start(f32[16,1280]{1,0:T(8,128)S(1)} %fusion.29), channel_id=1, source_target_pairs={{0,256},{32,288},{64,320},{96,352},{128,384},{160,416},{192,448},{... | collective-permute-start | bytes 245768 | tf_op jit(solution)/shard_map/ppermute | solution.py:20
  110.0 11.2 %collective-permute-start.11 = (f32[16,1280]{1,0:T(8,128)S(1)}, f32[16,1280]{1,0:T(8,128)S(1)}, u32[]{:S(2)}, u32[]{:S(2)}) collective-permute-start(f32[16,1280]{1,0:T(8,128)S(1)} %fusion.29), channel_id=1, source_target_pairs={{0,384},{32,416},{64,448},{96,480},{128,0},{160,32},{192,64},{224,... | collective-permute-start | bytes 245768 | tf_op jit(solution)/shard_map/ppermute | solution.py:20
  121.3 13.9 %collective-permute-start.16 = (f32[4,16,1280]{2,1,0:T(8,128)S(1)}, f32[4,16,1280]{2,1,0:T(8,128)S(1)}, u32[]{:S(2)}, u32[]{:S(2)}) collective-permute-start(f32[4,16,1280]{2,1,0:T(8,128)S(1)} %get-tuple-element.31), channel_id=1, source_target_pairs={{0,32},{32,64},{64,96},{96,128},{128,160},{160,192},{192,224},{224... | collective-permute-start | bytes 983048 | tf_op jit(solution)/shard_map/ppermute | solution.py:20
  124.9 15.8 %collective-permute-start.15 = (f32[4,16,1280]{2,1,0:T(8,128)S(1)}, f32[4,16,1280]{2,1,0:T(8,128)S(1)}, u32[]{:S(2)}, u32[]{:S(2)}) collective-permute-start(f32[4,16,1280]{2,1,0:T(8,128)S(1)} %get-tuple-element.31), channel_id=1, source_target_pairs={{0,448},{32,480},{64,0},{96,32},{128,64},{160,96},{192,128},{224,1... | collective-permute-start | bytes 983048 | tf_op jit(solution)/shard_map/ppermute | solution.py:20
  131.0 18.1 %collective-permute-start.14 = (f32[4,16,1280]{2,1,0:T(8,128)S(1)}, f32[4,16,1280]{2,1,0:T(8,128)S(1)}, u32[]{:S(2)}, u32[]{:S(2)}) collective-permute-start(f32[4,16,1280]{2,1,0:T(8,128)S(1)} %get-tuple-element.31), channel_id=1, source_target_pairs={{0,480},{32,0},{64,32},{96,64},{128,96},{160,128},{192,160},{224,1... | collective-permute-start | bytes 983048 | tf_op jit(solution)/shard_map/ppermute | solution.py:20
  133.0 28.5 %collective-permute-start.19 = (f32[128,1024]{1,0:T(8,128)}, f32[128,1024]{1,0:T(8,128)S(1)}, u32[]{:S(2)}, u32[]{:S(2)}) collective-permute-start(f32[128,1024]{1,0:T(8,128)} %copy-done.1), channel_id=1, source_target_pairs={{0,480},{32,0},{64,32},{96,64},{128,96},{160,128},{192,160},{224,1... | collective-permute-start | bytes 1572872 | tf_op jit(solution)/shard_map/ppermute | solution.py:20
  135.2 26.3 %collective-permute-start.18 = (f32[128,1024]{1,0:T(8,128)}, f32[128,1024]{1,0:T(8,128)S(1)}, u32[]{:S(2)}, u32[]{:S(2)}) collective-permute-start(f32[128,1024]{1,0:T(8,128)} %collective-permute-done.2), channel_id=1, source_target_pairs={{0,32},{32,64},{64,96},{96,128},{128,160},{160,192},{192,224},{224... | collective-permute-start | bytes 1572872 | tf_op jit(solution)/shard_map/ppermute | solution.py:20
  149.3 1.6 copy-start
  158.2 5.4 %copy-start.2 = (f32[128,1024]{1,0:T(8,128)S(1)}, f32[128,1024]{1,0:T(8,128)}, u32[]{:S(2)}) copy-start(f32[128,1024]{1,0:T(8,128)} %copy-done.1) | copy-start | bytes 1572868
  158.2 18.4 %collective-permute-start.17 = (f32[256,1024]{1,0:T(8,128)S(1)}, f32[256,1024]{1,0:T(8,128)S(1)}, u32[]{:S(2)}, u32[]{:S(2)}) collective-permute-start(f32[256,1024]{1,0:T(8,128)S(1)} %maximum_select_fusion.4), channel_id=1, source_target_pairs={{0,16},{16,0},{1,17},{17,1},{2,18},{18,2},{3,19},{19,3},{4,20},{20... | collective-permute-start | bytes 3145736 | tf_op jit(solution)/shard_map/ppermute | solution.py:24
  181.5 35.5 %all-to-all-start = ((f32[32,8,640]{2,1,0:T(8,128)}), f32[32,8,640]{2,1,0:T(8,128)S(1)}, u32[]{:S(2)}, u32[]{:S(2)}) async-start(f32[32,8,640]{2,1,0:T(8,128)} %maximum_bitcast_fusion), calls=%async_computation | async-start | bytes 1310720 | tf_op jit(solution)/shard_map/all_to_all | solution.py:143
Sparse Core Ops, SparseCore 0:
  9.4 82.6 all-gather.1

commit v5 on v4

--- a/solution.py
+++ b/solution.py
@@ -82,9 +82,8 @@
     total_rows = rows * lax.axis_size("z") * lax.axis_size("yh")
 
     own_inverse = lax.all_gather(inverse_factors[0], "z", axis=0)
-    other_train, plus1, minus1 = lax.optimization_barrier(
-        (swap_y(train), shift_z(query, -1), shift_z(query, 1))
-    )
+    other_train = swap_y(train)
+    plus1, minus1 = shift_z(query, -1), shift_z(query, 1)
     pair_train = jnp.where(
         first_half,
         jnp.concatenate([train, other_train]),
@@ -95,9 +94,11 @@
     strip2 = dot(turned[:, 2 * quarter : 3 * quarter], turned[:, 2 * quarter :], ((0,), (0,)))
     partial = jnp.concatenate([strip0, strip2], axis=1)
     blocks = partial.reshape(4, 4, quarter // 16, 5 * quarter)
-    near_sums, plus1, minus1 = lax.optimization_barrier((reduce_near(blocks, place), plus1, minus1))
+    near_sums = reduce_near(blocks, place)
+    part, own_inverse, plus1, minus1 = lax.optimization_barrier(
+        (reduce_far(near_sums, place), own_inverse, plus1, minus1)
+    )
     plus2, minus2 = shift_z(plus1, -1), shift_z(minus1, 1)
-    part, own_inverse = lax.optimization_barrier((reduce_far(near_sums, place), own_inverse))
     other_inverse = swap_y(own_inverse)
     pieces = gather_near(gather_far(part))
     inverse = jnp.where(

time: 226 us -> 241 us (1.066)
  waiting for transfers between devices: 73.1 us -> 91.7 us
  starting transfers between devices: 107 us -> 103 us
    ppermute x3, waiting for transfers between devices: 7.91 us -> 23.8 us  [swap_y(): return lax.ppermute(value, 'yh', [(0, 1), (1, 0)])]
    all_to_all x1, starting transfers between devices: 22.6 us -> 9.78 us  [on_device(): lax.all_to_all(jnp.concatenate([upper, lower]), ('yh', 'yl', 'x', 'c'), 0...]
    ppermute x17, starting transfers between devices: 72.2 us -> 77.8 us  [shift_z(): lax.ppermute(value, 'z', [(i, (i + steps) % count) for i in range(count)])]
    ppermute x3, starting transfers between devices: 12.7 us -> 15.6 us  [swap_y(): return lax.ppermute(value, 'yh', [(0, 1), (1, 0)])]
    ppermute x17, waiting for transfers between devices: 51.7 us -> 54.4 us  [shift_z(): lax.ppermute(value, 'z', [(i, (i + steps) % count) for i in range(count)])]
  transfers between devices with their start and end apart: 22 -> 22, of which waited for: 12 -> 11; matrix products, arithmetic and copies ran while one was open for 10% -> 10% of each run, Pallas kernels for 0% -> 0%
where the time goes in v5:
time: 241 us; the launch traced here: 240 us
  starting transfers between devices  103 us (43%)
  waiting for transfers between devices  91.7 us (38%)
  matrix products  14.2 us (6%)
  between operations  14.1 us (6%)
  other arithmetic  11 us (5%)
  local copies, waits for them, and re-layouts  5.34 us (2%)
    ppermute x17, starting transfers between devices, shift_z(): lax.ppermute(value, 'z', [(i, (i + steps) % count) for i in range(count)])  77.8 us
    ppermute x17, waiting for transfers between devices, shift_z(): lax.ppermute(value, 'z', [(i, (i + steps) % count) for i in range(count)])  54.4 us
    ppermute x3, waiting for transfers between devices, swap_y(): return lax.ppermute(value, 'yh', [(0, 1), (1, 0)])  23.8 us
    ppermute x3, starting transfers between devices, swap_y(): return lax.ppermute(value, 'yh', [(0, 1), (1, 0)])  15.6 us
    dot_general x11, matrix products, dot(): lax.dot_general(left, right, (dims, ((), ())), precision=FAST, preferred_...  14.2 us
    all_to_all x1, waiting for transfers between devices, on_device(): lax.all_to_all(jnp.concatenate([upper, lower]), ('yh', 'yl', 'x', 'c'), 0...  12.8 us
    all_to_all x1, starting transfers between devices, on_device(): lax.all_to_all(jnp.concatenate([upper, lower]), ('yh', 'yl', 'x', 'c'), 0...  9.78 us
  transfers between devices with their start and end apart: 22, of which 11 were waited for; matrix products, arithmetic and copies ran while one was open for 10% of the time, Pallas kernels for 0%

profile of v5, /device:TPU:1, one launch (start us, length us, event | category | flops | bytes accessed | tf_op | source)
XLA Modules:
  0.0 239.5 jit_solution(5238977347192366468)
XLA Ops:
  9.1 5.7 %collective-permute-start = (f32[128,1024]{1,0:T(8,128)S(1)}, f32[128,1024]{1,0:T(8,128)S(1)}, u32[]{:S(2)}, u32[]{:S(2)}) collective-permute-start(f32[128,1024]{1,0:T(8,128)S(1)} %bitcast_multiply_fusion), channel_id=1, source_target_pairs={{0,16},{16,0},{1,17},{17,1},{2,18},{18,2},{3,19},{19,3},{4,20},{20... | collective-permute-start | bytes 1572872 | tf_op jit(solution)/shard_map/ppermute | solution.py:24
  14.8 8.3 %collective-permute-done = f32[128,1024]{1,0:T(8,128)S(1)} collective-permute-done((f32[128,1024]{1,0:T(8,128)S(1)}, f32[128,1024]{1,0:T(8,128)S(1)}, u32[]{:S(2)}, u32[]{:S(2)}) %collective-permute-start) | collective-permute-done | bytes 524320 | tf_op jit(solution)/shard_map/ppermute | solution.py:24
  25.3 14.3 %collective-permute-start.2 = (f32[4,16,1280]{2,1,0:T(8,128)}, f32[4,16,1280]{2,1,0:T(8,128)S(1)}, u32[]{:S(2)}, u32[]{:S(2)}) collective-permute-start(f32[4,16,1280]{2,1,0:T(8,128)} %get-tuple-element.19), channel_id=1, source_target_pairs={{0,480},{32,0},{64,32},{96,64},{128,96},{160,128},{192,160},{224,1... | collective-permute-start | bytes 983048 | tf_op jit(solution)/shard_map/ppermute | solution.py:20
  42.3 3.8 %collective-permute-start.4 = (f32[4,8,1280]{2,1,0:T(8,128)}, f32[4,8,1280]{2,1,0:T(8,128)}, u32[]{:S(2)}, u32[]{:S(2)}) collective-permute-start(f32[4,8,1280]{2,1,0:T(8,128)} %get-tuple-element.28), channel_id=1, source_target_pairs={{0,448},{32,480},{64,0},{96,32},{128,64},{160,96},{192,128},{224,1... | collective-permute-start | bytes 491528 | tf_op jit(solution)/shard_map/ppermute | solution.py:20
  46.1 2.4 collective-permute-start.3
  48.6 10.7 %collective-permute-done.4 = f32[4,8,1280]{2,1,0:T(8,128)} collective-permute-done((f32[4,8,1280]{2,1,0:T(8,128)}, f32[4,8,1280]{2,1,0:T(8,128)}, u32[]{:S(2)}, u32[]{:S(2)}) %collective-permute-start.4) | collective-permute-done | bytes 163872 | tf_op jit(solution)/shard_map/ppermute | solution.py:20
  62.0 8.9 %collective-permute-start.7 = (f32[16,1280]{1,0:T(8,128)S(1)}, f32[16,1280]{1,0:T(8,128)S(1)}, u32[]{:S(2)}, u32[]{:S(2)}) collective-permute-start(f32[16,1280]{1,0:T(8,128)S(1)} %get-tuple-element.25), channel_id=1, source_target_pairs={{0,256},{32,288},{64,320},{96,352},{128,384},{160,416},{192,448},{... | collective-permute-start | bytes 245768 | tf_op jit(solution)/shard_map/ppermute | solution.py:20
  72.8 7.3 %collective-permute-start.5 = (f32[16,1280]{1,0:T(8,128)S(1)}, f32[16,1280]{1,0:T(8,128)S(1)}, u32[]{:S(2)}, u32[]{:S(2)}) collective-permute-start(f32[16,1280]{1,0:T(8,128)S(1)} %get-tuple-element.24), channel_id=1, source_target_pairs={{0,128},{32,160},{64,192},{96,224},{128,256},{160,288},{192,320},{... | collective-permute-start | bytes 245768 | tf_op jit(solution)/shard_map/ppermute | solution.py:20
  80.2 2.3 collective-permute-start.8
  82.6 4.4 %collective-permute-start.9 = (f32[128,1024]{1,0:T(8,128)S(1)}, f32[128,1024]{1,0:T(8,128)S(1)}, u32[]{:S(2)}, u32[]{:S(2)}) collective-permute-start(f32[128,1024]{1,0:T(8,128)S(1)} %bitcast.74), channel_id=1, source_target_pairs={{0,32},{32,64},{64,96},{96,128},{128,160},{160,192},{192,224},{224... | collective-permute-start | bytes 1572872 | tf_op jit(solution)/shard_map/ppermute | solution.py:20
  87.0 2.9 %collective-permute-done.6 = f32[16,1280]{1,0:T(8,128)S(1)} collective-permute-done((f32[16,1280]{1,0:T(8,128)S(1)}, f32[16,1280]{1,0:T(8,128)S(1)}, u32[]{:S(2)}, u32[]{:S(2)}) %collective-permute-start.6) | collective-permute-done | bytes 81952 | tf_op jit(solution)/shard_map/ppermute | solution.py:20
  90.0 14.7 %collective-permute-done.8 = f32[128,1024]{1,0:T(8,128)S(1)} collective-permute-done((f32[128,1024]{1,0:T(8,128)S(1)}, f32[128,1024]{1,0:T(8,128)S(1)}, u32[]{:S(2)}, u32[]{:S(2)}) %collective-permute-start.8) | collective-permute-done | bytes 524320 | tf_op jit(solution)/shard_map/ppermute | solution.py:20
  104.6 5.7 %collective-permute-start.10 = (f32[16,32,1024]{2,1,0:T(8,128)}, f32[16,32,1024]{2,1,0:T(8,128)}, u32[]{:S(2)}, u32[]{:S(2)}) collective-permute-start(f32[16,32,1024]{2,1,0:T(8,128)} %all-gather.2.cloned.1.call-done), channel_id=1, source_target_pairs={{0,16},{16,0},{1,17},{17,1},{2,18},{18,2},{3,19},{19,3},{4,20},{20... | collective-permute-start | bytes 6291464 | tf_op jit(solution)/shard_map/ppermute | solution.py:24
  110.3 3.0 %collective-permute-start.13 = (f32[16,1280]{1,0:T(8,128)S(1)}, f32[16,1280]{1,0:T(8,128)S(1)}, u32[]{:S(2)}, u32[]{:S(2)}) collective-permute-start(f32[16,1280]{1,0:T(8,128)S(1)} %fusion.29), channel_id=1, source_target_pairs={{0,128},{32,160},{64,192},{96,224},{128,256},{160,288},{192,320},{... | collective-permute-start | bytes 245768 | tf_op jit(solution)/shard_map/ppermute | solution.py:20
  113.4 7.3 %collective-permute-start.12 = (f32[16,1280]{1,0:T(8,128)S(1)}, f32[16,1280]{1,0:T(8,128)S(1)}, u32[]{:S(2)}, u32[]{:S(2)}) collective-permute-start(f32[16,1280]{1,0:T(8,128)S(1)} %fusion.29), channel_id=1, source_target_pairs={{0,256},{32,288},{64,320},{96,352},{128,384},{160,416},{192,448},{... | collective-permute-start | bytes 245768 | tf_op jit(solution)/shard_map/ppermute | solution.py:20
  120.6 4.7 %collective-permute-start.11 = (f32[16,1280]{1,0:T(8,128)S(1)}, f32[16,1280]{1,0:T(8,128)S(1)}, u32[]{:S(2)}, u32[]{:S(2)}) collective-permute-start(f32[16,1280]{1,0:T(8,128)S(1)} %fusion.29), channel_id=1, source_target_pairs={{0,384},{32,416},{64,448},{96,480},{128,0},{160,32},{192,64},{224,... | collective-permute-start | bytes 245768 | tf_op jit(solution)/shard_map/ppermute | solution.py:20
  125.4 2.8 %collective-permute-done.12 = f32[16,1280]{1,0:T(8,128)S(1)} collective-permute-done((f32[16,1280]{1,0:T(8,128)S(1)}, f32[16,1280]{1,0:T(8,128)S(1)}, u32[]{:S(2)}, u32[]{:S(2)}) %collective-permute-start.12) | collective-permute-done | bytes 81952 | tf_op jit(solution)/shard_map/ppermute | solution.py:20
  128.2 11.2 %collective-permute-done.11 = f32[16,1280]{1,0:T(8,128)S(1)} collective-permute-done((f32[16,1280]{1,0:T(8,128)S(1)}, f32[16,1280]{1,0:T(8,128)S(1)}, u32[]{:S(2)}, u32[]{:S(2)}) %collective-permute-start.11) | collective-permute-done | bytes 81952 | tf_op jit(solution)/shard_map/ppermute | solution.py:20
  142.1 4.9 %collective-permute-start.15 = (f32[4,16,1280]{2,1,0:T(8,128)}, f32[4,16,1280]{2,1,0:T(8,128)S(1)}, u32[]{:S(2)}, u32[]{:S(2)}) collective-permute-start(f32[4,16,1280]{2,1,0:T(8,128)} %get-tuple-element.23), channel_id=1, source_target_pairs={{0,448},{32,480},{64,0},{96,32},{128,64},{160,96},{192,128},{224,1... | collective-permute-start | bytes 983048 | tf_op jit(solution)/shard_map/ppermute | solution.py:20
  147.1 3.4 %collective-permute-start.14 = (f32[4,16,1280]{2,1,0:T(8,128)}, f32[4,16,1280]{2,1,0:T(8,128)}, u32[]{:S(2)}, u32[]{:S(2)}) collective-permute-start(f32[4,16,1280]{2,1,0:T(8,128)} %get-tuple-element.23), channel_id=1, source_target_pairs={{0,480},{32,0},{64,32},{96,64},{128,96},{160,128},{192,160},{224,1... | collective-permute-start | bytes 983048 | tf_op jit(solution)/shard_map/ppermute | solution.py:20
  152.4 3.4 %collective-permute-start.18 = (f32[128,1024]{1,0:T(8,128)S(1)}, f32[128,1024]{1,0:T(8,128)S(1)}, u32[]{:S(2)}, u32[]{:S(2)}) collective-permute-start(f32[128,1024]{1,0:T(8,128)S(1)} %collective-permute-done.9), channel_id=1, source_target_pairs={{0,32},{32,64},{64,96},{96,128},{128,160},{160,192},{192,224},{224... | collective-permute-start | bytes 1572872 | tf_op jit(solution)/shard_map/ppermute | solution.py:20
  157.6 2.7 %collective-permute-done.15 = f32[4,16,1280]{2,1,0:T(8,128)S(1)} collective-permute-done((f32[4,16,1280]{2,1,0:T(8,128)}, f32[4,16,1280]{2,1,0:T(8,128)S(1)}, u32[]{:S(2)}, u32[]{:S(2)}) %collective-permute-start.15) | collective-permute-done | bytes 327712 | tf_op jit(solution)/shard_map/ppermute | solution.py:20
  160.4 7.9 %collective-permute-done.14 = f32[4,16,1280]{2,1,0:T(8,128)} collective-permute-done((f32[4,16,1280]{2,1,0:T(8,128)}, f32[4,16,1280]{2,1,0:T(8,128)}, u32[]{:S(2)}, u32[]{:S(2)}) %collective-permute-start.14) | collective-permute-done | bytes 327712 | tf_op jit(solution)/shard_map/ppermute | solution.py:20
  170.9 2.9 %maximum_select_fusion = f32[16,2,32,1024]{3,2,1,0:T(8,128)S(1)} fusion(f32[16,1,32,1024]{3,2,1,0:T(8,128)} %bitcast.10, f32[16,1,32,1024]{3,2,1,0:T(8,128)S(1)} %bitcast.76, pred[]{:T(512)S(6)} %eq.15), kind=kLoop, calls=%fused_computation | loop fusion | flops 3145728 | bytes 8388609 | tf_op jit(solution)/shard_map/jit(_where)/select_n | solution.py:104
  173.8 2.3 fusion.36
  178.3 4.3 %collective-permute-start.17 = (f32[256,1024]{1,0:T(8,128)S(1)}, f32[256,1024]{1,0:T(8,128)S(1)}, u32[]{:S(2)}, u32[]{:S(2)}) collective-permute-start(f32[256,1024]{1,0:T(8,128)S(1)} %maximum_select_fusion.4), channel_id=1, source_target_pairs={{0,16},{16,0},{1,17},{17,1},{2,18},{18,2},{3,19},{19,3},{4,20},{20... | collective-permute-start | bytes 3145736 | tf_op jit(solution)/shard_map/ppermute | solution.py:24
  182.6 2.2 fusion.7
  184.8 4.0 %fusion = f32[384,1024]{1,0:T(8,128)} fusion(f32[1024,1024]{1,0:T(8,128)S(1)} %bitcast.69, f32[128,1024]{1,0:T(8,128)S(1)} %collective-permute-done.8, f32[128,1024]{1,0:T(8,128)S(1)} %bitcast.75, f32[128,1024]{1,0:T(8,128)S(1)} %collective-permute-done.9), kind=kOutput, calls=%fused_computation.3 | convolution fusion | flops 2416705536 | bytes 7340032 | tf_op jit(solution)/shard_map/dot_general | solution.py:13
  188.8 15.5 %collective-permute-done.17 = f32[256,1024]{1,0:T(8,128)S(1)} collective-permute-done((f32[256,1024]{1,0:T(8,128)S(1)}, f32[256,1024]{1,0:T(8,128)S(1)}, u32[]{:S(2)}, u32[]{:S(2)}) %collective-permute-start.17) | collective-permute-done | bytes 1048608 | tf_op jit(solution)/shard_map/ppermute | solution.py:24
  205.6 2.4 %fusion.38 = f32[256,384]{1,0:T(8,128)S(1)} fusion(f32[256,1024]{1,0:T(8,128)S(1)} %multiply_subtract_fusion, f32[384,1024]{1,0:T(8,128)} %fusion), kind=kOutput, calls=%fused_computation.74 | convolution fusion | flops 603979776 | bytes 3014656 | tf_op jit(solution)/shard_map/dot_general | solution.py:13
  209.2 9.8 %all-to-all-start = ((f32[32,8,640]{2,1,0:T(8,128)}), f32[32,8,640]{2,1,0:T(8,128)S(1)}, u32[]{:S(2)}, u32[]{:S(2)}) async-start(f32[32,8,640]{2,1,0:T(8,128)} %maximum_bitcast_fusion), calls=%async_computation | async-start | bytes 1310720 | tf_op jit(solution)/shard_map/all_to_all | solution.py:144
  219.1 12.8 %all-to-all-done = f32[32,8,640]{2,1,0:T(8,128)S(1)} async-done(((f32[32,8,640]{2,1,0:T(8,128)}), f32[32,8,640]{2,1,0:T(8,128)S(1)}, u32[]{:S(2)}, u32[]{:S(2)}) %all-to-all-start) | async-done | bytes 655392 | tf_op jit(solution)/shard_map/all_to_all | solution.py:144
  (68 shorter events, 26.7 us)
Async XLA Ops:
  6.5 98.1 %all-gather.2.cloned.1.call-start = ((), (), s32[]{:S(2)}) async-start(), calls=%async_computation.1 | async-start | bytes 2228224 | tf_op jit(solution)/shard_map/all_gather | solution.py:84
  9.1 14.0 %collective-permute-start = (f32[128,1024]{1,0:T(8,128)S(1)}, f32[128,1024]{1,0:T(8,128)S(1)}, u32[]{:S(2)}, u32[]{:S(2)}) collective-permute-start(f32[128,1024]{1,0:T(8,128)S(1)} %bitcast_multiply_fusion), channel_id=1, source_target_pairs={{0,16},{16,0},{1,17},{17,1},{2,18},{18,2},{3,19},{19,3},{4,20},{20... | collective-permute-start | bytes 1572872 | tf_op jit(solution)/shard_map/ppermute | solution.py:24
  25.3 54.8 %copy-start.1 = (f32[128,1,1024]{2,1,0:T(1,128)S(1)}, f32[128,1,1024]{2,1,0:T(1,128)}, u32[]{:S(2)}) copy-start(f32[128,1,1024]{2,1,0:T(1,128)} %param.5) | copy-start | bytes 1572868
  25.3 35.4 %collective-permute-start.2 = (f32[4,16,1280]{2,1,0:T(8,128)}, f32[4,16,1280]{2,1,0:T(8,128)S(1)}, u32[]{:S(2)}, u32[]{:S(2)}) collective-permute-start(f32[4,16,1280]{2,1,0:T(8,128)} %get-tuple-element.19), channel_id=1, source_target_pairs={{0,480},{32,0},{64,32},{96,64},{128,96},{160,128},{192,160},{224,1... | collective-permute-start | bytes 983048 | tf_op jit(solution)/shard_map/ppermute | solution.py:20
  39.6 21.1 %collective-permute-start.1 = (f32[4,16,1280]{2,1,0:T(8,128)S(1)}, f32[4,16,1280]{2,1,0:T(8,128)}, u32[]{:S(2)}, u32[]{:S(2)}) collective-permute-start(f32[4,16,1280]{2,1,0:T(8,128)S(1)} %get-tuple-element.17), channel_id=1, source_target_pairs={{0,32},{32,64},{64,96},{96,128},{128,160},{160,192},{192,224},{224... | collective-permute-start | bytes 983048 | tf_op jit(solution)/shard_map/ppermute | solution.py:20
  42.3 16.9 %collective-permute-start.4 = (f32[4,8,1280]{2,1,0:T(8,128)}, f32[4,8,1280]{2,1,0:T(8,128)}, u32[]{:S(2)}, u32[]{:S(2)}) collective-permute-start(f32[4,8,1280]{2,1,0:T(8,128)} %get-tuple-element.28), channel_id=1, source_target_pairs={{0,448},{32,480},{64,0},{96,32},{128,64},{160,96},{192,128},{224,1... | collective-permute-start | bytes 491528 | tf_op jit(solution)/shard_map/ppermute | solution.py:20
  46.1 14.6 %collective-permute-start.3 = (f32[4,8,1280]{2,1,0:T(8,128)}, f32[4,8,1280]{2,1,0:T(8,128)}, u32[]{:S(2)}, u32[]{:S(2)}) collective-permute-start(f32[4,8,1280]{2,1,0:T(8,128)} %get-tuple-element.27), channel_id=1, source_target_pairs={{0,64},{32,96},{64,128},{96,160},{128,192},{160,224},{192,256},{22... | collective-permute-start | bytes 491528 | tf_op jit(solution)/shard_map/ppermute | solution.py:20
  62.0 25.0 %collective-permute-start.7 = (f32[16,1280]{1,0:T(8,128)S(1)}, f32[16,1280]{1,0:T(8,128)S(1)}, u32[]{:S(2)}, u32[]{:S(2)}) collective-permute-start(f32[16,1280]{1,0:T(8,128)S(1)} %get-tuple-element.25), channel_id=1, source_target_pairs={{0,256},{32,288},{64,320},{96,352},{128,384},{160,416},{192,448},{... | collective-permute-start | bytes 245768 | tf_op jit(solution)/shard_map/ppermute | solution.py:20
  70.9 19.0 %collective-permute-start.6 = (f32[16,1280]{1,0:T(8,128)S(1)}, f32[16,1280]{1,0:T(8,128)S(1)}, u32[]{:S(2)}, u32[]{:S(2)}) collective-permute-start(f32[16,1280]{1,0:T(8,128)S(1)} %get-tuple-element.26), channel_id=1, source_target_pairs={{0,384},{32,416},{64,448},{96,480},{128,0},{160,32},{192,64},{224,... | collective-permute-start | bytes 245768 | tf_op jit(solution)/shard_map/ppermute | solution.py:20
  72.8 17.1 %collective-permute-start.5 = (f32[16,1280]{1,0:T(8,128)S(1)}, f32[16,1280]{1,0:T(8,128)S(1)}, u32[]{:S(2)}, u32[]{:S(2)}) collective-permute-start(f32[16,1280]{1,0:T(8,128)S(1)} %get-tuple-element.24), channel_id=1, source_target_pairs={{0,128},{32,160},{64,192},{96,224},{128,256},{160,288},{192,320},{... | collective-permute-start | bytes 245768 | tf_op jit(solution)/shard_map/ppermute | solution.py:20
  80.2 24.4 %collective-permute-start.8 = (f32[128,1024]{1,0:T(8,128)S(1)}, f32[128,1024]{1,0:T(8,128)S(1)}, u32[]{:S(2)}, u32[]{:S(2)}) collective-permute-start(f32[128,1024]{1,0:T(8,128)S(1)} %bitcast.73), channel_id=1, source_target_pairs={{0,480},{32,0},{64,32},{96,64},{128,96},{160,128},{192,160},{224,1... | collective-permute-start | bytes 1572872 | tf_op jit(solution)/shard_map/ppermute | solution.py:20
  82.6 22.1 %collective-permute-start.9 = (f32[128,1024]{1,0:T(8,128)S(1)}, f32[128,1024]{1,0:T(8,128)S(1)}, u32[]{:S(2)}, u32[]{:S(2)}) collective-permute-start(f32[128,1024]{1,0:T(8,128)S(1)} %bitcast.74), channel_id=1, source_target_pairs={{0,32},{32,64},{64,96},{96,128},{128,160},{160,192},{192,224},{224... | collective-permute-start | bytes 1572872 | tf_op jit(solution)/shard_map/ppermute | solution.py:20
  104.6 65.1 %collective-permute-start.10 = (f32[16,32,1024]{2,1,0:T(8,128)}, f32[16,32,1024]{2,1,0:T(8,128)}, u32[]{:S(2)}, u32[]{:S(2)}) collective-permute-start(f32[16,32,1024]{2,1,0:T(8,128)} %all-gather.2.cloned.1.call-done), channel_id=1, source_target_pairs={{0,16},{16,0},{1,17},{17,1},{2,18},{18,2},{3,19},{19,3},{4,20},{20... | collective-permute-start | bytes 6291464 | tf_op jit(solution)/shard_map/ppermute | solution.py:24
  110.3 15.1 %collective-permute-start.13 = (f32[16,1280]{1,0:T(8,128)S(1)}, f32[16,1280]{1,0:T(8,128)S(1)}, u32[]{:S(2)}, u32[]{:S(2)}) collective-permute-start(f32[16,1280]{1,0:T(8,128)S(1)} %fusion.29), channel_id=1, source_target_pairs={{0,128},{32,160},{64,192},{96,224},{128,256},{160,288},{192,320},{... | collective-permute-start | bytes 245768 | tf_op jit(solution)/shard_map/ppermute | solution.py:20
  113.4 14.8 %collective-permute-start.12 = (f32[16,1280]{1,0:T(8,128)S(1)}, f32[16,1280]{1,0:T(8,128)S(1)}, u32[]{:S(2)}, u32[]{:S(2)}) collective-permute-start(f32[16,1280]{1,0:T(8,128)S(1)} %fusion.29), channel_id=1, source_target_pairs={{0,256},{32,288},{64,320},{96,352},{128,384},{160,416},{192,448},{... | collective-permute-start | bytes 245768 | tf_op jit(solution)/shard_map/ppermute | solution.py:20
  120.6 18.7 %collective-permute-start.11 = (f32[16,1280]{1,0:T(8,128)S(1)}, f32[16,1280]{1,0:T(8,128)S(1)}, u32[]{:S(2)}, u32[]{:S(2)}) collective-permute-start(f32[16,1280]{1,0:T(8,128)S(1)} %fusion.29), channel_id=1, source_target_pairs={{0,384},{32,416},{64,448},{96,480},{128,0},{160,32},{192,64},{224,... | collective-permute-start | bytes 245768 | tf_op jit(solution)/shard_map/ppermute | solution.py:20
  140.2 12.2 %collective-permute-start.16 = (f32[4,16,1280]{2,1,0:T(8,128)}, f32[4,16,1280]{2,1,0:T(8,128)}, u32[]{:S(2)}, u32[]{:S(2)}) collective-permute-start(f32[4,16,1280]{2,1,0:T(8,128)} %get-tuple-element.23), channel_id=1, source_target_pairs={{0,32},{32,64},{64,96},{96,128},{128,160},{160,192},{192,224},{224... | collective-permute-start | bytes 983048 | tf_op jit(solution)/shard_map/ppermute | solution.py:20
  142.1 18.3 %collective-permute-start.15 = (f32[4,16,1280]{2,1,0:T(8,128)}, f32[4,16,1280]{2,1,0:T(8,128)S(1)}, u32[]{:S(2)}, u32[]{:S(2)}) collective-permute-start(f32[4,16,1280]{2,1,0:T(8,128)} %get-tuple-element.23), channel_id=1, source_target_pairs={{0,448},{32,480},{64,0},{96,32},{128,64},{160,96},{192,128},{224,1... | collective-permute-start | bytes 983048 | tf_op jit(solution)/shard_map/ppermute | solution.py:20
  147.1 21.2 %collective-permute-start.14 = (f32[4,16,1280]{2,1,0:T(8,128)}, f32[4,16,1280]{2,1,0:T(8,128)}, u32[]{:S(2)}, u32[]{:S(2)}) collective-permute-start(f32[4,16,1280]{2,1,0:T(8,128)} %get-tuple-element.23), channel_id=1, source_target_pairs={{0,480},{32,0},{64,32},{96,64},{128,96},{160,128},{192,160},{224,1... | collective-permute-start | bytes 983048 | tf_op jit(solution)/shard_map/ppermute | solution.py:20
  150.4 32.2 %collective-permute-start.19 = (f32[128,1024]{1,0:T(8,128)S(1)}, f32[128,1024]{1,0:T(8,128)S(1)}, u32[]{:S(2)}, u32[]{:S(2)}) collective-permute-start(f32[128,1024]{1,0:T(8,128)S(1)} %collective-permute-done.8), channel_id=1, source_target_pairs={{0,480},{32,0},{64,32},{96,64},{128,96},{160,128},{192,160},{224,1... | collective-permute-start | bytes 1572872 | tf_op jit(solution)/shard_map/ppermute | solution.py:20
  152.4 30.2 %collective-permute-start.18 = (f32[128,1024]{1,0:T(8,128)S(1)}, f32[128,1024]{1,0:T(8,128)S(1)}, u32[]{:S(2)}, u32[]{:S(2)}) collective-permute-start(f32[128,1024]{1,0:T(8,128)S(1)} %collective-permute-done.9), channel_id=1, source_target_pairs={{0,32},{32,64},{64,96},{96,128},{128,160},{160,192},{192,224},{224... | collective-permute-start | bytes 1572872 | tf_op jit(solution)/shard_map/ppermute | solution.py:20
  169.3 1.6 copy-start
  178.3 26.0 %collective-permute-start.17 = (f32[256,1024]{1,0:T(8,128)S(1)}, f32[256,1024]{1,0:T(8,128)S(1)}, u32[]{:S(2)}, u32[]{:S(2)}) collective-permute-start(f32[256,1024]{1,0:T(8,128)S(1)} %maximum_select_fusion.4), channel_id=1, source_target_pairs={{0,16},{16,0},{1,17},{17,1},{2,18},{18,2},{3,19},{19,3},{4,20},{20... | collective-permute-start | bytes 3145736 | tf_op jit(solution)/shard_map/ppermute | solution.py:24
  209.2 22.7 %all-to-all-start = ((f32[32,8,640]{2,1,0:T(8,128)}), f32[32,8,640]{2,1,0:T(8,128)S(1)}, u32[]{:S(2)}, u32[]{:S(2)}) async-start(f32[32,8,640]{2,1,0:T(8,128)} %maximum_bitcast_fusion), calls=%async_computation | async-start | bytes 1310720 | tf_op jit(solution)/shard_map/all_to_all | solution.py:144
Sparse Core Ops, SparseCore 0:
  9.4 87.2 all-gather.1

commit v6 on v4

--- a/solution.py
+++ b/solution.py
@@ -61,11 +61,13 @@
         parts,
         shift_z(parts, -1),
         shift_z(parts, 1),
-        shift_z(parts, -2),
+        shift_z(parts[:, :8], -2),
+        shift_z(parts[:, 8:], 2),
     )
 
 
-def joined(parts, plus1, minus1, two):
+def joined(parts, plus1, minus1, plus2, minus2):
+    two = jnp.concatenate([plus2, jnp.roll(minus2, -1, axis=0)], axis=1)
     three = jnp.roll(minus1, -1, axis=0)
     return jnp.stack([parts, plus1, two, three], axis=1)
 
@@ -96,7 +98,6 @@
     partial = jnp.concatenate([strip0, strip2], axis=1)
     blocks = partial.reshape(4, 4, quarter // 16, 5 * quarter)
     near_sums, plus1, minus1 = lax.optimization_barrier((reduce_near(blocks, place), plus1, minus1))
-    plus2, minus2 = shift_z(plus1, -1), shift_z(minus1, 1)
     part, own_inverse = lax.optimization_barrier((reduce_far(near_sums, place), own_inverse))
     other_inverse = swap_y(own_inverse)
     pieces = gather_near(gather_far(part))
@@ -106,6 +107,7 @@
         jnp.stack([other_inverse, own_inverse], axis=1),
     ).reshape(width, width)
     side = dot(pair_train, inverse, ((1,), (0,)))
+    pieces, side = lax.optimization_barrier((pieces, side))
 
     gathered = joined(*pieces).reshape(quarter, 5 * quarter)
     strips = jnp.roll(gathered, place * (quarter // 16), axis=0)
@@ -127,6 +129,8 @@
     )
     product = jnp.where(first_half, product, jnp.roll(product, quarter, axis=1))
     other_product = swap_y(product)
+    plus1, minus1, product = lax.optimization_barrier((plus1, minus1, product))
+    plus2, minus2 = shift_z(plus1, -1), shift_z(minus1, 1)
     queries = jnp.concatenate([minus1, query, plus1]), jnp.concatenate([minus2, plus2])
     first = [dot(piece, inverse, ((1,), (1,))) for piece in queries]
     left = 2.0 * pair_train - DAMPING * side - (product + other_product) * (1.0 / total_rows)

time: 226 us -> 217 us (0.960)
  waiting for transfers between devices: 73.1 us -> 58.7 us
  starting transfers between devices: 107 us -> 114 us
  matrix products: 15.2 us -> 12.8 us
    ppermute x17 -> x18, starting transfers between devices: 72.2 us -> 91.7 us  [shift_z(): lax.ppermute(value, 'z', [(i, (i + steps) % count) for i in range(count)])]
    all_to_all x1, starting transfers between devices: 22.6 us -> 12.2 us  [on_device(): lax.all_to_all(jnp.concatenate([upper, lower]), ('yh', 'yl', 'x', 'c'), 0...]
    ppermute x17 -> x18, waiting for transfers between devices: 51.7 us -> 42.3 us  [shift_z(): lax.ppermute(value, 'z', [(i, (i + steps) % count) for i in range(count)])]
    ppermute x3, waiting for transfers between devices: 7.91 us -> 2.84 us  [swap_y(): return lax.ppermute(value, 'yh', [(0, 1), (1, 0)])]
    ppermute x3, starting transfers between devices: 12.7 us -> 9.78 us  [swap_y(): return lax.ppermute(value, 'yh', [(0, 1), (1, 0)])]
    dot_general x11, matrix products: 15.2 us -> 12.8 us  [dot(): lax.dot_general(left, right, (dims, ((), ())), precision=FAST, preferred_...]
  transfers between devices with their start and end apart: 22 -> 23, of which waited for: 12 -> 11; matrix products, arithmetic and copies ran while one was open for 10% -> 9% of each run, Pallas kernels for 0% -> 0%
where the time goes in v6:
time: 217 us; the launch traced here: 214 us
  starting transfers between devices  114 us (53%)
  waiting for transfers between devices  58.7 us (27%)
  between operations  14.2 us (7%)
  matrix products  12.8 us (6%)
  other arithmetic  10.8 us (5%)
  local copies, waits for them, and re-layouts  4.19 us (2%)
    ppermute x18, starting transfers between devices, shift_z(): lax.ppermute(value, 'z', [(i, (i + steps) % count) for i in range(count)])  91.7 us
    ppermute x18, waiting for transfers between devices, shift_z(): lax.ppermute(value, 'z', [(i, (i + steps) % count) for i in range(count)])  42.3 us
    all_to_all x1, waiting for transfers between devices, on_device(): lax.all_to_all(jnp.concatenate([upper, lower]), ('yh', 'yl', 'x', 'c'), 0...  12.8 us
    dot_general x11, matrix products, dot(): lax.dot_general(left, right, (dims, ((), ())), precision=FAST, preferred_...  12.8 us
    all_to_all x1, starting transfers between devices, on_device(): lax.all_to_all(jnp.concatenate([upper, lower]), ('yh', 'yl', 'x', 'c'), 0...  12.2 us
    ppermute x3, starting transfers between devices, swap_y(): return lax.ppermute(value, 'yh', [(0, 1), (1, 0)])  9.78 us
    select_n x1, other arithmetic, on_device(): jnp.where(first_half, jnp.stack([own_inverse, other_inverse], axis=1), jn...  4.39 us
  transfers between devices with their start and end apart: 23, of which 11 were waited for; matrix products, arithmetic and copies ran while one was open for 9% of the time, Pallas kernels for 0%

profile of v6, /device:TPU:1, one launch (start us, length us, event | category | flops | bytes accessed | tf_op | source)
XLA Modules:
  0.0 214.2 jit_solution(10789971567826537064)
XLA Ops:
  9.1 5.7 %collective-permute-start = (f32[128,1024]{1,0:T(8,128)S(1)}, f32[128,1024]{1,0:T(8,128)S(1)}, u32[]{:S(2)}, u32[]{:S(2)}) collective-permute-start(f32[128,1024]{1,0:T(8,128)S(1)} %bitcast_multiply_fusion), channel_id=1, source_target_pairs={{0,16},{16,0},{1,17},{17,1},{2,18},{18,2},{3,19},{19,3},{4,20},{20... | collective-permute-start | bytes 1572872 | tf_op jit(solution)/shard_map/ppermute | solution.py:24
  15.9 11.1 %collective-permute-start.1 = (f32[128,1024]{1,0:T(8,128)S(1)}, f32[128,1024]{1,0:T(8,128)S(1)}, u32[]{:S(2)}, u32[]{:S(2)}) collective-permute-start(f32[128,1024]{1,0:T(8,128)S(1)} %bitcast.74), channel_id=1, source_target_pairs={{0,480},{32,0},{64,32},{96,64},{128,96},{160,128},{192,160},{224,1... | collective-permute-start | bytes 1572872 | tf_op jit(solution)/shard_map/ppermute | solution.py:20
  27.1 1.9 collective-permute-start.2
  29.0 10.5 %collective-permute-done.1 = f32[128,1024]{1,0:T(8,128)S(1)} collective-permute-done((f32[128,1024]{1,0:T(8,128)S(1)}, f32[128,1024]{1,0:T(8,128)S(1)}, u32[]{:S(2)}, u32[]{:S(2)}) %collective-permute-start.1) | collective-permute-done | bytes 524320 | tf_op jit(solution)/shard_map/ppermute | solution.py:20
  40.4 6.4 %collective-permute-done.2 = f32[128,1024]{1,0:T(8,128)} collective-permute-done((f32[128,1024]{1,0:T(8,128)S(1)}, f32[128,1024]{1,0:T(8,128)}, u32[]{:S(2)}, u32[]{:S(2)}) %collective-permute-start.2) | collective-permute-done | bytes 524320 | tf_op jit(solution)/shard_map/ppermute | solution.py:20
  51.0 4.6 %collective-permute-start.4 = (f32[4,16,1280]{2,1,0:T(8,128)S(1)}, f32[4,16,1280]{2,1,0:T(8,128)}, u32[]{:S(2)}, u32[]{:S(2)}) collective-permute-start(f32[4,16,1280]{2,1,0:T(8,128)S(1)} %get-tuple-element.45), channel_id=1, source_target_pairs={{0,480},{32,0},{64,32},{96,64},{128,96},{160,128},{192,160},{224,1... | collective-permute-start | bytes 983048 | tf_op jit(solution)/shard_map/ppermute | solution.py:20
  58.2 5.5 %collective-permute-start.6 = (f32[4,8,1280]{2,1,0:T(8,128)}, f32[4,8,1280]{2,1,0:T(8,128)}, u32[]{:S(2)}, u32[]{:S(2)}) collective-permute-start(f32[4,8,1280]{2,1,0:T(8,128)} %get-tuple-element.54), channel_id=1, source_target_pairs={{0,448},{32,480},{64,0},{96,32},{128,64},{160,96},{192,128},{224,1... | collective-permute-start | bytes 491528 | tf_op jit(solution)/shard_map/ppermute | solution.py:20
  63.8 8.4 %collective-permute-done.5 = f32[4,8,1280]{2,1,0:T(8,128)} collective-permute-done((f32[4,8,1280]{2,1,0:T(8,128)}, f32[4,8,1280]{2,1,0:T(8,128)}, u32[]{:S(2)}, u32[]{:S(2)}) %collective-permute-start.5) | collective-permute-done | bytes 163872 | tf_op jit(solution)/shard_map/ppermute | solution.py:20
  74.2 1.9 collective-permute-start.7
  76.1 7.3 %collective-permute-start.8 = (f32[16,1280]{1,0:T(8,128)S(1)}, f32[16,1280]{1,0:T(8,128)S(1)}, u32[]{:S(2)}, u32[]{:S(2)}) collective-permute-start(f32[16,1280]{1,0:T(8,128)S(1)} %get-tuple-element.52), channel_id=1, source_target_pairs={{0,384},{32,416},{64,448},{96,480},{128,0},{160,32},{192,64},{224,... | collective-permute-start | bytes 245768 | tf_op jit(solution)/shard_map/ppermute | solution.py:20
  83.4 6.4 %collective-permute-start.9 = (f32[16,1280]{1,0:T(8,128)S(1)}, f32[16,1280]{1,0:T(8,128)S(1)}, u32[]{:S(2)}, u32[]{:S(2)}) collective-permute-start(f32[16,1280]{1,0:T(8,128)S(1)} %get-tuple-element.51), channel_id=1, source_target_pairs={{0,256},{32,288},{64,320},{96,352},{128,384},{160,416},{192,448},{... | collective-permute-start | bytes 245768 | tf_op jit(solution)/shard_map/ppermute | solution.py:20
  89.9 7.6 %collective-permute-done.9 = f32[16,1280]{1,0:T(8,128)S(1)} collective-permute-done((f32[16,1280]{1,0:T(8,128)S(1)}, f32[16,1280]{1,0:T(8,128)S(1)}, u32[]{:S(2)}, u32[]{:S(2)}) %collective-permute-start.9) | collective-permute-done | bytes 81952 | tf_op jit(solution)/shard_map/ppermute | solution.py:20
  97.5 1.9 collective-permute-start.17
  99.5 4.9 %collective-permute-start.10 = (f32[16,1280]{1,0:T(8,128)S(1)}, f32[16,1280]{1,0:T(8,128)S(1)}, u32[]{:S(2)}, u32[]{:S(2)}) collective-permute-start(f32[16,1280]{1,0:T(8,128)S(1)} %fusion.29), channel_id=1, source_target_pairs={{0,384},{32,416},{64,448},{96,480},{128,0},{160,32},{192,64},{224,... | collective-permute-start | bytes 245768 | tf_op jit(solution)/shard_map/ppermute | solution.py:20
  104.4 6.5 %collective-permute-start.11 = (f32[16,1280]{1,0:T(8,128)S(1)}, f32[16,1280]{1,0:T(8,128)S(1)}, u32[]{:S(2)}, u32[]{:S(2)}) collective-permute-start(f32[16,1280]{1,0:T(8,128)S(1)} %fusion.29), channel_id=1, source_target_pairs={{0,256},{32,288},{64,320},{96,352},{128,384},{160,416},{192,448},{... | collective-permute-start | bytes 245768 | tf_op jit(solution)/shard_map/ppermute | solution.py:20
  110.9 6.1 %collective-permute-start.12 = (f32[16,1280]{1,0:T(8,128)S(1)}, f32[16,1280]{1,0:T(8,128)S(1)}, u32[]{:S(2)}, u32[]{:S(2)}) collective-permute-start(f32[16,1280]{1,0:T(8,128)S(1)} %fusion.29), channel_id=1, source_target_pairs={{0,128},{32,160},{64,192},{96,224},{128,256},{160,288},{192,320},{... | collective-permute-start | bytes 245768 | tf_op jit(solution)/shard_map/ppermute | solution.py:20
  118.3 2.2 %collective-permute-done.12 = f32[16,1280]{1,0:T(8,128)S(1)} collective-permute-done((f32[16,1280]{1,0:T(8,128)S(1)}, f32[16,1280]{1,0:T(8,128)S(1)}, u32[]{:S(2)}, u32[]{:S(2)}) %collective-permute-start.12) | collective-permute-done | bytes 81952 | tf_op jit(solution)/shard_map/ppermute | solution.py:20
  120.5 6.8 %collective-permute-start.13 = (f32[4,16,1280]{2,1,0:T(8,128)S(1)}, f32[4,16,1280]{2,1,0:T(8,128)S(1)}, u32[]{:S(2)}, u32[]{:S(2)}) collective-permute-start(f32[4,16,1280]{2,1,0:T(8,128)S(1)} %pad_maximum_fusion.2), channel_id=1, source_target_pairs={{0,480},{32,0},{64,32},{96,64},{128,96},{160,128},{192,160},{224,1... | collective-permute-start | bytes 983048 | tf_op jit(solution)/shard_map/ppermute | solution.py:20
  127.3 5.6 %collective-permute-start.14 = (f32[4,16,1280]{2,1,0:T(8,128)S(1)}, f32[4,16,1280]{2,1,0:T(8,128)S(1)}, u32[]{:S(2)}, u32[]{:S(2)}) collective-permute-start(f32[4,16,1280]{2,1,0:T(8,128)S(1)} %pad_maximum_fusion.2), channel_id=1, source_target_pairs={{0,32},{32,64},{64,96},{96,128},{128,160},{160,192},{192,224},{224... | collective-permute-start | bytes 983048 | tf_op jit(solution)/shard_map/ppermute | solution.py:20
  132.9 2.2 %collective-permute-start.15 = (f32[4,8,1280]{2,1,0:T(8,128)S(1)}, f32[4,8,1280]{2,1,0:T(8,128)S(1)}, u32[]{:S(2)}, u32[]{:S(2)}) collective-permute-start(f32[4,8,1280]{2,1,0:T(8,128)S(1)} %get-tuple-element.49), channel_id=1, source_target_pairs={{0,448},{32,480},{64,0},{96,32},{128,64},{160,96},{192,128},{224,1... | collective-permute-start | bytes 491528 | tf_op jit(solution)/shard_map/ppermute | solution.py:20
  135.1 3.9 %collective-permute-start.16 = (f32[4,8,1280]{2,1,0:T(8,128)S(1)}, f32[4,8,1280]{2,1,0:T(8,128)S(1)}, u32[]{:S(2)}, u32[]{:S(2)}) collective-permute-start(f32[4,8,1280]{2,1,0:T(8,128)S(1)} %get-tuple-element.48), channel_id=1, source_target_pairs={{0,64},{32,96},{64,128},{96,160},{128,192},{160,224},{192,256},{22... | collective-permute-start | bytes 491528 | tf_op jit(solution)/shard_map/ppermute | solution.py:20
  139.1 2.8 %collective-permute-done.17 = f32[16,32,1024]{2,1,0:T(8,128)} collective-permute-done((f32[16,32,1024]{2,1,0:T(8,128)}, f32[16,32,1024]{2,1,0:T(8,128)}, u32[]{:S(2)}, u32[]{:S(2)}) %collective-permute-start.17) | collective-permute-done | bytes 2097184 | tf_op jit(solution)/shard_map/ppermute | solution.py:24
  141.9 4.4 %maximum_select_fusion = f32[16,2,32,1024]{3,2,1,0:T(8,128)S(1)} fusion(f32[16,1,32,1024]{3,2,1,0:T(8,128)} %bitcast.14, f32[16,1,32,1024]{3,2,1,0:T(8,128)} %bitcast.77, pred[]{:T(512)S(6)} %eq.15), kind=kLoop, calls=%fused_computation | loop fusion | flops 3145728 | bytes 8388609 | tf_op jit(solution)/shard_map/jit(_where)/select_n | solution.py:104
  146.3 2.3 %fusion.36 = f32[256,1024]{1,0:T(8,128)S(1)} fusion(f32[256,1024]{1,0:T(8,128)S(1)} %maximum_select_fusion.1, f32[1024,1024]{1,0:T(8,128)S(1)} %bitcast.67), kind=kOutput, calls=%fused_computation.73 | convolution fusion | flops 1610612736 | bytes 6291456 | tf_op jit(solution)/shard_map/dot_general | solution.py:13
  151.4 2.2 %collective-permute-start.18 = (f32[256,1024]{1,0:T(8,128)S(1)}, f32[256,1024]{1,0:T(8,128)S(1)}, u32[]{:S(2)}, u32[]{:S(2)}) collective-permute-start(f32[256,1024]{1,0:T(8,128)S(1)} %maximum_select_fusion.4), channel_id=1, source_target_pairs={{0,16},{16,0},{1,17},{17,1},{2,18},{18,2},{3,19},{19,3},{4,20},{20... | collective-permute-start | bytes 3145736 | tf_op jit(solution)/shard_map/ppermute | solution.py:24
  153.6 11.0 %collective-permute-start.19 = (f32[128,1024]{1,0:T(8,128)}, f32[128,1024]{1,0:T(8,128)S(1)}, u32[]{:S(2)}, u32[]{:S(2)}) collective-permute-start(f32[128,1024]{1,0:T(8,128)} %collective-permute-done.2), channel_id=1, source_target_pairs={{0,32},{32,64},{64,96},{96,128},{128,160},{160,192},{192,224},{224... | collective-permute-start | bytes 1572872 | tf_op jit(solution)/shard_map/ppermute | solution.py:20
  164.6 2.1 collective-permute-start.20
  166.7 3.9 %fusion = f32[384,1024]{1,0:T(8,128)S(1)} fusion(f32[1024,1024]{1,0:T(8,128)S(1)} %bitcast.68, f32[128,1024]{1,0:T(8,128)S(1)} %copy-done.1, f32[128,1024]{1,0:T(8,128)S(1)} %bitcast.76, f32[128,1024]{1,0:T(8,128)} %collective-permute-done.2), kind=kOutput, calls=%fused_computation.3 | convolution fusion | flops 2416705536 | bytes 7340032 | tf_op jit(solution)/shard_map/dot_general | solution.py:13
  172.2 3.5 %collective-permute-done.20 = f32[128,1024]{1,0:T(8,128)S(1)} collective-permute-done((f32[128,1024]{1,0:T(8,128)S(1)}, f32[128,1024]{1,0:T(8,128)S(1)}, u32[]{:S(2)}, u32[]{:S(2)}) %collective-permute-start.20) | collective-permute-done | bytes 524320 | tf_op jit(solution)/shard_map/ppermute | solution.py:20
  175.8 2.2 %fusion.7 = f32[256,1024]{1,0:T(8,128)S(1)} fusion(f32[1024,1024]{1,0:T(8,128)S(1)} %bitcast.69, f32[128,1024]{1,0:T(8,128)S(1)} %collective-permute-done.20, f32[128,1024]{1,0:T(8,128)S(1)} %collective-permute-done.19), kind=kOutput, calls=%fused_computation.18 | convolution fusion | flops 1610874880 | bytes 6291456 | tf_op jit(solution)/shard_map/dot_general | solution.py:13
  181.6 12.2 %all-to-all-start = ((f32[32,8,640]{2,1,0:T(8,128)}), f32[32,8,640]{2,1,0:T(8,128)S(1)}, u32[]{:S(2)}, u32[]{:S(2)}) async-start(f32[32,8,640]{2,1,0:T(8,128)} %maximum_bitcast_fusion), calls=%async_computation | async-start | bytes 1310720 | tf_op jit(solution)/shard_map/all_to_all | solution.py:147
  193.8 12.8 %all-to-all-done = f32[32,8,640]{2,1,0:T(8,128)S(1)} async-done(((f32[32,8,640]{2,1,0:T(8,128)}), f32[32,8,640]{2,1,0:T(8,128)S(1)}, u32[]{:S(2)}, u32[]{:S(2)}) %all-to-all-start) | async-done | bytes 655392 | tf_op jit(solution)/shard_map/all_to_all | solution.py:147
  (74 shorter events, 23.2 us)
Async XLA Ops:
  6.5 91.0 %all-gather.2.cloned.1.call-start = ((), (), s32[]{:S(2)}) async-start(), calls=%async_computation.1 | async-start | bytes 2228224 | tf_op jit(solution)/shard_map/all_gather | solution.py:86
  9.1 19.9 %collective-permute-start = (f32[128,1024]{1,0:T(8,128)S(1)}, f32[128,1024]{1,0:T(8,128)S(1)}, u32[]{:S(2)}, u32[]{:S(2)}) collective-permute-start(f32[128,1024]{1,0:T(8,128)S(1)} %bitcast_multiply_fusion), channel_id=1, source_target_pairs={{0,16},{16,0},{1,17},{17,1},{2,18},{18,2},{3,19},{19,3},{4,20},{20... | collective-permute-start | bytes 1572872 | tf_op jit(solution)/shard_map/ppermute | solution.py:24
  15.9 23.7 %collective-permute-start.1 = (f32[128,1024]{1,0:T(8,128)S(1)}, f32[128,1024]{1,0:T(8,128)S(1)}, u32[]{:S(2)}, u32[]{:S(2)}) collective-permute-start(f32[128,1024]{1,0:T(8,128)S(1)} %bitcast.74), channel_id=1, source_target_pairs={{0,480},{32,0},{64,32},{96,64},{128,96},{160,128},{192,160},{224,1... | collective-permute-start | bytes 1572872 | tf_op jit(solution)/shard_map/ppermute | solution.py:20
  27.1 19.8 %collective-permute-start.2 = (f32[128,1024]{1,0:T(8,128)S(1)}, f32[128,1024]{1,0:T(8,128)}, u32[]{:S(2)}, u32[]{:S(2)}) collective-permute-start(f32[128,1024]{1,0:T(8,128)S(1)} %bitcast.75), channel_id=1, source_target_pairs={{0,32},{32,64},{64,96},{96,128},{128,160},{160,192},{192,224},{224... | collective-permute-start | bytes 1572872 | tf_op jit(solution)/shard_map/ppermute | solution.py:20
  39.6 0.8 copy-start
  49.1 23.9 %collective-permute-start.3 = (f32[4,16,1280]{2,1,0:T(8,128)}, f32[4,16,1280]{2,1,0:T(8,128)S(1)}, u32[]{:S(2)}, u32[]{:S(2)}) collective-permute-start(f32[4,16,1280]{2,1,0:T(8,128)} %get-tuple-element.43), channel_id=1, source_target_pairs={{0,32},{32,64},{64,96},{96,128},{128,160},{160,192},{192,224},{224... | collective-permute-start | bytes 983048 | tf_op jit(solution)/shard_map/ppermute | solution.py:20
  51.0 22.0 %collective-permute-start.4 = (f32[4,16,1280]{2,1,0:T(8,128)S(1)}, f32[4,16,1280]{2,1,0:T(8,128)}, u32[]{:S(2)}, u32[]{:S(2)}) collective-permute-start(f32[4,16,1280]{2,1,0:T(8,128)S(1)} %get-tuple-element.45), channel_id=1, source_target_pairs={{0,480},{32,0},{64,32},{96,64},{128,96},{160,128},{192,160},{224,1... | collective-permute-start | bytes 983048 | tf_op jit(solution)/shard_map/ppermute | solution.py:20
  56.3 15.8 %collective-permute-start.5 = (f32[4,8,1280]{2,1,0:T(8,128)}, f32[4,8,1280]{2,1,0:T(8,128)}, u32[]{:S(2)}, u32[]{:S(2)}) collective-permute-start(f32[4,8,1280]{2,1,0:T(8,128)} %get-tuple-element.53), channel_id=1, source_target_pairs={{0,64},{32,96},{64,128},{96,160},{128,192},{160,224},{192,256},{22... | collective-permute-start | bytes 491528 | tf_op jit(solution)/shard_map/ppermute | solution.py:20
  58.2 14.7 %collective-permute-start.6 = (f32[4,8,1280]{2,1,0:T(8,128)}, f32[4,8,1280]{2,1,0:T(8,128)}, u32[]{:S(2)}, u32[]{:S(2)}) collective-permute-start(f32[4,8,1280]{2,1,0:T(8,128)} %get-tuple-element.54), channel_id=1, source_target_pairs={{0,448},{32,480},{64,0},{96,32},{128,64},{160,96},{192,128},{224,1... | collective-permute-start | bytes 491528 | tf_op jit(solution)/shard_map/ppermute | solution.py:20
  74.2 15.6 %collective-permute-start.7 = (f32[16,1280]{1,0:T(8,128)S(1)}, f32[16,1280]{1,0:T(8,128)S(1)}, u32[]{:S(2)}, u32[]{:S(2)}) collective-permute-start(f32[16,1280]{1,0:T(8,128)S(1)} %get-tuple-element.50), channel_id=1, source_target_pairs={{0,128},{32,160},{64,192},{96,224},{128,256},{160,288},{192,320},{... | collective-permute-start | bytes 245768 | tf_op jit(solution)/shard_map/ppermute | solution.py:20
  76.1 13.7 %collective-permute-start.8 = (f32[16,1280]{1,0:T(8,128)S(1)}, f32[16,1280]{1,0:T(8,128)S(1)}, u32[]{:S(2)}, u32[]{:S(2)}) collective-permute-start(f32[16,1280]{1,0:T(8,128)S(1)} %get-tuple-element.52), channel_id=1, source_target_pairs={{0,384},{32,416},{64,448},{96,480},{128,0},{160,32},{192,64},{224,... | collective-permute-start | bytes 245768 | tf_op jit(solution)/shard_map/ppermute | solution.py:20
  83.4 14.1 %collective-permute-start.9 = (f32[16,1280]{1,0:T(8,128)S(1)}, f32[16,1280]{1,0:T(8,128)S(1)}, u32[]{:S(2)}, u32[]{:S(2)}) collective-permute-start(f32[16,1280]{1,0:T(8,128)S(1)} %get-tuple-element.51), channel_id=1, source_target_pairs={{0,256},{32,288},{64,320},{96,352},{128,384},{160,416},{192,448},{... | collective-permute-start | bytes 245768 | tf_op jit(solution)/shard_map/ppermute | solution.py:20
  97.5 44.4 %collective-permute-start.17 = (f32[16,32,1024]{2,1,0:T(8,128)}, f32[16,32,1024]{2,1,0:T(8,128)}, u32[]{:S(2)}, u32[]{:S(2)}) collective-permute-start(f32[16,32,1024]{2,1,0:T(8,128)} %all-gather.2.cloned.1.call-done), channel_id=1, source_target_pairs={{0,16},{16,0},{1,17},{17,1},{2,18},{18,2},{3,19},{19,3},{4,20},{20... | collective-permute-start | bytes 6291464 | tf_op jit(solution)/shard_map/ppermute | solution.py:24
  99.5 17.6 %collective-permute-start.10 = (f32[16,1280]{1,0:T(8,128)S(1)}, f32[16,1280]{1,0:T(8,128)S(1)}, u32[]{:S(2)}, u32[]{:S(2)}) collective-permute-start(f32[16,1280]{1,0:T(8,128)S(1)} %fusion.29), channel_id=1, source_target_pairs={{0,384},{32,416},{64,448},{96,480},{128,0},{160,32},{192,64},{224,... | collective-permute-start | bytes 245768 | tf_op jit(solution)/shard_map/ppermute | solution.py:20
  104.4 13.9 %collective-permute-start.11 = (f32[16,1280]{1,0:T(8,128)S(1)}, f32[16,1280]{1,0:T(8,128)S(1)}, u32[]{:S(2)}, u32[]{:S(2)}) collective-permute-start(f32[16,1280]{1,0:T(8,128)S(1)} %fusion.29), channel_id=1, source_target_pairs={{0,256},{32,288},{64,320},{96,352},{128,384},{160,416},{192,448},{... | collective-permute-start | bytes 245768 | tf_op jit(solution)/shard_map/ppermute | solution.py:20
  110.9 9.6 %collective-permute-start.12 = (f32[16,1280]{1,0:T(8,128)S(1)}, f32[16,1280]{1,0:T(8,128)S(1)}, u32[]{:S(2)}, u32[]{:S(2)}) collective-permute-start(f32[16,1280]{1,0:T(8,128)S(1)} %fusion.29), channel_id=1, source_target_pairs={{0,128},{32,160},{64,192},{96,224},{128,256},{160,288},{192,320},{... | collective-permute-start | bytes 245768 | tf_op jit(solution)/shard_map/ppermute | solution.py:20
  120.5 28.1 %collective-permute-start.13 = (f32[4,16,1280]{2,1,0:T(8,128)S(1)}, f32[4,16,1280]{2,1,0:T(8,128)S(1)}, u32[]{:S(2)}, u32[]{:S(2)}) collective-permute-start(f32[4,16,1280]{2,1,0:T(8,128)S(1)} %pad_maximum_fusion.2), channel_id=1, source_target_pairs={{0,480},{32,0},{64,32},{96,64},{128,96},{160,128},{192,160},{224,1... | collective-permute-start | bytes 983048 | tf_op jit(solution)/shard_map/ppermute | solution.py:20
  127.3 21.3 %collective-permute-start.14 = (f32[4,16,1280]{2,1,0:T(8,128)S(1)}, f32[4,16,1280]{2,1,0:T(8,128)S(1)}, u32[]{:S(2)}, u32[]{:S(2)}) collective-permute-start(f32[4,16,1280]{2,1,0:T(8,128)S(1)} %pad_maximum_fusion.2), channel_id=1, source_target_pairs={{0,32},{32,64},{64,96},{96,128},{128,160},{160,192},{192,224},{224... | collective-permute-start | bytes 983048 | tf_op jit(solution)/shard_map/ppermute | solution.py:20
  132.9 15.7 %collective-permute-start.15 = (f32[4,8,1280]{2,1,0:T(8,128)S(1)}, f32[4,8,1280]{2,1,0:T(8,128)S(1)}, u32[]{:S(2)}, u32[]{:S(2)}) collective-permute-start(f32[4,8,1280]{2,1,0:T(8,128)S(1)} %get-tuple-element.49), channel_id=1, source_target_pairs={{0,448},{32,480},{64,0},{96,32},{128,64},{160,96},{192,128},{224,1... | collective-permute-start | bytes 491528 | tf_op jit(solution)/shard_map/ppermute | solution.py:20
  135.1 13.5 %collective-permute-start.16 = (f32[4,8,1280]{2,1,0:T(8,128)S(1)}, f32[4,8,1280]{2,1,0:T(8,128)S(1)}, u32[]{:S(2)}, u32[]{:S(2)}) collective-permute-start(f32[4,8,1280]{2,1,0:T(8,128)S(1)} %get-tuple-element.48), channel_id=1, source_target_pairs={{0,64},{32,96},{64,128},{96,160},{128,192},{160,224},{192,256},{22... | collective-permute-start | bytes 491528 | tf_op jit(solution)/shard_map/ppermute | solution.py:20
  151.2 13.4 %copy-start.1 = (f32[128,1024]{1,0:T(8,128)S(1)}, f32[128,1024]{1,0:T(8,128)}, u32[]{:S(2)}) copy-start(f32[128,1024]{1,0:T(8,128)} %copy-done) | copy-start | bytes 1572868
  151.4 26.5 %collective-permute-start.18 = (f32[256,1024]{1,0:T(8,128)S(1)}, f32[256,1024]{1,0:T(8,128)S(1)}, u32[]{:S(2)}, u32[]{:S(2)}) collective-permute-start(f32[256,1024]{1,0:T(8,128)S(1)} %maximum_select_fusion.4), channel_id=1, source_target_pairs={{0,16},{16,0},{1,17},{17,1},{2,18},{18,2},{3,19},{19,3},{4,20},{20... | collective-permute-start | bytes 3145736 | tf_op jit(solution)/shard_map/ppermute | solution.py:24
  153.6 18.6 %collective-permute-start.19 = (f32[128,1024]{1,0:T(8,128)}, f32[128,1024]{1,0:T(8,128)S(1)}, u32[]{:S(2)}, u32[]{:S(2)}) collective-permute-start(f32[128,1024]{1,0:T(8,128)} %collective-permute-done.2), channel_id=1, source_target_pairs={{0,32},{32,64},{64,96},{96,128},{128,160},{160,192},{192,224},{224... | collective-permute-start | bytes 1572872 | tf_op jit(solution)/shard_map/ppermute | solution.py:20
  164.6 11.1 %collective-permute-start.20 = (f32[128,1024]{1,0:T(8,128)S(1)}, f32[128,1024]{1,0:T(8,128)S(1)}, u32[]{:S(2)}, u32[]{:S(2)}) collective-permute-start(f32[128,1024]{1,0:T(8,128)S(1)} %copy-done.1), channel_id=1, source_target_pairs={{0,480},{32,0},{64,32},{96,64},{128,96},{160,128},{192,160},{224,1... | collective-permute-start | bytes 1572872 | tf_op jit(solution)/shard_map/ppermute | solution.py:20
  181.6 25.1 %all-to-all-start = ((f32[32,8,640]{2,1,0:T(8,128)}), f32[32,8,640]{2,1,0:T(8,128)S(1)}, u32[]{:S(2)}, u32[]{:S(2)}) async-start(f32[32,8,640]{2,1,0:T(8,128)} %maximum_bitcast_fusion), calls=%async_computation | async-start | bytes 1310720 | tf_op jit(solution)/shard_map/all_to_all | solution.py:147
Sparse Core Ops, SparseCore 0:
  9.4 81.0 all-gather.1

commit v7 on v6

--- a/solution.py
+++ b/solution.py
@@ -97,7 +97,12 @@
     strip2 = dot(turned[:, 2 * quarter : 3 * quarter], turned[:, 2 * quarter :], ((0,), (0,)))
     partial = jnp.concatenate([strip0, strip2], axis=1)
     blocks = partial.reshape(4, 4, quarter // 16, 5 * quarter)
-    near_sums, plus1, minus1 = lax.optimization_barrier((reduce_near(blocks, place), plus1, minus1))
+    halves = pair_train.reshape(2 * rows, width // 64, 2, 32)
+    even, odd = (halves[:, :, i].reshape(2 * rows, width // 2) for i in range(2))
+    own_half, other_half = jnp.where(first_half, even, odd), jnp.where(first_half, odd, even)
+    near_sums, plus1, minus1, own_half, other_half = lax.optimization_barrier(
+        (reduce_near(blocks, place), plus1, minus1, own_half, other_half)
+    )
     part, own_inverse = lax.optimization_barrier((reduce_far(near_sums, place), own_inverse))
     other_inverse = swap_y(own_inverse)
     pieces = gather_near(gather_far(part))
@@ -106,7 +111,8 @@
         jnp.stack([own_inverse, other_inverse], axis=1),
         jnp.stack([other_inverse, own_inverse], axis=1),
     ).reshape(width, width)
-    side = dot(pair_train, inverse, ((1,), (0,)))
+    side = dot(own_half, own_inverse.reshape(width // 2, width), ((1,), (0,)))
+    side = side + dot(other_half, other_inverse.reshape(width // 2, width), ((1,), (0,)))
     pieces, side = lax.optimization_barrier((pieces, side))
 
     gathered = joined(*pieces).reshape(quarter, 5 * quarter)

time: 217 us -> 221 us (1.018)
  waiting for transfers between devices: 58.7 us -> 70.5 us
  starting transfers between devices: 114 us -> 106 us
  matrix products: 12.8 us -> 17.1 us
  other arithmetic: 10.8 us -> 8.19 us
    ppermute x18, starting transfers between devices: 91.7 us -> 74 us  [shift_z(): lax.ppermute(value, 'z', [(i, (i + steps) % count) for i in range(count)])]
    ppermute x18, waiting for transfers between devices: 42.3 us -> 49.3 us  [shift_z(): lax.ppermute(value, 'z', [(i, (i + steps) % count) for i in range(count)])]
    ppermute x3, starting transfers between devices: 9.78 us -> 14.9 us  [swap_y(): return lax.ppermute(value, 'yh', [(0, 1), (1, 0)])]
    all_to_all x1, starting transfers between devices: 12.2 us -> 16.7 us  [on_device(): lax.all_to_all(jnp.concatenate([upper, lower]), ('yh', 'yl', 'x', 'c'), 0...]
    all_gather x1, waiting for transfers between devices: 0.02 us -> 4.51 us  [on_device(): own_inverse = lax.all_gather(inverse_factors[0], 'z', axis=0)]
    dot_general x11 -> x12, matrix products: 12.8 us -> 17.1 us  [dot(): lax.dot_general(left, right, (dims, ((), ())), precision=FAST, preferred_...]
    select_n x1, other arithmetic: 4.39 us -> 0.63 us  [on_device(): jnp.where(first_half, jnp.stack([own_inverse, other_inverse], axis=1), jn...]
  transfers between devices with their start and end apart: 23 -> 23, of which waited for: 11 -> 15; matrix products, arithmetic and copies ran while one was open for 9% -> 8% of each run, Pallas kernels for 0% -> 0%
where the time goes in v7:
time: 221 us; the launch traced here: 220 us
  starting transfers between devices  106 us (48%)
  waiting for transfers between devices  70.5 us (32%)
  matrix products  17.1 us (8%)
  between operations  14.2 us (6%)
  other arithmetic  8.19 us (4%)
  local copies, waits for them, and re-layouts  4.73 us (2%)
    ppermute x18, starting transfers between devices, shift_z(): lax.ppermute(value, 'z', [(i, (i + steps) % count) for i in range(count)])  74 us
    ppermute x18, waiting for transfers between devices, shift_z(): lax.ppermute(value, 'z', [(i, (i + steps) % count) for i in range(count)])  49.3 us
    dot_general x12, matrix products, dot(): lax.dot_general(left, right, (dims, ((), ())), precision=FAST, preferred_...  17.1 us
    all_to_all x1, starting transfers between devices, on_device(): lax.all_to_all(jnp.concatenate([upper, lower]), ('yh', 'yl', 'x', 'c'), 0...  16.7 us
    ppermute x3, starting transfers between devices, swap_y(): return lax.ppermute(value, 'yh', [(0, 1), (1, 0)])  14.9 us
    all_to_all x1, waiting for transfers between devices, on_device(): lax.all_to_all(jnp.concatenate([upper, lower]), ('yh', 'yl', 'x', 'c'), 0...  12.8 us
    all_gather x1, waiting for transfers between devices, on_device(): own_inverse = lax.all_gather(inverse_factors[0], 'z', axis=0)  4.51 us
  transfers between devices with their start and end apart: 23, of which 15 were waited for; matrix products, arithmetic and copies ran while one was open for 8% of the time, Pallas kernels for 0%

profile of v7, /device:TPU:1, one launch (start us, length us, event | category | flops | bytes accessed | tf_op | source)
XLA Modules:
  0.0 220.4 jit_solution(12421456812050655225)
XLA Ops:
  8.5 5.7 %collective-permute-start = (f32[128,1024]{1,0:T(8,128)S(1)}, f32[128,1024]{1,0:T(8,128)S(1)}, u32[]{:S(2)}, u32[]{:S(2)}) collective-permute-start(f32[128,1024]{1,0:T(8,128)S(1)} %bitcast_multiply_fusion), channel_id=1, source_target_pairs={{0,16},{16,0},{1,17},{17,1},{2,18},{18,2},{3,19},{19,3},{4,20},{20... | collective-permute-start | bytes 1572872 | tf_op jit(solution)/shard_map/ppermute | solution.py:24
  15.3 11.1 %collective-permute-start.1 = (f32[128,1024]{1,0:T(8,128)S(1)}, f32[128,1024]{1,0:T(8,128)}, u32[]{:S(2)}, u32[]{:S(2)}) collective-permute-start(f32[128,1024]{1,0:T(8,128)S(1)} %bitcast.85), channel_id=1, source_target_pairs={{0,480},{32,0},{64,32},{96,64},{128,96},{160,128},{192,160},{224,1... | collective-permute-start | bytes 1572872 | tf_op jit(solution)/shard_map/ppermute | solution.py:20
  29.0 7.7 %collective-permute-done.1 = f32[128,1024]{1,0:T(8,128)} collective-permute-done((f32[128,1024]{1,0:T(8,128)S(1)}, f32[128,1024]{1,0:T(8,128)}, u32[]{:S(2)}, u32[]{:S(2)}) %collective-permute-start.1) | collective-permute-done | bytes 524320 | tf_op jit(solution)/shard_map/ppermute | solution.py:20
  36.7 5.1 %collective-permute-done.2 = f32[128,1024]{1,0:T(8,128)} collective-permute-done((f32[128,1024]{1,0:T(8,128)S(1)}, f32[128,1024]{1,0:T(8,128)}, u32[]{:S(2)}, u32[]{:S(2)}) %collective-permute-start.2) | collective-permute-done | bytes 524320 | tf_op jit(solution)/shard_map/ppermute | solution.py:20
  47.1 4.3 %collective-permute-start.5 = (f32[4,8,1280]{2,1,0:T(8,128)S(1)}, f32[4,8,1280]{2,1,0:T(8,128)S(1)}, u32[]{:S(2)}, u32[]{:S(2)}) collective-permute-start(f32[4,8,1280]{2,1,0:T(8,128)S(1)} %get-tuple-element.59), channel_id=1, source_target_pairs={{0,64},{32,96},{64,128},{96,160},{128,192},{160,224},{192,256},{22... | collective-permute-start | bytes 491528 | tf_op jit(solution)/shard_map/ppermute | solution.py:20
  51.4 2.6 %collective-permute-start.4 = (f32[4,16,1280]{2,1,0:T(8,128)S(1)}, f32[4,16,1280]{2,1,0:T(8,128)S(1)}, u32[]{:S(2)}, u32[]{:S(2)}) collective-permute-start(f32[4,16,1280]{2,1,0:T(8,128)S(1)} %get-tuple-element.49), channel_id=1, source_target_pairs={{0,480},{32,0},{64,32},{96,64},{128,96},{160,128},{192,160},{224,1... | collective-permute-start | bytes 983048 | tf_op jit(solution)/shard_map/ppermute | solution.py:20
  54.1 2.6 %collective-permute-start.3 = (f32[4,16,1280]{2,1,0:T(8,128)S(1)}, f32[4,16,1280]{2,1,0:T(8,128)S(1)}, u32[]{:S(2)}, u32[]{:S(2)}) collective-permute-start(f32[4,16,1280]{2,1,0:T(8,128)S(1)} %get-tuple-element.47), channel_id=1, source_target_pairs={{0,32},{32,64},{64,96},{96,128},{128,160},{160,192},{192,224},{224... | collective-permute-start | bytes 983048 | tf_op jit(solution)/shard_map/ppermute | solution.py:20
  57.9 4.8 %collective-permute-done.5 = f32[4,8,1280]{2,1,0:T(8,128)S(1)} collective-permute-done((f32[4,8,1280]{2,1,0:T(8,128)S(1)}, f32[4,8,1280]{2,1,0:T(8,128)S(1)}, u32[]{:S(2)}, u32[]{:S(2)}) %collective-permute-start.5) | collective-permute-done | bytes 163872 | tf_op jit(solution)/shard_map/ppermute | solution.py:20
  62.8 4.8 %collective-permute-done.4 = f32[4,16,1280]{2,1,0:T(8,128)S(1)} collective-permute-done((f32[4,16,1280]{2,1,0:T(8,128)S(1)}, f32[4,16,1280]{2,1,0:T(8,128)S(1)}, u32[]{:S(2)}, u32[]{:S(2)}) %collective-permute-start.4) | collective-permute-done | bytes 327712 | tf_op jit(solution)/shard_map/ppermute | solution.py:20
  67.6 5.2 %collective-permute-done.3 = f32[4,16,1280]{2,1,0:T(8,128)S(1)} collective-permute-done((f32[4,16,1280]{2,1,0:T(8,128)S(1)}, f32[4,16,1280]{2,1,0:T(8,128)S(1)}, u32[]{:S(2)}, u32[]{:S(2)}) %collective-permute-start.3) | collective-permute-done | bytes 327712 | tf_op jit(solution)/shard_map/ppermute | solution.py:20
  72.9 6.9 %collective-permute-start.9 = (f32[16,1280]{1,0:T(8,128)S(1)}, f32[16,1280]{1,0:T(8,128)S(1)}, u32[]{:S(2)}, u32[]{:S(2)}) collective-permute-start(f32[16,1280]{1,0:T(8,128)S(1)} %get-tuple-element.57), channel_id=1, source_target_pairs={{0,256},{32,288},{64,320},{96,352},{128,384},{160,416},{192,448},{... | collective-permute-start | bytes 245768 | tf_op jit(solution)/shard_map/ppermute | solution.py:20
  79.8 4.5 %collective-permute-start.8 = (f32[16,1280]{1,0:T(8,128)S(1)}, f32[16,1280]{1,0:T(8,128)S(1)}, u32[]{:S(2)}, u32[]{:S(2)}) collective-permute-start(f32[16,1280]{1,0:T(8,128)S(1)} %get-tuple-element.58), channel_id=1, source_target_pairs={{0,384},{32,416},{64,448},{96,480},{128,0},{160,32},{192,64},{224,... | collective-permute-start | bytes 245768 | tf_op jit(solution)/shard_map/ppermute | solution.py:20
  84.3 4.7 %collective-permute-start.7 = (f32[16,1280]{1,0:T(8,128)S(1)}, f32[16,1280]{1,0:T(8,128)S(1)}, u32[]{:S(2)}, u32[]{:S(2)}) collective-permute-start(f32[16,1280]{1,0:T(8,128)S(1)} %get-tuple-element.56), channel_id=1, source_target_pairs={{0,128},{32,160},{64,192},{96,224},{128,256},{160,288},{192,320},{... | collective-permute-start | bytes 245768 | tf_op jit(solution)/shard_map/ppermute | solution.py:20
  89.0 2.5 %collective-permute-done.9 = f32[16,1280]{1,0:T(8,128)S(1)} collective-permute-done((f32[16,1280]{1,0:T(8,128)S(1)}, f32[16,1280]{1,0:T(8,128)S(1)}, u32[]{:S(2)}, u32[]{:S(2)}) %collective-permute-start.9) | collective-permute-done | bytes 81952 | tf_op jit(solution)/shard_map/ppermute | solution.py:20
  91.6 9.3 %collective-permute-done.8 = f32[16,1280]{1,0:T(8,128)S(1)} collective-permute-done((f32[16,1280]{1,0:T(8,128)S(1)}, f32[16,1280]{1,0:T(8,128)S(1)}, u32[]{:S(2)}, u32[]{:S(2)}) %collective-permute-start.8) | collective-permute-done | bytes 81952 | tf_op jit(solution)/shard_map/ppermute | solution.py:20
  100.9 4.5 %all-gather.2.cloned.1.call-done = f32[16,32,1024]{2,1,0:T(8,128)} async-done(((f32[1,32,1024]{2,1,0:T(8,128)}), f32[16,32,1024]{2,1,0:T(8,128)}) %all-gather.2.cloned.1.call-update) | async-done | bytes 2097168 | tf_op jit(solution)/shard_map/all_gather | solution.py:86
  105.5 4.9 %collective-permute-start.17 = (f32[16,32,1024]{2,1,0:T(8,128)}, f32[16,32,1024]{2,1,0:T(8,128)S(1)}, u32[]{:S(2)}, u32[]{:S(2)}) collective-permute-start(f32[16,32,1024]{2,1,0:T(8,128)} %all-gather.2.cloned.1.call-done), channel_id=1, source_target_pairs={{0,16},{16,0},{1,17},{17,1},{2,18},{18,2},{3,19},{19,3},{4,20},{20... | collective-permute-start | bytes 6291464 | tf_op jit(solution)/shard_map/ppermute | solution.py:24
  110.4 4.3 %collective-permute-start.12 = (f32[16,1280]{1,0:T(8,128)S(1)}, f32[16,1280]{1,0:T(8,128)S(1)}, u32[]{:S(2)}, u32[]{:S(2)}) collective-permute-start(f32[16,1280]{1,0:T(8,128)S(1)} %fusion.29), channel_id=1, source_target_pairs={{0,128},{32,160},{64,192},{96,224},{128,256},{160,288},{192,320},{... | collective-permute-start | bytes 245768 | tf_op jit(solution)/shard_map/ppermute | solution.py:20
  114.6 7.4 %collective-permute-start.11 = (f32[16,1280]{1,0:T(8,128)S(1)}, f32[16,1280]{1,0:T(8,128)S(1)}, u32[]{:S(2)}, u32[]{:S(2)}) collective-permute-start(f32[16,1280]{1,0:T(8,128)S(1)} %fusion.29), channel_id=1, source_target_pairs={{0,256},{32,288},{64,320},{96,352},{128,384},{160,416},{192,448},{... | collective-permute-start | bytes 245768 | tf_op jit(solution)/shard_map/ppermute | solution.py:20
  122.1 4.9 %collective-permute-start.10 = (f32[16,1280]{1,0:T(8,128)S(1)}, f32[16,1280]{1,0:T(8,128)S(1)}, u32[]{:S(2)}, u32[]{:S(2)}) collective-permute-start(f32[16,1280]{1,0:T(8,128)S(1)} %fusion.29), channel_id=1, source_target_pairs={{0,384},{32,416},{64,448},{96,480},{128,0},{160,32},{192,64},{224,... | collective-permute-start | bytes 245768 | tf_op jit(solution)/shard_map/ppermute | solution.py:20
  127.0 2.8 %fusion.36 = f32[256,1024]{1,0:T(8,128)S(1)} fusion(f32[256,512]{0,1:T(8,128)} %bitcast.89, f32[512,1024]{1,0:T(8,128)} %bitcast.77), kind=kOutput, calls=%fused_computation.78 | convolution fusion | flops 805306368 | bytes 3670016 | tf_op jit(solution)/shard_map/dot_general | solution.py:13
  130.3 5.2 %collective-permute-done.10 = f32[16,1280]{1,0:T(8,128)S(1)} collective-permute-done((f32[16,1280]{1,0:T(8,128)S(1)}, f32[16,1280]{1,0:T(8,128)S(1)}, u32[]{:S(2)}, u32[]{:S(2)}) %collective-permute-start.10) | collective-permute-done | bytes 81952 | tf_op jit(solution)/shard_map/ppermute | solution.py:20
  137.4 3.4 %collective-permute-start.14 = (f32[4,16,1280]{2,1,0:T(8,128)S(1)}, f32[4,16,1280]{2,1,0:T(8,128)S(1)}, u32[]{:S(2)}, u32[]{:S(2)}) collective-permute-start(f32[4,16,1280]{2,1,0:T(8,128)S(1)} %pad_maximum_fusion.2), channel_id=1, source_target_pairs={{0,32},{32,64},{64,96},{96,128},{128,160},{160,192},{192,224},{224... | collective-permute-start | bytes 983048 | tf_op jit(solution)/shard_map/ppermute | solution.py:20
  142.8 4.3 %collective-permute-start.16 = (f32[4,8,1280]{2,1,0:T(8,128)S(1)}, f32[4,8,1280]{2,1,0:T(8,128)S(1)}, u32[]{:S(2)}, u32[]{:S(2)}) collective-permute-start(f32[4,8,1280]{2,1,0:T(8,128)S(1)} %get-tuple-element.54), channel_id=1, source_target_pairs={{0,64},{32,96},{64,128},{96,160},{128,192},{160,224},{192,256},{22... | collective-permute-start | bytes 491528 | tf_op jit(solution)/shard_map/ppermute | solution.py:20
  147.0 3.7 %collective-permute-done.17 = f32[16,32,1024]{2,1,0:T(8,128)S(1)} collective-permute-done((f32[16,32,1024]{2,1,0:T(8,128)}, f32[16,32,1024]{2,1,0:T(8,128)S(1)}, u32[]{:S(2)}, u32[]{:S(2)}) %collective-permute-start.17) | collective-permute-done | bytes 2097184 | tf_op jit(solution)/shard_map/ppermute | solution.py:24
  157.9 4.4 %collective-permute-start.18 = (f32[256,1024]{1,0:T(8,128)S(1)}, f32[256,1024]{1,0:T(8,128)S(1)}, u32[]{:S(2)}, u32[]{:S(2)}) collective-permute-start(f32[256,1024]{1,0:T(8,128)S(1)} %maximum_select_fusion.5), channel_id=1, source_target_pairs={{0,16},{16,0},{1,17},{17,1},{2,18},{18,2},{3,19},{19,3},{4,20},{20... | collective-permute-start | bytes 3145736 | tf_op jit(solution)/shard_map/ppermute | solution.py:24
  164.2 3.5 %collective-permute-start.19 = (f32[128,1024]{1,0:T(8,128)}, f32[128,1024]{1,0:T(8,128)S(1)}, u32[]{:S(2)}, u32[]{:S(2)}) collective-permute-start(f32[128,1024]{1,0:T(8,128)} %collective-permute-done.2), channel_id=1, source_target_pairs={{0,32},{32,64},{64,96},{96,128},{128,160},{160,192},{192,224},{224... | collective-permute-start | bytes 1572872 | tf_op jit(solution)/shard_map/ppermute | solution.py:20
  168.8 5.2 %fusion = f32[384,1024]{1,0:T(8,128)} fusion(f32[1024,1024]{1,0:T(8,128)S(1)} %bitcast.75, f32[128,1024]{1,0:T(8,128)} %collective-permute-done.1, f32[128,1024]{1,0:T(8,128)S(1)} %bitcast.87, f32[128,1024]{1,0:T(8,128)} %collective-permute-done.2), kind=kOutput, calls=%fused_computation.3 | convolution fusion | flops 2416705536 | bytes 7340032 | tf_op jit(solution)/shard_map/dot_general | solution.py:13
  176.0 2.2 fusion.7
  179.5 2.4 %fusion.38 = f32[256,384]{1,0:T(8,128)S(1)} fusion(f32[256,1024]{1,0:T(8,128)S(1)} %multiply_subtract_fusion, f32[384,1024]{1,0:T(8,128)} %fusion), kind=kOutput, calls=%fused_computation.80 | convolution fusion | flops 603979776 | bytes 3014656 | tf_op jit(solution)/shard_map/dot_general | solution.py:13
  183.2 16.7 %all-to-all-start = ((f32[32,8,640]{2,1,0:T(8,128)}), f32[32,8,640]{2,1,0:T(8,128)S(1)}, u32[]{:S(2)}, u32[]{:S(2)}) async-start(f32[32,8,640]{2,1,0:T(8,128)} %maximum_bitcast_fusion), calls=%async_computation | async-start | bytes 1310720 | tf_op jit(solution)/shard_map/all_to_all | solution.py:153
  200.0 12.8 %all-to-all-done = f32[32,8,640]{2,1,0:T(8,128)S(1)} async-done(((f32[32,8,640]{2,1,0:T(8,128)}), f32[32,8,640]{2,1,0:T(8,128)S(1)}, u32[]{:S(2)}, u32[]{:S(2)}) %all-to-all-start) | async-done | bytes 655392 | tf_op jit(solution)/shard_map/all_to_all | solution.py:153
  (92 shorter events, 31.7 us)
Async XLA Ops:
  6.5 21.9 %copy-start.6 = (f32[128,1,1024]{2,1,0:T(1,128)S(1)}, f32[128,1,1024]{2,1,0:T(1,128)}, u32[]{:S(2)}) copy-start(f32[128,1,1024]{2,1,0:T(1,128)} %param.4) | copy-start | bytes 1572868
  6.5 98.9 %all-gather.2.cloned.1.call-start = ((), (), s32[]{:S(2)}) async-start(), calls=%async_computation.1 | async-start | bytes 2228224 | tf_op jit(solution)/shard_map/all_gather | solution.py:86
  8.5 20.5 %collective-permute-start = (f32[128,1024]{1,0:T(8,128)S(1)}, f32[128,1024]{1,0:T(8,128)S(1)}, u32[]{:S(2)}, u32[]{:S(2)}) collective-permute-start(f32[128,1024]{1,0:T(8,128)S(1)} %bitcast_multiply_fusion), channel_id=1, source_target_pairs={{0,16},{16,0},{1,17},{17,1},{2,18},{18,2},{3,19},{19,3},{4,20},{20... | collective-permute-start | bytes 1572872 | tf_op jit(solution)/shard_map/ppermute | solution.py:24
  15.3 21.4 %copy-start.3 = (f32[128,1,1024]{2,0,1:T(8,128)}, f32[128,1,1024]{2,0,1:T(8,128)S(1)}, u32[]{:S(2)}) copy-start(f32[128,1,1024]{2,0,1:T(8,128)S(1)} %copy.45) | copy-start | bytes 1572868
  15.3 21.4 %collective-permute-start.1 = (f32[128,1024]{1,0:T(8,128)S(1)}, f32[128,1024]{1,0:T(8,128)}, u32[]{:S(2)}, u32[]{:S(2)}) collective-permute-start(f32[128,1024]{1,0:T(8,128)S(1)} %bitcast.85), channel_id=1, source_target_pairs={{0,480},{32,0},{64,32},{96,64},{128,96},{160,128},{192,160},{224,1... | collective-permute-start | bytes 1572872 | tf_op jit(solution)/shard_map/ppermute | solution.py:20
  26.4 15.4 %collective-permute-start.2 = (f32[128,1024]{1,0:T(8,128)S(1)}, f32[128,1024]{1,0:T(8,128)}, u32[]{:S(2)}, u32[]{:S(2)}) collective-permute-start(f32[128,1024]{1,0:T(8,128)S(1)} %bitcast.86), channel_id=1, source_target_pairs={{0,32},{32,64},{64,96},{96,128},{128,160},{160,192},{192,224},{224... | collective-permute-start | bytes 1572872 | tf_op jit(solution)/shard_map/ppermute | solution.py:20
  45.2 12.7 %collective-permute-start.6 = (f32[4,8,1280]{2,1,0:T(8,128)S(1)}, f32[4,8,1280]{2,1,0:T(8,128)S(1)}, u32[]{:S(2)}, u32[]{:S(2)}) collective-permute-start(f32[4,8,1280]{2,1,0:T(8,128)S(1)} %get-tuple-element.60), channel_id=1, source_target_pairs={{0,448},{32,480},{64,0},{96,32},{128,64},{160,96},{192,128},{224,1... | collective-permute-start | bytes 491528 | tf_op jit(solution)/shard_map/ppermute | solution.py:20
  47.1 15.6 %collective-permute-start.5 = (f32[4,8,1280]{2,1,0:T(8,128)S(1)}, f32[4,8,1280]{2,1,0:T(8,128)S(1)}, u32[]{:S(2)}, u32[]{:S(2)}) collective-permute-start(f32[4,8,1280]{2,1,0:T(8,128)S(1)} %get-tuple-element.59), channel_id=1, source_target_pairs={{0,64},{32,96},{64,128},{96,160},{128,192},{160,224},{192,256},{22... | collective-permute-start | bytes 491528 | tf_op jit(solution)/shard_map/ppermute | solution.py:20
  51.4 16.2 %collective-permute-start.4 = (f32[4,16,1280]{2,1,0:T(8,128)S(1)}, f32[4,16,1280]{2,1,0:T(8,128)S(1)}, u32[]{:S(2)}, u32[]{:S(2)}) collective-permute-start(f32[4,16,1280]{2,1,0:T(8,128)S(1)} %get-tuple-element.49), channel_id=1, source_target_pairs={{0,480},{32,0},{64,32},{96,64},{128,96},{160,128},{192,160},{224,1... | collective-permute-start | bytes 983048 | tf_op jit(solution)/shard_map/ppermute | solution.py:20
  54.1 18.7 %collective-permute-start.3 = (f32[4,16,1280]{2,1,0:T(8,128)S(1)}, f32[4,16,1280]{2,1,0:T(8,128)S(1)}, u32[]{:S(2)}, u32[]{:S(2)}) collective-permute-start(f32[4,16,1280]{2,1,0:T(8,128)S(1)} %get-tuple-element.47), channel_id=1, source_target_pairs={{0,32},{32,64},{64,96},{96,128},{128,160},{160,192},{192,224},{224... | collective-permute-start | bytes 983048 | tf_op jit(solution)/shard_map/ppermute | solution.py:20
  72.9 18.6 %collective-permute-start.9 = (f32[16,1280]{1,0:T(8,128)S(1)}, f32[16,1280]{1,0:T(8,128)S(1)}, u32[]{:S(2)}, u32[]{:S(2)}) collective-permute-start(f32[16,1280]{1,0:T(8,128)S(1)} %get-tuple-element.57), channel_id=1, source_target_pairs={{0,256},{32,288},{64,320},{96,352},{128,384},{160,416},{192,448},{... | collective-permute-start | bytes 245768 | tf_op jit(solution)/shard_map/ppermute | solution.py:20
  79.8 21.1 %collective-permute-start.8 = (f32[16,1280]{1,0:T(8,128)S(1)}, f32[16,1280]{1,0:T(8,128)S(1)}, u32[]{:S(2)}, u32[]{:S(2)}) collective-permute-start(f32[16,1280]{1,0:T(8,128)S(1)} %get-tuple-element.58), channel_id=1, source_target_pairs={{0,384},{32,416},{64,448},{96,480},{128,0},{160,32},{192,64},{224,... | collective-permute-start | bytes 245768 | tf_op jit(solution)/shard_map/ppermute | solution.py:20
  84.3 16.6 %collective-permute-start.7 = (f32[16,1280]{1,0:T(8,128)S(1)}, f32[16,1280]{1,0:T(8,128)S(1)}, u32[]{:S(2)}, u32[]{:S(2)}) collective-permute-start(f32[16,1280]{1,0:T(8,128)S(1)} %get-tuple-element.56), channel_id=1, source_target_pairs={{0,128},{32,160},{64,192},{96,224},{128,256},{160,288},{192,320},{... | collective-permute-start | bytes 245768 | tf_op jit(solution)/shard_map/ppermute | solution.py:20
  105.5 45.3 %collective-permute-start.17 = (f32[16,32,1024]{2,1,0:T(8,128)}, f32[16,32,1024]{2,1,0:T(8,128)S(1)}, u32[]{:S(2)}, u32[]{:S(2)}) collective-permute-start(f32[16,32,1024]{2,1,0:T(8,128)} %all-gather.2.cloned.1.call-done), channel_id=1, source_target_pairs={{0,16},{16,0},{1,17},{17,1},{2,18},{18,2},{3,19},{19,3},{4,20},{20... | collective-permute-start | bytes 6291464 | tf_op jit(solution)/shard_map/ppermute | solution.py:24
  110.4 19.4 %collective-permute-start.12 = (f32[16,1280]{1,0:T(8,128)S(1)}, f32[16,1280]{1,0:T(8,128)S(1)}, u32[]{:S(2)}, u32[]{:S(2)}) collective-permute-start(f32[16,1280]{1,0:T(8,128)S(1)} %fusion.29), channel_id=1, source_target_pairs={{0,128},{32,160},{64,192},{96,224},{128,256},{160,288},{192,320},{... | collective-permute-start | bytes 245768 | tf_op jit(solution)/shard_map/ppermute | solution.py:20
  114.6 15.6 %collective-permute-start.11 = (f32[16,1280]{1,0:T(8,128)S(1)}, f32[16,1280]{1,0:T(8,128)S(1)}, u32[]{:S(2)}, u32[]{:S(2)}) collective-permute-start(f32[16,1280]{1,0:T(8,128)S(1)} %fusion.29), channel_id=1, source_target_pairs={{0,256},{32,288},{64,320},{96,352},{128,384},{160,416},{192,448},{... | collective-permute-start | bytes 245768 | tf_op jit(solution)/shard_map/ppermute | solution.py:20
  122.1 13.4 %collective-permute-start.10 = (f32[16,1280]{1,0:T(8,128)S(1)}, f32[16,1280]{1,0:T(8,128)S(1)}, u32[]{:S(2)}, u32[]{:S(2)}) collective-permute-start(f32[16,1280]{1,0:T(8,128)S(1)} %fusion.29), channel_id=1, source_target_pairs={{0,384},{32,416},{64,448},{96,480},{128,0},{160,32},{192,64},{224,... | collective-permute-start | bytes 245768 | tf_op jit(solution)/shard_map/ppermute | solution.py:20
  129.8 20.9 %copy-start.5 = (f32[256,16,1,32]{0,3,2,1:T(8,128)S(1)}, f32[256,16,1,32]{0,3,2,1:T(8,128)}, u32[]{:S(2)}) copy-start(f32[256,16,1,32]{0,3,2,1:T(8,128)} %get-tuple-element.50) | copy-start | bytes 1572868
  135.5 18.5 %collective-permute-start.13 = (f32[4,16,1280]{2,1,0:T(8,128)S(1)}, f32[4,16,1280]{2,1,0:T(8,128)S(1)}, u32[]{:S(2)}, u32[]{:S(2)}) collective-permute-start(f32[4,16,1280]{2,1,0:T(8,128)S(1)} %pad_maximum_fusion.2), channel_id=1, source_target_pairs={{0,480},{32,0},{64,32},{96,64},{128,96},{160,128},{192,160},{224,1... | collective-permute-start | bytes 983048 | tf_op jit(solution)/shard_map/ppermute | solution.py:20
  137.4 16.6 %collective-permute-start.14 = (f32[4,16,1280]{2,1,0:T(8,128)S(1)}, f32[4,16,1280]{2,1,0:T(8,128)S(1)}, u32[]{:S(2)}, u32[]{:S(2)}) collective-permute-start(f32[4,16,1280]{2,1,0:T(8,128)S(1)} %pad_maximum_fusion.2), channel_id=1, source_target_pairs={{0,32},{32,64},{64,96},{96,128},{128,160},{160,192},{192,224},{224... | collective-permute-start | bytes 983048 | tf_op jit(solution)/shard_map/ppermute | solution.py:20
  140.8 11.1 %collective-permute-start.15 = (f32[4,8,1280]{2,1,0:T(8,128)S(1)}, f32[4,8,1280]{2,1,0:T(8,128)S(1)}, u32[]{:S(2)}, u32[]{:S(2)}) collective-permute-start(f32[4,8,1280]{2,1,0:T(8,128)S(1)} %get-tuple-element.55), channel_id=1, source_target_pairs={{0,448},{32,480},{64,0},{96,32},{128,64},{160,96},{192,128},{224,1... | collective-permute-start | bytes 491528 | tf_op jit(solution)/shard_map/ppermute | solution.py:20
  142.8 11.3 %collective-permute-start.16 = (f32[4,8,1280]{2,1,0:T(8,128)S(1)}, f32[4,8,1280]{2,1,0:T(8,128)S(1)}, u32[]{:S(2)}, u32[]{:S(2)}) collective-permute-start(f32[4,8,1280]{2,1,0:T(8,128)S(1)} %get-tuple-element.54), channel_id=1, source_target_pairs={{0,64},{32,96},{64,128},{96,160},{128,192},{160,224},{192,256},{22... | collective-permute-start | bytes 491528 | tf_op jit(solution)/shard_map/ppermute | solution.py:20
  151.9 2.3 %copy-start = (f32[256,1024]{1,0:T(8,128)}, f32[256,1024]{1,0:T(8,128)S(1)}, u32[]{:S(2)}) copy-start(f32[256,1024]{1,0:T(8,128)S(1)} %convolution_add_fusion) | copy-start | bytes 3145732
  154.3 1.2 copy-start.1
  154.3 1.3 slice-start
  154.3 1.5 slice-start.1
  157.3 10.4 %copy-start.2 = (f32[16,32,1024]{2,1,0:T(8,128)S(1)}, f32[16,32,1024]{2,1,0:T(8,128)}, u32[]{:S(2)}) copy-start(f32[16,32,1024]{2,1,0:T(8,128)} %all-gather.2.cloned.1.call-done) | copy-start | bytes 6291460
  157.9 20.3 %collective-permute-start.18 = (f32[256,1024]{1,0:T(8,128)S(1)}, f32[256,1024]{1,0:T(8,128)S(1)}, u32[]{:S(2)}, u32[]{:S(2)}) collective-permute-start(f32[256,1024]{1,0:T(8,128)S(1)} %maximum_select_fusion.5), channel_id=1, source_target_pairs={{0,16},{16,0},{1,17},{17,1},{2,18},{18,2},{3,19},{19,3},{4,20},{20... | collective-permute-start | bytes 3145736 | tf_op jit(solution)/shard_map/ppermute | solution.py:24
  162.3 11.7 %collective-permute-start.20 = (f32[128,1024]{1,0:T(8,128)}, f32[128,1024]{1,0:T(8,128)S(1)}, u32[]{:S(2)}, u32[]{:S(2)}) collective-permute-start(f32[128,1024]{1,0:T(8,128)} %collective-permute-done.1), channel_id=1, source_target_pairs={{0,480},{32,0},{64,32},{96,64},{128,96},{160,128},{192,160},{224,1... | collective-permute-start | bytes 1572872 | tf_op jit(solution)/shard_map/ppermute | solution.py:20
  164.2 11.8 %collective-permute-start.19 = (f32[128,1024]{1,0:T(8,128)}, f32[128,1024]{1,0:T(8,128)S(1)}, u32[]{:S(2)}, u32[]{:S(2)}) collective-permute-start(f32[128,1024]{1,0:T(8,128)} %collective-permute-done.2), channel_id=1, source_target_pairs={{0,32},{32,64},{64,96},{96,128},{128,160},{160,192},{192,224},{224... | collective-permute-start | bytes 1572872 | tf_op jit(solution)/shard_map/ppermute | solution.py:20
  167.8 1.0 copy-start.4
  183.2 29.6 %all-to-all-start = ((f32[32,8,640]{2,1,0:T(8,128)}), f32[32,8,640]{2,1,0:T(8,128)S(1)}, u32[]{:S(2)}, u32[]{:S(2)}) async-start(f32[32,8,640]{2,1,0:T(8,128)} %maximum_bitcast_fusion), calls=%async_computation | async-start | bytes 1310720 | tf_op jit(solution)/shard_map/all_to_all | solution.py:153
Sparse Core Ops, SparseCore 0:
  28.5 76.9 all-gather.1

commit v8 on v6

--- a/solution.py
+++ b/solution.py
@@ -84,9 +84,8 @@
     total_rows = rows * lax.axis_size("z") * lax.axis_size("yh")
 
     own_inverse = lax.all_gather(inverse_factors[0], "z", axis=0)
-    other_train, plus1, minus1 = lax.optimization_barrier(
-        (swap_y(train), shift_z(query, -1), shift_z(query, 1))
-    )
+    other_train, plus1 = lax.optimization_barrier((swap_y(train), shift_z(query, -1)))
+    minus1 = shift_z(query, 1)
     pair_train = jnp.where(
         first_half,
         jnp.concatenate([train, other_train]),

time: 217 us -> 227 us (1.046)
  waiting for transfers between devices: 58.7 us -> 73.4 us
  starting transfers between devices: 114 us -> 109 us
    ppermute x18, waiting for transfers between devices: 42.3 us -> 54.4 us  [shift_z(): lax.ppermute(value, 'z', [(i, (i + steps) % count) for i in range(count)])]
    ppermute x18, starting transfers between devices: 91.7 us -> 87.2 us  [shift_z(): lax.ppermute(value, 'z', [(i, (i + steps) % count) for i in range(count)])]
    ppermute x3, waiting for transfers between devices: 2.84 us -> 5.43 us  [swap_y(): return lax.ppermute(value, 'yh', [(0, 1), (1, 0)])]
where the time goes in v8:
time: 227 us; the launch traced here: 223 us
  starting transfers between devices  109 us (48%)
  waiting for transfers between devices  73.4 us (32%)
  between operations  14.2 us (6%)
  matrix products  12.9 us (6%)
  other arithmetic  10.8 us (5%)
  local copies, waits for them, and re-layouts  3.37 us (1%)
    ppermute x18, starting transfers between devices, shift_z(): lax.ppermute(value, 'z', [(i, (i + steps) % count) for i in range(count)])  87.2 us
    ppermute x18, waiting for transfers between devices, shift_z(): lax.ppermute(value, 'z', [(i, (i + steps) % count) for i in range(count)])  54.4 us
    dot_general x11, matrix products, dot(): lax.dot_general(left, right, (dims, ((), ())), precision=FAST, preferred_...  12.9 us
    all_to_all x1, waiting for transfers between devices, on_device(): lax.all_to_all(jnp.concatenate([upper, lower]), ('yh', 'yl', 'x', 'c'), 0...  12.8 us
    all_to_all x1, starting transfers between devices, on_device(): lax.all_to_all(jnp.concatenate([upper, lower]), ('yh', 'yl', 'x', 'c'), 0...  11.9 us
    ppermute x3, starting transfers between devices, swap_y(): return lax.ppermute(value, 'yh', [(0, 1), (1, 0)])  9.49 us
    ppermute x3, waiting for transfers between devices, swap_y(): return lax.ppermute(value, 'yh', [(0, 1), (1, 0)])  5.43 us
  transfers between devices with their start and end apart: 23, of which 11 were waited for; matrix products, arithmetic and copies ran while one was open for 9% of the time, Pallas kernels for 0%

profile of v8, /device:TPU:1, one launch (start us, length us, event | category | flops | bytes accessed | tf_op | source)
XLA Modules:
  0.0 223.3 jit_solution(16098306592274883132)
XLA Ops:
  9.1 5.7 %collective-permute-start = (f32[128,1024]{1,0:T(8,128)S(1)}, f32[128,1024]{1,0:T(8,128)S(1)}, u32[]{:S(2)}, u32[]{:S(2)}) collective-permute-start(f32[128,1024]{1,0:T(8,128)S(1)} %bitcast_multiply_fusion), channel_id=1, source_target_pairs={{0,16},{16,0},{1,17},{17,1},{2,18},{18,2},{3,19},{19,3},{4,20},{20... | collective-permute-start | bytes 1572872 | tf_op jit(solution)/shard_map/ppermute | solution.py:24
  15.9 11.1 %collective-permute-start.1 = (f32[128,1024]{1,0:T(8,128)S(1)}, f32[128,1024]{1,0:T(8,128)}, u32[]{:S(2)}, u32[]{:S(2)}) collective-permute-start(f32[128,1024]{1,0:T(8,128)S(1)} %bitcast.74), channel_id=1, source_target_pairs={{0,480},{32,0},{64,32},{96,64},{128,96},{160,128},{192,160},{224,1... | collective-permute-start | bytes 1572872 | tf_op jit(solution)/shard_map/ppermute | solution.py:20
  27.1 13.3 %collective-permute-done.1 = f32[128,1024]{1,0:T(8,128)} collective-permute-done((f32[128,1024]{1,0:T(8,128)S(1)}, f32[128,1024]{1,0:T(8,128)}, u32[]{:S(2)}, u32[]{:S(2)}) %collective-permute-start.1) | collective-permute-done | bytes 524320 | tf_op jit(solution)/shard_map/ppermute | solution.py:20
  44.6 5.4 %collective-permute-start.3 = (f32[4,16,1280]{2,1,0:T(8,128)S(1)}, f32[4,16,1280]{2,1,0:T(8,128)}, u32[]{:S(2)}, u32[]{:S(2)}) collective-permute-start(f32[4,16,1280]{2,1,0:T(8,128)S(1)} %get-tuple-element.43), channel_id=1, source_target_pairs={{0,480},{32,0},{64,32},{96,64},{128,96},{160,128},{192,160},{224,1... | collective-permute-start | bytes 983048 | tf_op jit(solution)/shard_map/ppermute | solution.py:20
  52.6 5.5 %collective-permute-start.5 = (f32[4,8,1280]{2,1,0:T(8,128)}, f32[4,8,1280]{2,1,0:T(8,128)}, u32[]{:S(2)}, u32[]{:S(2)}) collective-permute-start(f32[4,8,1280]{2,1,0:T(8,128)} %get-tuple-element.52), channel_id=1, source_target_pairs={{0,448},{32,480},{64,0},{96,32},{128,64},{160,96},{192,128},{224,1... | collective-permute-start | bytes 491528 | tf_op jit(solution)/shard_map/ppermute | solution.py:20
  58.1 1.9 collective-permute-start.6
  60.1 5.5 %collective-permute-done.4 = f32[4,8,1280]{2,1,0:T(8,128)} collective-permute-done((f32[4,8,1280]{2,1,0:T(8,128)}, f32[4,8,1280]{2,1,0:T(8,128)}, u32[]{:S(2)}, u32[]{:S(2)}) %collective-permute-start.4) | collective-permute-done | bytes 163872 | tf_op jit(solution)/shard_map/ppermute | solution.py:20
  67.9 18.2 %collective-permute-done.6 = f32[128,1024]{1,0:T(8,128)} collective-permute-done((f32[128,1024]{1,0:T(8,128)S(1)}, f32[128,1024]{1,0:T(8,128)}, u32[]{:S(2)}, u32[]{:S(2)}) %collective-permute-start.6) | collective-permute-done | bytes 524320 | tf_op jit(solution)/shard_map/ppermute | solution.py:20
  88.1 7.3 %collective-permute-start.8 = (f32[16,1280]{1,0:T(8,128)S(1)}, f32[16,1280]{1,0:T(8,128)S(1)}, u32[]{:S(2)}, u32[]{:S(2)}) collective-permute-start(f32[16,1280]{1,0:T(8,128)S(1)} %get-tuple-element.50), channel_id=1, source_target_pairs={{0,384},{32,416},{64,448},{96,480},{128,0},{160,32},{192,64},{224,... | collective-permute-start | bytes 245768 | tf_op jit(solution)/shard_map/ppermute | solution.py:20
  95.3 7.1 %collective-permute-start.9 = (f32[16,1280]{1,0:T(8,128)S(1)}, f32[16,1280]{1,0:T(8,128)S(1)}, u32[]{:S(2)}, u32[]{:S(2)}) collective-permute-start(f32[16,1280]{1,0:T(8,128)S(1)} %get-tuple-element.49), channel_id=1, source_target_pairs={{0,256},{32,288},{64,320},{96,352},{128,384},{160,416},{192,448},{... | collective-permute-start | bytes 245768 | tf_op jit(solution)/shard_map/ppermute | solution.py:20
  102.5 6.8 %collective-permute-done.9 = f32[16,1280]{1,0:T(8,128)S(1)} collective-permute-done((f32[16,1280]{1,0:T(8,128)S(1)}, f32[16,1280]{1,0:T(8,128)S(1)}, u32[]{:S(2)}, u32[]{:S(2)}) %collective-permute-start.9) | collective-permute-done | bytes 81952 | tf_op jit(solution)/shard_map/ppermute | solution.py:20
  109.4 1.9 collective-permute-start.17
  111.3 6.8 %collective-permute-start.10 = (f32[16,1280]{1,0:T(8,128)S(1)}, f32[16,1280]{1,0:T(8,128)S(1)}, u32[]{:S(2)}, u32[]{:S(2)}) collective-permute-start(f32[16,1280]{1,0:T(8,128)S(1)} %fusion.29), channel_id=1, source_target_pairs={{0,384},{32,416},{64,448},{96,480},{128,0},{160,32},{192,64},{224,... | collective-permute-start | bytes 245768 | tf_op jit(solution)/shard_map/ppermute | solution.py:20
  118.1 4.1 %collective-permute-start.11 = (f32[16,1280]{1,0:T(8,128)S(1)}, f32[16,1280]{1,0:T(8,128)S(1)}, u32[]{:S(2)}, u32[]{:S(2)}) collective-permute-start(f32[16,1280]{1,0:T(8,128)S(1)} %fusion.29), channel_id=1, source_target_pairs={{0,256},{32,288},{64,320},{96,352},{128,384},{160,416},{192,448},{... | collective-permute-start | bytes 245768 | tf_op jit(solution)/shard_map/ppermute | solution.py:20
  122.1 7.3 %collective-permute-start.12 = (f32[16,1280]{1,0:T(8,128)S(1)}, f32[16,1280]{1,0:T(8,128)S(1)}, u32[]{:S(2)}, u32[]{:S(2)}) collective-permute-start(f32[16,1280]{1,0:T(8,128)S(1)} %fusion.29), channel_id=1, source_target_pairs={{0,128},{32,160},{64,192},{96,224},{128,256},{160,288},{192,320},{... | collective-permute-start | bytes 245768 | tf_op jit(solution)/shard_map/ppermute | solution.py:20
  129.4 2.8 %collective-permute-done.11 = f32[16,1280]{1,0:T(8,128)S(1)} collective-permute-done((f32[16,1280]{1,0:T(8,128)S(1)}, f32[16,1280]{1,0:T(8,128)S(1)}, u32[]{:S(2)}, u32[]{:S(2)}) %collective-permute-start.11) | collective-permute-done | bytes 81952 | tf_op jit(solution)/shard_map/ppermute | solution.py:20
  132.3 3.1 %collective-permute-done.12 = f32[16,1280]{1,0:T(8,128)S(1)} collective-permute-done((f32[16,1280]{1,0:T(8,128)S(1)}, f32[16,1280]{1,0:T(8,128)S(1)}, u32[]{:S(2)}, u32[]{:S(2)}) %collective-permute-start.12) | collective-permute-done | bytes 81952 | tf_op jit(solution)/shard_map/ppermute | solution.py:20
  135.4 5.0 %collective-permute-start.13 = (f32[4,16,1280]{2,1,0:T(8,128)S(1)}, f32[4,16,1280]{2,1,0:T(8,128)S(1)}, u32[]{:S(2)}, u32[]{:S(2)}) collective-permute-start(f32[4,16,1280]{2,1,0:T(8,128)S(1)} %pad_maximum_fusion.2), channel_id=1, source_target_pairs={{0,480},{32,0},{64,32},{96,64},{128,96},{160,128},{192,160},{224,1... | collective-permute-start | bytes 983048 | tf_op jit(solution)/shard_map/ppermute | solution.py:20
  140.4 1.9 collective-permute-start.14
  142.4 3.1 %collective-permute-start.15 = (f32[4,8,1280]{2,1,0:T(8,128)S(1)}, f32[4,8,1280]{2,1,0:T(8,128)S(1)}, u32[]{:S(2)}, u32[]{:S(2)}) collective-permute-start(f32[4,8,1280]{2,1,0:T(8,128)S(1)} %get-tuple-element.47), channel_id=1, source_target_pairs={{0,448},{32,480},{64,0},{96,32},{128,64},{160,96},{192,128},{224,1... | collective-permute-start | bytes 491528 | tf_op jit(solution)/shard_map/ppermute | solution.py:20
  145.5 3.7 %collective-permute-start.16 = (f32[4,8,1280]{2,1,0:T(8,128)S(1)}, f32[4,8,1280]{2,1,0:T(8,128)S(1)}, u32[]{:S(2)}, u32[]{:S(2)}) collective-permute-start(f32[4,8,1280]{2,1,0:T(8,128)S(1)} %get-tuple-element.46), channel_id=1, source_target_pairs={{0,64},{32,96},{64,128},{96,160},{128,192},{160,224},{192,256},{22... | collective-permute-start | bytes 491528 | tf_op jit(solution)/shard_map/ppermute | solution.py:20
  149.2 5.4 %collective-permute-done.17 = f32[16,32,1024]{2,1,0:T(8,128)} collective-permute-done((f32[16,32,1024]{2,1,0:T(8,128)}, f32[16,32,1024]{2,1,0:T(8,128)}, u32[]{:S(2)}, u32[]{:S(2)}) %collective-permute-start.17) | collective-permute-done | bytes 2097184 | tf_op jit(solution)/shard_map/ppermute | solution.py:24
  154.6 4.4 %maximum_select_fusion = f32[16,2,32,1024]{3,2,1,0:T(8,128)S(1)} fusion(f32[16,1,32,1024]{3,2,1,0:T(8,128)} %bitcast.14, f32[16,1,32,1024]{3,2,1,0:T(8,128)} %bitcast.77, pred[]{:T(512)S(6)} %eq.15), kind=kLoop, calls=%fused_computation | loop fusion | flops 3145728 | bytes 8388609 | tf_op jit(solution)/shard_map/jit(_where)/select_n | solution.py:103
  159.0 2.3 %fusion.36 = f32[256,1024]{1,0:T(8,128)S(1)} fusion(f32[256,1024]{1,0:T(8,128)S(1)} %maximum_select_fusion.1, f32[1024,1024]{1,0:T(8,128)S(1)} %bitcast.67), kind=kOutput, calls=%fused_computation.73 | convolution fusion | flops 1610612736 | bytes 6291456 | tf_op jit(solution)/shard_map/dot_general | solution.py:13
  164.1 1.9 collective-permute-start.18
  166.0 5.6 %collective-permute-start.19 = (f32[128,1024]{1,0:T(8,128)}, f32[128,1024]{1,0:T(8,128)S(1)}, u32[]{:S(2)}, u32[]{:S(2)}) collective-permute-start(f32[128,1024]{1,0:T(8,128)} %collective-permute-done.6), channel_id=1, source_target_pairs={{0,32},{32,64},{64,96},{96,128},{128,160},{160,192},{192,224},{224... | collective-permute-start | bytes 1572872 | tf_op jit(solution)/shard_map/ppermute | solution.py:20
  171.6 5.8 %collective-permute-start.20 = (f32[128,1024]{1,0:T(8,128)}, f32[128,1024]{1,0:T(8,128)S(1)}, u32[]{:S(2)}, u32[]{:S(2)}) collective-permute-start(f32[128,1024]{1,0:T(8,128)} %collective-permute-done.1), channel_id=1, source_target_pairs={{0,480},{32,0},{64,32},{96,64},{128,96},{160,128},{192,160},{224,1... | collective-permute-start | bytes 1572872 | tf_op jit(solution)/shard_map/ppermute | solution.py:20
  177.4 4.1 %fusion = f32[384,1024]{1,0:T(8,128)S(1)} fusion(f32[1024,1024]{1,0:T(8,128)S(1)} %bitcast.68, f32[128,1024]{1,0:T(8,128)} %collective-permute-done.1, f32[128,1024]{1,0:T(8,128)S(1)} %bitcast.76, f32[128,1024]{1,0:T(8,128)} %collective-permute-done.6), kind=kOutput, calls=%fused_computation.3 | convolution fusion | flops 2416705536 | bytes 7340032 | tf_op jit(solution)/shard_map/dot_general | solution.py:13
  181.5 2.5 %collective-permute-done.19 = f32[128,1024]{1,0:T(8,128)S(1)} collective-permute-done((f32[128,1024]{1,0:T(8,128)}, f32[128,1024]{1,0:T(8,128)S(1)}, u32[]{:S(2)}, u32[]{:S(2)}) %collective-permute-start.19) | collective-permute-done | bytes 524320 | tf_op jit(solution)/shard_map/ppermute | solution.py:20
  185.1 2.2 fusion.7
  190.8 11.9 %all-to-all-start = ((f32[32,8,640]{2,1,0:T(8,128)}), f32[32,8,640]{2,1,0:T(8,128)S(1)}, u32[]{:S(2)}, u32[]{:S(2)}) async-start(f32[32,8,640]{2,1,0:T(8,128)} %maximum_bitcast_fusion), calls=%async_computation | async-start | bytes 1310720 | tf_op jit(solution)/shard_map/all_to_all | solution.py:146
  202.9 12.8 %all-to-all-done = f32[32,8,640]{2,1,0:T(8,128)S(1)} async-done(((f32[32,8,640]{2,1,0:T(8,128)}), f32[32,8,640]{2,1,0:T(8,128)S(1)}, u32[]{:S(2)}, u32[]{:S(2)}) %all-to-all-start) | async-done | bytes 655392 | tf_op jit(solution)/shard_map/all_to_all | solution.py:146
  (70 shorter events, 22.7 us)
Async XLA Ops:
  6.5 102.8 %all-gather.2.cloned.1.call-start = ((), (), s32[]{:S(2)}) async-start(), calls=%async_computation.1 | async-start | bytes 2228224 | tf_op jit(solution)/shard_map/all_gather | solution.py:86
  9.1 18.0 %collective-permute-start = (f32[128,1024]{1,0:T(8,128)S(1)}, f32[128,1024]{1,0:T(8,128)S(1)}, u32[]{:S(2)}, u32[]{:S(2)}) collective-permute-start(f32[128,1024]{1,0:T(8,128)S(1)} %bitcast_multiply_fusion), channel_id=1, source_target_pairs={{0,16},{16,0},{1,17},{17,1},{2,18},{18,2},{3,19},{19,3},{4,20},{20... | collective-permute-start | bytes 1572872 | tf_op jit(solution)/shard_map/ppermute | solution.py:24
  15.9 24.5 %collective-permute-start.1 = (f32[128,1024]{1,0:T(8,128)S(1)}, f32[128,1024]{1,0:T(8,128)}, u32[]{:S(2)}, u32[]{:S(2)}) collective-permute-start(f32[128,1024]{1,0:T(8,128)S(1)} %bitcast.74), channel_id=1, source_target_pairs={{0,480},{32,0},{64,32},{96,64},{128,96},{160,128},{192,160},{224,1... | collective-permute-start | bytes 1572872 | tf_op jit(solution)/shard_map/ppermute | solution.py:20
  42.7 24.0 %collective-permute-start.2 = (f32[4,16,1280]{2,1,0:T(8,128)}, f32[4,16,1280]{2,1,0:T(8,128)S(1)}, u32[]{:S(2)}, u32[]{:S(2)}) collective-permute-start(f32[4,16,1280]{2,1,0:T(8,128)} %get-tuple-element.41), channel_id=1, source_target_pairs={{0,32},{32,64},{64,96},{96,128},{128,160},{160,192},{192,224},{224... | collective-permute-start | bytes 983048 | tf_op jit(solution)/shard_map/ppermute | solution.py:20
  44.6 22.1 %collective-permute-start.3 = (f32[4,16,1280]{2,1,0:T(8,128)S(1)}, f32[4,16,1280]{2,1,0:T(8,128)}, u32[]{:S(2)}, u32[]{:S(2)}) collective-permute-start(f32[4,16,1280]{2,1,0:T(8,128)S(1)} %get-tuple-element.43), channel_id=1, source_target_pairs={{0,480},{32,0},{64,32},{96,64},{128,96},{160,128},{192,160},{224,1... | collective-permute-start | bytes 983048 | tf_op jit(solution)/shard_map/ppermute | solution.py:20
  50.7 14.9 %collective-permute-start.4 = (f32[4,8,1280]{2,1,0:T(8,128)}, f32[4,8,1280]{2,1,0:T(8,128)}, u32[]{:S(2)}, u32[]{:S(2)}) collective-permute-start(f32[4,8,1280]{2,1,0:T(8,128)} %get-tuple-element.51), channel_id=1, source_target_pairs={{0,64},{32,96},{64,128},{96,160},{128,192},{160,224},{192,256},{22... | collective-permute-start | bytes 491528 | tf_op jit(solution)/shard_map/ppermute | solution.py:20
  52.6 14.0 %collective-permute-start.5 = (f32[4,8,1280]{2,1,0:T(8,128)}, f32[4,8,1280]{2,1,0:T(8,128)}, u32[]{:S(2)}, u32[]{:S(2)}) collective-permute-start(f32[4,8,1280]{2,1,0:T(8,128)} %get-tuple-element.52), channel_id=1, source_target_pairs={{0,448},{32,480},{64,0},{96,32},{128,64},{160,96},{192,128},{224,1... | collective-permute-start | bytes 491528 | tf_op jit(solution)/shard_map/ppermute | solution.py:20
  58.1 28.0 %collective-permute-start.6 = (f32[128,1024]{1,0:T(8,128)S(1)}, f32[128,1024]{1,0:T(8,128)}, u32[]{:S(2)}, u32[]{:S(2)}) collective-permute-start(f32[128,1024]{1,0:T(8,128)S(1)} %bitcast.75), channel_id=1, source_target_pairs={{0,32},{32,64},{64,96},{96,128},{128,160},{160,192},{192,224},{224... | collective-permute-start | bytes 1572872 | tf_op jit(solution)/shard_map/ppermute | solution.py:20
  86.1 16.3 %collective-permute-start.7 = (f32[16,1280]{1,0:T(8,128)S(1)}, f32[16,1280]{1,0:T(8,128)S(1)}, u32[]{:S(2)}, u32[]{:S(2)}) collective-permute-start(f32[16,1280]{1,0:T(8,128)S(1)} %get-tuple-element.48), channel_id=1, source_target_pairs={{0,128},{32,160},{64,192},{96,224},{128,256},{160,288},{192,320},{... | collective-permute-start | bytes 245768 | tf_op jit(solution)/shard_map/ppermute | solution.py:20
  88.1 14.4 %collective-permute-start.8 = (f32[16,1280]{1,0:T(8,128)S(1)}, f32[16,1280]{1,0:T(8,128)S(1)}, u32[]{:S(2)}, u32[]{:S(2)}) collective-permute-start(f32[16,1280]{1,0:T(8,128)S(1)} %get-tuple-element.50), channel_id=1, source_target_pairs={{0,384},{32,416},{64,448},{96,480},{128,0},{160,32},{192,64},{224,... | collective-permute-start | bytes 245768 | tf_op jit(solution)/shard_map/ppermute | solution.py:20
  95.3 14.0 %collective-permute-start.9 = (f32[16,1280]{1,0:T(8,128)S(1)}, f32[16,1280]{1,0:T(8,128)S(1)}, u32[]{:S(2)}, u32[]{:S(2)}) collective-permute-start(f32[16,1280]{1,0:T(8,128)S(1)} %get-tuple-element.49), channel_id=1, source_target_pairs={{0,256},{32,288},{64,320},{96,352},{128,384},{160,416},{192,448},{... | collective-permute-start | bytes 245768 | tf_op jit(solution)/shard_map/ppermute | solution.py:20
  109.4 45.2 %collective-permute-start.17 = (f32[16,32,1024]{2,1,0:T(8,128)}, f32[16,32,1024]{2,1,0:T(8,128)}, u32[]{:S(2)}, u32[]{:S(2)}) collective-permute-start(f32[16,32,1024]{2,1,0:T(8,128)} %all-gather.2.cloned.1.call-done), channel_id=1, source_target_pairs={{0,16},{16,0},{1,17},{17,1},{2,18},{18,2},{3,19},{19,3},{4,20},{20... | collective-permute-start | bytes 6291464 | tf_op jit(solution)/shard_map/ppermute | solution.py:24
  111.3 18.1 %collective-permute-start.10 = (f32[16,1280]{1,0:T(8,128)S(1)}, f32[16,1280]{1,0:T(8,128)S(1)}, u32[]{:S(2)}, u32[]{:S(2)}) collective-permute-start(f32[16,1280]{1,0:T(8,128)S(1)} %fusion.29), channel_id=1, source_target_pairs={{0,384},{32,416},{64,448},{96,480},{128,0},{160,32},{192,64},{224,... | collective-permute-start | bytes 245768 | tf_op jit(solution)/shard_map/ppermute | solution.py:20
  118.1 14.2 %collective-permute-start.11 = (f32[16,1280]{1,0:T(8,128)S(1)}, f32[16,1280]{1,0:T(8,128)S(1)}, u32[]{:S(2)}, u32[]{:S(2)}) collective-permute-start(f32[16,1280]{1,0:T(8,128)S(1)} %fusion.29), channel_id=1, source_target_pairs={{0,256},{32,288},{64,320},{96,352},{128,384},{160,416},{192,448},{... | collective-permute-start | bytes 245768 | tf_op jit(solution)/shard_map/ppermute | solution.py:20
  122.1 13.2 %collective-permute-start.12 = (f32[16,1280]{1,0:T(8,128)S(1)}, f32[16,1280]{1,0:T(8,128)S(1)}, u32[]{:S(2)}, u32[]{:S(2)}) collective-permute-start(f32[16,1280]{1,0:T(8,128)S(1)} %fusion.29), channel_id=1, source_target_pairs={{0,128},{32,160},{64,192},{96,224},{128,256},{160,288},{192,320},{... | collective-permute-start | bytes 245768 | tf_op jit(solution)/shard_map/ppermute | solution.py:20
  135.4 25.9 %collective-permute-start.13 = (f32[4,16,1280]{2,1,0:T(8,128)S(1)}, f32[4,16,1280]{2,1,0:T(8,128)S(1)}, u32[]{:S(2)}, u32[]{:S(2)}) collective-permute-start(f32[4,16,1280]{2,1,0:T(8,128)S(1)} %pad_maximum_fusion.2), channel_id=1, source_target_pairs={{0,480},{32,0},{64,32},{96,64},{128,96},{160,128},{192,160},{224,1... | collective-permute-start | bytes 983048 | tf_op jit(solution)/shard_map/ppermute | solution.py:20
  140.4 20.9 %collective-permute-start.14 = (f32[4,16,1280]{2,1,0:T(8,128)S(1)}, f32[4,16,1280]{2,1,0:T(8,128)S(1)}, u32[]{:S(2)}, u32[]{:S(2)}) collective-permute-start(f32[4,16,1280]{2,1,0:T(8,128)S(1)} %pad_maximum_fusion.2), channel_id=1, source_target_pairs={{0,32},{32,64},{64,96},{96,128},{128,160},{160,192},{192,224},{224... | collective-permute-start | bytes 983048 | tf_op jit(solution)/shard_map/ppermute | solution.py:20
  142.4 18.9 %collective-permute-start.15 = (f32[4,8,1280]{2,1,0:T(8,128)S(1)}, f32[4,8,1280]{2,1,0:T(8,128)S(1)}, u32[]{:S(2)}, u32[]{:S(2)}) collective-permute-start(f32[4,8,1280]{2,1,0:T(8,128)S(1)} %get-tuple-element.47), channel_id=1, source_target_pairs={{0,448},{32,480},{64,0},{96,32},{128,64},{160,96},{192,128},{224,1... | collective-permute-start | bytes 491528 | tf_op jit(solution)/shard_map/ppermute | solution.py:20
  145.5 15.8 %collective-permute-start.16 = (f32[4,8,1280]{2,1,0:T(8,128)S(1)}, f32[4,8,1280]{2,1,0:T(8,128)S(1)}, u32[]{:S(2)}, u32[]{:S(2)}) collective-permute-start(f32[4,8,1280]{2,1,0:T(8,128)S(1)} %get-tuple-element.46), channel_id=1, source_target_pairs={{0,64},{32,96},{64,128},{96,160},{128,192},{160,224},{192,256},{22... | collective-permute-start | bytes 491528 | tf_op jit(solution)/shard_map/ppermute | solution.py:20
  164.1 23.2 %collective-permute-start.18 = (f32[256,1024]{1,0:T(8,128)S(1)}, f32[256,1024]{1,0:T(8,128)S(1)}, u32[]{:S(2)}, u32[]{:S(2)}) collective-permute-start(f32[256,1024]{1,0:T(8,128)S(1)} %maximum_select_fusion.4), channel_id=1, source_target_pairs={{0,16},{16,0},{1,17},{17,1},{2,18},{18,2},{3,19},{19,3},{4,20},{20... | collective-permute-start | bytes 3145736 | tf_op jit(solution)/shard_map/ppermute | solution.py:24
  166.0 18.1 %collective-permute-start.19 = (f32[128,1024]{1,0:T(8,128)}, f32[128,1024]{1,0:T(8,128)S(1)}, u32[]{:S(2)}, u32[]{:S(2)}) collective-permute-start(f32[128,1024]{1,0:T(8,128)} %collective-permute-done.6), channel_id=1, source_target_pairs={{0,32},{32,64},{64,96},{96,128},{128,160},{160,192},{192,224},{224... | collective-permute-start | bytes 1572872 | tf_op jit(solution)/shard_map/ppermute | solution.py:20
  171.6 13.4 %collective-permute-start.20 = (f32[128,1024]{1,0:T(8,128)}, f32[128,1024]{1,0:T(8,128)S(1)}, u32[]{:S(2)}, u32[]{:S(2)}) collective-permute-start(f32[128,1024]{1,0:T(8,128)} %collective-permute-done.1), channel_id=1, source_target_pairs={{0,480},{32,0},{64,32},{96,64},{128,96},{160,128},{192,160},{224,1... | collective-permute-start | bytes 1572872 | tf_op jit(solution)/shard_map/ppermute | solution.py:20
  190.8 24.8 %all-to-all-start = ((f32[32,8,640]{2,1,0:T(8,128)}), f32[32,8,640]{2,1,0:T(8,128)S(1)}, u32[]{:S(2)}, u32[]{:S(2)}) async-start(f32[32,8,640]{2,1,0:T(8,128)} %maximum_bitcast_fusion), calls=%async_computation | async-start | bytes 1310720 | tf_op jit(solution)/shard_map/all_to_all | solution.py:146
Sparse Core Ops, SparseCore 0:
  9.4 78.0 all-gather.1
